TPU v7x, 32 devices: a whole 2x2x4 slice. The times are simulated.
32 devices in a mesh: dp: 4 (over y, x), expert: 8 (over z, core).
Axes of the slice: x: 2, y: 2, z: 4, core: 2. Of those that a mesh axis runs over, the one named last changes fastest.
Arguments:
- target_in: bfloat16 [20480, 1408], P(('dp', 'expert')), may hold values from -6 to 6
- ln_gain: float32 [1408], replicated, may hold values from 0.1 to 1.9
- up_target: bfloat16 [1408, 3072], P('dp'), may hold values from -0.15625 to 0.15625
- down_target: bfloat16 [3072, 1408], P('dp'), may hold values from -0.109375 to 0.109375
- pred_rows: bfloat16 [3072, 1024], P('expert'), may hold values from -6 to 6
- expert_ids: int32 [3072, 2], P('expert'), may hold values from 0 to 31, all different within a row; in each aligned block of 384 rows (0 to 383, 384 to 767, ...) at most 32 rows name the same one
- combine_weights: float32 [3072, 2], P('expert'), may hold values from 0.25 to 1
- gate_experts: bfloat16 [32, 2816, 1024], P(('dp', 'expert')), may hold values from -0.1875 to 0.1875
- up_experts: bfloat16 [32, 2816, 1024], P(('dp', 'expert')), may hold values from -0.1875 to 0.1875
- down_experts: bfloat16 [32, 2816, 1024], P(('dp', 'expert')), may hold values from -0.21875 to 0.21875
Outputs:
- target_out: bfloat16 [20480, 1408], P(('dp', 'expert'))
- predicted: bfloat16 [3072, 1024], P('expert', 'dp')
Inputs may be any that keep to these rules, and one draw needn't show every extreme that they name: `expert_ids`: each row names 2 different experts. Within each aligned block of 384 rows (the rows of one device) no expert is named by more than 32 rows, a bound that some block reaches.
All inputs are finite; a program needn't handle non-finite values.
Results may differ from a plain program's by a relative error of at most 0.004.
Values may be sent and summed in bfloat16 or wider, within the bound.
No kernel may reach another device: no remote copies, remote signals or barrier semaphores. Data moves between devices by JAX's collectives and lax.ppermute only.
A program may use at most 128 MiB of HBM per device.

v0:
```python
import jax
import jax.numpy as jnp
from jax import lax
from jax.sharding import PartitionSpec as P

EXP_DEV = 4
TOP = 2
CAP = 32


def on_device(
    target_in,
    ln_gain,
    up_target,
    down_target,
    pred_rows,
    expert_ids,
    combine_weights,
    gate_experts,
    up_experts,
    down_experts,
):
    values = target_in.astype(jnp.float32)
    average = jnp.mean(values, axis=-1, keepdims=True)
    centered = values - average
    variance = jnp.mean(centered * centered, axis=-1, keepdims=True)
    normed = (centered * lax.rsqrt(variance + 1e-06) * ln_gain).astype(jnp.bfloat16)
    columns = normed
    pre_act = jnp.dot(
        columns,
        lax.all_gather(up_target, "dp", axis=0, tiled=True),
        preferred_element_type=jnp.float32,
    )
    hidden = jax.nn.gelu(pre_act, approximate=True).astype(jnp.bfloat16)
    columns = hidden
    projected = jnp.dot(
        columns,
        lax.all_gather(down_target, "dp", axis=0, tiled=True),
        preferred_element_type=jnp.float32,
    )
    target_out = (values + projected).astype(jnp.bfloat16)
    owner_count = lax.axis_size("expert")
    model_width = pred_rows.shape[1]
    group_index = lax.axis_index("dp") % EXP_DEV
    flat_ids = expert_ids.reshape(-1)
    in_group = flat_ids // owner_count == group_index
    target_owner = flat_ids % owner_count
    matches = (
        target_owner[:, None] == jnp.arange(owner_count, dtype=jnp.int32)[None, :]
    ) & in_group[:, None]
    onehot = matches.astype(jnp.int32)
    running = jnp.cumsum(onehot, axis=0) - onehot
    slot_index = jnp.sum(running * onehot, axis=1)
    base_pos = target_owner * CAP + slot_index
    send_pos = jnp.where(in_group, base_pos, owner_count * CAP)
    row_index = jnp.arange(flat_ids.shape[0], dtype=jnp.int32) // TOP
    outgoing = jnp.zeros((owner_count * CAP, model_width), jnp.bfloat16)
    outgoing = outgoing.at[send_pos].set(pred_rows[row_index], mode="drop")
    incoming = lax.all_to_all(
        outgoing.reshape(owner_count, CAP, model_width),
        "expert",
        split_axis=0,
        concat_axis=0,
        tiled=True,
    )
    slot_rows = incoming.reshape(owner_count * CAP, model_width)
    contract = (((1,), (1,)), ((), ()))
    gate_vals = lax.dot_general(
        slot_rows, gate_experts[0], contract, preferred_element_type=jnp.float32
    )
    up_vals = lax.dot_general(
        slot_rows, up_experts[0], contract, preferred_element_type=jnp.float32
    )
    inner_act = (jax.nn.silu(gate_vals) * up_vals).astype(jnp.bfloat16)
    partial_out = jnp.dot(inner_act, down_experts[0], preferred_element_type=jnp.float32)
    returned = lax.all_to_all(
        partial_out.reshape(owner_count, CAP, model_width),
        "expert",
        split_axis=0,
        concat_axis=0,
        tiled=True,
    )
    pick_pos = jnp.where(in_group, base_pos, 0)
    picked = returned.reshape(-1, model_width)[pick_pos].reshape(-1, TOP, model_width)
    weights_used = jnp.where(in_group.reshape(-1, TOP), combine_weights, jnp.float32(0.0))
    mixed_part = jnp.sum(picked * weights_used[:, :, None], axis=1)
    mixed_out = lax.psum_scatter(mixed_part, "dp", scatter_dimension=1, tiled=True)
    share_cols = mixed_out.shape[1]
    residual = lax.dynamic_slice_in_dim(
        pred_rows, lax.axis_index("dp") * share_cols, share_cols, 1
    ).astype(jnp.float32)
    predicted = (residual + mixed_out).astype(jnp.bfloat16)
    return (target_out, predicted)


def solution(mesh):
    in_specs = (
        P(("dp", "expert"), None),
        P(),
        P("dp", None),
        P("dp", None),
        P("expert", None),
        P("expert", None),
        P("expert", None),
        P(("dp", "expert"), None, None),
        P(("dp", "expert"), None, None),
        P(("dp", "expert"), None, None),
    )
    out_specs = (P(("dp", "expert"), None), P("expert", "dp"))
    return jax.shard_map(
        on_device, mesh=mesh, in_specs=in_specs, out_specs=out_specs, check_vma=False
    )
```

profile of v0, /device:TPU:0, one launch (start us, length us, event | category | flops | bytes accessed | tf_op | source)
XLA Modules:
  0.0 346.7 jit_solution(5088685948920484158)
XLA Ops:
  7.2 0.8 copy.15
  8.0 0.2 reshape.279
  8.1 0.1 reshape.281
  8.3 0.1 reshape.280
  8.6 1.7 reduce-window.6
  10.3 0.1 slice.12
  10.4 0.1 copy.18
  10.5 0.2 reduce-window.9
  10.7 0.1 copy.19
  10.7 0.1 fusion.43
  10.9 22.5 %scatter_custom_fusion = bf16[256,1024]{1,0:T(8,128)(2,1)S(1)} fusion(s32[768]{0:T(1024)S(1)} %get-tuple-element.3, bf16[384,1024]{1,0:T(8,128)(2,1)} %param.14, s32[1024]{0:T(1024)S(1)} %pad_clamp_fusion.1, bf16[]{:T(256)} %constant.81.clone.1), kind=kCustom, calls=%fused_computation.39 | custom fusion | bytes 524800 | tf_op jit(solution)/shard_map/scatter | solution.py:58
  33.5 0.0 slice-start
  33.5 21.7 %all_to_all.10 = bf16[8,32,1024]{2,1,0:T(8,128)(2,1)S(1)} all-to-all(bf16[8,32,1024]{2,1,0:T(8,128)(2,1)S(1)} %bitcast.38), channel_id=1, replica_groups=mesh['dp'=4,'expert'=8] {'expert'}, dimensions={0} | all-to-all | bytes 1048576 | tf_op jit(solution)/shard_map/all_to_all | solution.py:59
  55.2 0.0 slice-start.1
  55.2 4.5 %fusion.12 = f32[256,2816]{1,0:T(8,128)S(1)} fusion(bf16[256,1024]{1,0:T(8,128)(2,1)S(1)} %bitcast.39, bf16[1,2816,1024]{2,1,0:T(8,128)(2,1)} %param.17), kind=kOutput, calls=%fused_computation.16 | convolution fusion | flops 1476395008 | bytes 9175040 | tf_op jit(solution)/shard_map/dot_general | solution.py:68
  59.7 0.0 slice-done
  59.7 0.0 slice-done.1
  59.7 0.0 slice-start.3
  59.8 2.2 fusion.25
  61.9 0.0 slice-done.2
  61.9 0.0 slice-done.3
  61.9 0.0 copy-start.1
  62.0 0.0 copy-start.2
  62.0 2.6 fusion.8
  64.6 3.6 %all-to-all-start.1 = ((f32[8,32,1024]{2,1,0:T(8,128)}), f32[8,32,1024]{2,1,0:T(8,128)S(1)}, u32[]{:S(2)}, u32[]{:S(2)}) async-start(f32[8,32,1024]{2,1,0:T(8,128)} %fusion.8), calls=%async_computation.1 | async-start | bytes 2097152 | tf_op jit(solution)/shard_map/all_to_all | solution.py:76
  68.2 0.0 reduce-scatter.2.cloned.1.call-start
  68.2 0.0 copy-done.1
  68.2 0.0 copy-done.2
  68.2 0.1 copy.20
  68.4 26.3 %all-to-all-done.1 = f32[8,32,1024]{2,1,0:T(8,128)S(1)} async-done(((f32[8,32,1024]{2,1,0:T(8,128)}), f32[8,32,1024]{2,1,0:T(8,128)S(1)}, u32[]{:S(2)}, u32[]{:S(2)}) %all-to-all-start.1) | async-done | bytes 1048608 | tf_op jit(solution)/shard_map/all_to_all | solution.py:76
  94.7 3.6 %gather_fusion = f32[768,1024]{1,0:T(8,128)} fusion(f32[256,1024]{1,0:T(8,128)S(1)} %bitcast.37, s32[1024]{0:T(1024)S(1)} %pad_clamp_fusion), kind=kCustom, calls=%fused_computation.1 | custom fusion | bytes 6294528 | tf_op jit(solution)/shard_map/gather | solution.py:84
  98.3 3.7 %reshape.286 = f32[384,2,1024]{2,1,0:T(2,128)S(1)} reshape(f32[768,1024]{1,0:T(8,128)} %gather_fusion) | data formatting | bytes 6291456 | tf_op jit(solution)/shard_map/reshape | solution.py:84
  102.0 5.1 %multiply_reduce_fusion = f32[384,1024]{1,0:T(8,128)} fusion(f32[384,2,1024]{2,1,0:T(2,128)S(1)} %reshape.286, f32[384,2]{1,0:T(8,128)S(1)} %copy.20), kind=kLoop, calls=%fused_computation.34 | loop fusion | flops 1179648 | bytes 4721664 | tf_op jit(solution)/shard_map/reduce_sum | solution.py:86
  107.1 0.0 reduce-scatter.2.cloned.1.call-update
  107.1 0.0 all-gather.5.cloned.1.call-start
  107.2 0.7 all-gather.5.cloned.1.call-update
  107.9 0.0 copy-start.3
  107.9 0.3 all-gather.3.cloned.1.call-start
  108.2 0.5 all-gather.3.cloned.1.call-update
  108.6 0.0 copy-done
  108.6 0.3 convert_reduce_fusion
  109.0 0.6 fusion.28
  109.6 27.5 %reduce-scatter.2.cloned.1.call-done = f32[384,256]{1,0:T(8,128)} async-done(((f32[384,1024]{1,0:T(8,128)}), f32[384,256]{1,0:T(8,128)}) %reduce-scatter.2.cloned.1.call-update) | async-done | bytes 393232 | tf_op jit(solution)/shard_map/reduce_scatter | solution.py:87
  137.1 1.8 add_convert_fusion
  138.9 89.9 %all-gather.5.cloned.1.call-done = bf16[3072,1408]{1,0:T(8,128)(2,1)} async-done(((bf16[768,1408]{1,0:T(8,128)(2,1)}), bf16[3072,1408]{1,0:T(8,128)(2,1)}) %all-gather.5.cloned.1.call-update) | async-done | bytes 8650768 | tf_op jit(solution)/shard_map/all_gather | solution.py:38
  228.8 91.7 %all-gather.3.cloned.1.call-done = bf16[1408,3072]{1,0:T(8,128)(2,1)} async-done(((bf16[352,3072]{1,0:T(8,128)(2,1)}), bf16[1408,3072]{1,0:T(8,128)(2,1)}) %all-gather.3.cloned.1.call-update) | async-done | bytes 8650768 | tf_op jit(solution)/shard_map/all_gather | solution.py:31
  320.4 0.0 copy-done.3
  320.4 19.8 %fusion.31 = bf16[640,1408]{1,0:T(8,128)(2,1)} fusion(bf16[640,1408]{1,0:T(8,128)(2,1)S(1)} %copy-done, bf16[3072,1408]{1,0:T(8,128)(2,1)} %all-gather.5.cloned.1.call-done, bf16[1408,3072]{1,0:T(8,128)(2,1)} %all-gather.3.cloned.1.call-done, f32[1408]{0:T(1024)S(1)} %copy-done.3, f32[640]{0:T(1024)S(1)} %add_rsqrt_fusion, f32[640]{0:T(1024)S(1)} %broadcast_multiply_fusion), kind=kOutput, calls=%fused_computation.33 | convolution fusion | flops 11097866240 | bytes 20916736 | tf_op jit(solution)/shard_map/dot_general | solution.py:36
  (17 shorter events, 0.2 us)
Async XLA Ops:
  33.5 26.3 %slice-start = ((s8[5767168]{0:T(1024)(128)(4,1)}), s8[4194304]{0:T(1024)(128)(4,1)S(1)}, s32[]{:S(2)}) async-start(s8[5767168]{0:T(1024)(128)(4,1)} %bitcast.43), calls=%async_computation.6 | async-start | bytes 8388608
  55.2 4.5 %slice-start.1 = ((s8[5767168]{0:T(1024)(128)(4,1)}), s8[1572864]{0:T(1024)(128)(4,1)S(1)}, s32[]{:S(2)}) async-start(s8[5767168]{0:T(1024)(128)(4,1)} %bitcast.43), calls=%async_computation.7 | async-start | bytes 3145728
  55.2 6.7 %slice-start.2 = ((s8[5767168]{0:T(1024)(128)(4,1)}), s8[4194304]{0:T(1024)(128)(4,1)S(1)}, s32[]{:S(2)}) async-start(s8[5767168]{0:T(1024)(128)(4,1)} %bitcast.45), calls=%async_computation.8 | async-start | bytes 8388608
  59.7 2.2 slice-start.3
  61.9 6.3 %copy-start.1 = (s32[384,2]{0,1:T(2,128)S(1)}, s32[384,2]{0,1:T(2,128)}, u32[]{:S(2)}) copy-start(s32[384,2]{0,1:T(2,128)} %param.15) | copy-start | bytes 9220
  62.0 6.3 %copy-start.2 = (f32[384,2]{0,1:T(2,128)S(1)}, f32[384,2]{0,1:T(2,128)}, u32[]{:S(2)}) copy-start(f32[384,2]{0,1:T(2,128)} %param.16) | copy-start | bytes 9220
  64.6 30.1 %all-to-all-start.1 = ((f32[8,32,1024]{2,1,0:T(8,128)}), f32[8,32,1024]{2,1,0:T(8,128)S(1)}, u32[]{:S(2)}, u32[]{:S(2)}) async-start(f32[8,32,1024]{2,1,0:T(8,128)} %fusion.8), calls=%async_computation.1 | async-start | bytes 2097152 | tf_op jit(solution)/shard_map/all_to_all | solution.py:76
  68.2 68.9 %reduce-scatter.2.cloned.1.call-start = ((), (), s32[]{:S(2)}) async-start(), calls=%async_computation.5 | async-start | bytes 1966080 | tf_op jit(solution)/shard_map/reduce_scatter | solution.py:87
  107.1 1.5 copy-start
  107.1 121.6 %all-gather.5.cloned.1.call-start = ((), (), s32[]{:S(2)}) async-start(), calls=%async_computation.4 | async-start | bytes 10813440 | tf_op jit(solution)/shard_map/all_gather | solution.py:38
  107.9 212.5 %copy-start.3 = (f32[1408]{0:T(1024)S(1)}, f32[1408]{0:T(1024)}, u32[]{:S(2)}) copy-start(f32[1408]{0:T(1024)} %param.11) | copy-start | bytes 16900
  107.9 212.5 %all-gather.3.cloned.1.call-start = ((), (), s32[]{:S(2)}) async-start(), calls=%async_computation.3 | async-start | bytes 10813440 | tf_op jit(solution)/shard_map/all_gather | solution.py:31
Sparse Core Ops, SparseCore 0:
  107.2 29.8 reduce-scatter.1
  138.9 89.7 all-gather.4
  230.6 89.7 all-gather.2
where the time goes:
time: 347 us
  waiting for transfers between devices  237 us (68%)
  local copies, waits for them, and re-layouts  31.6 us (9%)
  matrix products  29 us (8%)
  blocking collectives  21.7 us (6%)
  between operations  14 us (4%)
  other arithmetic  9.89 us (3%)
  starting transfers between devices  3.9 us (1%)
    all_gather x1, waiting for transfers between devices, on_device(): lax.all_gather(up_target, 'dp', axis=0, tiled=True)  91.7 us
    all_gather x1, waiting for transfers between devices, on_device(): lax.all_gather(down_target, 'dp', axis=0, tiled=True)  89.9 us
    reduce_scatter x1, waiting for transfers between devices, on_device(): lax.psum_scatter(mixed_part, 'dp', scatter_dimension=1, tiled=True)  27.5 us
    all_to_all x1, waiting for transfers between devices, on_device(): lax.all_to_all(partial_out.reshape(owner_count, CAP, model_width), 'exper...  26.3 us
    scatter x1, local copies, waits for them, and re-layouts, on_device(): outgoing = outgoing.at[send_pos].set(pred_rows[row_index], mode='drop')  22.5 us
    all_to_all x1, blocking collectives, on_device(): lax.all_to_all(outgoing.reshape(owner_count, CAP, model_width), 'expert',...  21.7 us
    dot_general x1, matrix products, on_device(): jnp.dot(columns, lax.all_gather(down_target, 'dp', axis=0, tiled=True), p...  19.8 us
  transfers between devices with their start and end apart: 4, of which 4 were waited for; matrix products, arithmetic and copies ran while one was open for 1% of the time, Pallas kernels for 0%

commit v1 on v0

v1 whole, which is shorter than its diff:
```python
import jax
import jax.numpy as jnp
from jax import lax
from jax.sharding import PartitionSpec as P

EXP_DEV = 4
TOP = 2
CAP = 32
BF = jnp.bfloat16
F32 = jnp.float32


def xor_perm(size, bits):
    return [(i, i ^ bits) for i in range(size)]


def norm_rows(rows, gain):
    values = rows.astype(F32)
    average = jnp.mean(values, axis=-1, keepdims=True)
    centered = values - average
    variance = jnp.mean(centered * centered, axis=-1, keepdims=True)
    return (centered * lax.rsqrt(variance + 1e-06) * gain).astype(BF)


def dot(a, b):
    return jnp.dot(a, b, preferred_element_type=F32)


def feed_forward(normed, up, down):
    hidden = jax.nn.gelu(dot(normed, up), approximate=True).astype(BF)
    return dot(hidden, down)


def target_gathered(target_in, ln_gain, up_target, down_target):
    normed = norm_rows(target_in, ln_gain)
    projected = feed_forward(
        normed,
        lax.all_gather(up_target, "dp", axis=0, tiled=True),
        lax.all_gather(down_target, "dp", axis=0, tiled=True),
    )
    return (target_in.astype(F32) + projected).astype(BF)


def target_square(target_in, ln_gain, up_target, down_target):
    depth, width = up_target.shape
    block = width // 4
    half = block // 2
    me = lax.axis_index("dp")
    core = lax.axis_index("expert") % 2
    n_exp = lax.axis_size("expert")
    px, py, pc = xor_perm(4, 1), xor_perm(4, 2), xor_perm(n_exp, 1)

    other_in = lax.ppermute(target_in, "expert", pc)

    def place(pieces, rows):
        out = jnp.zeros((4 * rows, pieces[0].shape[1]), BF)
        for i, piece in enumerate(pieces):
            out = lax.dynamic_update_slice(out, piece, ((me ^ i) * rows, 0))
        return out

    own_sum = other_sum = None
    weights = []
    for start, count in ((0, 256), (256, 128)):
        up_0 = jnp.concatenate(
            [
                lax.dynamic_slice(
                    up_target, (0, b * block + core * half + start), (depth, count)
                )
                for b in range(4)
            ],
            axis=1,
        )
        down_0 = lax.dynamic_slice(
            down_target, (core * half + start, 0), (count, down_target.shape[1])
        )
        up_x, up_y = lax.ppermute(up_0, "dp", px), lax.ppermute(up_0, "dp", py)
        down_x, down_y = lax.ppermute(down_0, "dp", px), lax.ppermute(down_0, "dp", py)
        up_d, down_d = lax.ppermute(up_y, "dp", px), lax.ppermute(down_x, "dp", py)
        weights.append((
            place([up_0, up_x, up_y, up_d], depth),
            place([down_0, down_x, down_y, down_d], count),
        ))
    other_n = norm_rows(other_in, ln_gain)
    own_n = norm_rows(target_in, ln_gain)
    other_sum = sum(feed_forward(other_n, *w) for w in weights)
    own_sum = sum(feed_forward(own_n, *w) for w in weights)
    received = lax.ppermute(other_sum.astype(BF), "expert", pc)
    return (target_in.astype(F32) + own_sum + received.astype(F32)).astype(BF)


def exchange(blocks, axis, size):
    me = lax.axis_index(axis)
    out = jnp.zeros_like(blocks)
    out = lax.dynamic_update_index_in_dim(
        out, lax.dynamic_index_in_dim(blocks, me, 0, keepdims=False), me, 0
    )
    for bits in range(1, size):
        sent = lax.dynamic_index_in_dim(blocks, me ^ bits, 0, keepdims=False)
        got = lax.ppermute(sent, axis, xor_perm(size, bits))
        out = lax.dynamic_update_index_in_dim(out, got, me ^ bits, 0)
    return out


def experts_part(
    pred_rows, expert_ids, combine_weights, gate_experts, up_experts, down_experts
):
    owners = lax.axis_size("expert")
    n_dp = lax.axis_size("dp")
    rows, width = pred_rows.shape
    n_all = EXP_DEV * owners
    group = lax.axis_index("dp") % EXP_DEV
    chosen = expert_ids.T
    each = jnp.arange(n_all, dtype=jnp.int32)[:, None]
    named_k = [chosen[k][None, :] == each for k in range(TOP)]
    named = named_k[0]
    for more in named_k[1:]:
        named = named | more
    before = jnp.arange(rows)[:, None] < jnp.arange(rows)[None, :]
    slot = dot(named.astype(BF), before.astype(BF)).astype(jnp.int32)
    slot = jnp.where(named, slot, -1)
    spread = slot[:, None, :] == jnp.arange(CAP, dtype=jnp.int32)[None, :, None]
    mine = lax.dynamic_slice_in_dim(slot, group * owners, owners, 0)
    pick = mine[:, None, :] == jnp.arange(CAP, dtype=jnp.int32)[None, :, None]
    pick = pick.reshape(owners * CAP, rows).astype(BF)
    outgoing = dot(pick, pred_rows).astype(BF)
    slot_rows = exchange(
        outgoing.reshape(owners, CAP, width), "expert", owners
    ).reshape(owners * CAP, width)
    contract = (((1,), (1,)), ((), ()))
    gate_vals = lax.dot_general(
        slot_rows, gate_experts[0], contract, preferred_element_type=F32
    )
    up_vals = lax.dot_general(
        slot_rows, up_experts[0], contract, preferred_element_type=F32
    )
    inner_act = (jax.nn.silu(gate_vals) * up_vals).astype(BF)
    partial_out = dot(inner_act, down_experts[0]).astype(BF)
    share = width // n_dp
    by_cols = partial_out.reshape(owners * CAP, n_dp, share).transpose(1, 0, 2)
    by_cols = exchange(by_cols, "dp", n_dp)
    by_rows = by_cols.reshape(n_dp, owners, CAP * share).transpose(1, 0, 2)
    back = exchange(by_rows, "expert", owners)
    back = back.reshape(owners, n_dp, CAP, share).transpose(1, 0, 2, 3)
    back = back.reshape(n_dp // EXP_DEV, n_all * CAP, share)
    if n_dp > EXP_DEV:
        back = jnp.sum(back.astype(F32), axis=0)
    else:
        back = back[0]
    mixed_out = 0.0
    weight = sum(
        jnp.where(named_k[k], combine_weights[:, k][None, :], 0.0) for k in range(TOP)
    )
    mix = jnp.where(spread, weight[:, None, :], 0.0).reshape(n_all * CAP, rows)
    over = (((0,), (0,)), ((), ()))
    high = mix.astype(BF)
    low = (mix - high.astype(F32)).astype(BF)
    if n_dp > EXP_DEV:
        mixed_out = lax.dot_general(
            mix, back, over, precision=lax.Precision.HIGHEST, preferred_element_type=F32
        )
    else:
        mixed_out = lax.dot_general(
            high, back, over, preferred_element_type=F32
        ) + lax.dot_general(low, back, over, preferred_element_type=F32)
    residual = lax.dynamic_slice_in_dim(
        pred_rows, lax.axis_index("dp") * share, share, 1
    ).astype(F32)
    return (residual + mixed_out).astype(BF)


def solution(mesh):
    square = mesh.shape["dp"] == 4 and mesh.shape["expert"] % 2 == 0
    target_part = target_square if square else target_gathered

    def on_device(
        target_in,
        ln_gain,
        up_target,
        down_target,
        pred_rows,
        expert_ids,
        combine_weights,
        gate_experts,
        up_experts,
        down_experts,
    ):
        predicted = experts_part(
            pred_rows,
            expert_ids,
            combine_weights,
            gate_experts,
            up_experts,
            down_experts,
        )
        target_out = target_part(target_in, ln_gain, up_target, down_target)
        return (target_out, predicted)

    in_specs = (
        P(("dp", "expert"), None),
        P(),
        P("dp", None),
        P("dp", None),
        P("expert", None),
        P("expert", None),
        P("expert", None),
        P(("dp", "expert"), None, None),
        P(("dp", "expert"), None, None),
        P(("dp", "expert"), None, None),
    )
    out_specs = (P(("dp", "expert"), None), P("expert", "dp"))
    return jax.shard_map(
        on_device, mesh=mesh, in_specs=in_specs, out_specs=out_specs, check_vma=False
    )
```

time: 347 us -> 209 us (0.60)
  waiting for transfers between devices: 237 us -> 49.2 us
  starting transfers between devices: 3.9 us -> 37.3 us
  local copies, waits for them, and re-layouts: 31.6 us -> 61.1 us
  matrix products: 29 us -> 51.1 us
  blocking collectives: 21.7 us -> 0 us
  between operations: 14 us -> 1.23 us
    all_gather x2 -> x0, waiting for transfers between devices: 182 us -> none  [the longest x1 91.7 us: on_device(): lax.all_gather(up_target, 'dp', axis=0, tiled=True)]
    ppermute x0 -> x31, waiting for transfers between devices: none -> 49.2 us  [the longest x17 15.9 us: exchange(): got = lax.ppermute(sent, axis, xor_perm(size, bits))]
    dynamic_update_slice x0 -> x33, local copies, waits for them, and re-layouts: none -> 38.5 us  [the longest x17 18.8 us: exchange(): out = lax.dynamic_update_index_in_dim(out, got, me ^ bits, 0)]
    ppermute x0 -> x31, starting transfers between devices: none -> 37.3 us  [the longest x17 23.5 us: exchange(): got = lax.ppermute(sent, axis, xor_perm(size, bits))]
    reduce_scatter x1 -> x0, waiting for transfers between devices: 27.5 us -> none  [on_device(): lax.psum_scatter(mixed_part, 'dp', scatter_dimension=1, tiled=True)]
    all_to_all x1 -> x0, waiting for transfers between devices: 26.3 us -> none  [on_device(): lax.all_to_all(partial_out.reshape(owner_count, CAP, model_width), 'exper...]
    scatter x1 -> x0, local copies, waits for them, and re-layouts: 22.5 us -> none  [on_device(): outgoing = outgoing.at[send_pos].set(pred_rows[row_index], mode='drop')]
    dot_general x4 -> x10, matrix products: 29 us -> 51.1 us  [the longest x7 41.7 us: dot(): return jnp.dot(a, b, preferred_element_type=F32)]
  transfers between devices with their start and end apart: 4 -> 31, of which waited for: 4 -> 12; matrix products, arithmetic and copies ran while one was open for 1% -> 41% of each run, Pallas kernels for 0% -> 0%
where the time goes in v1:
time: 209 us; the launch traced here: 207 us
  local copies, waits for them, and re-layouts  61.1 us (29%)
  matrix products  51.1 us (24%)
  waiting for transfers between devices  49.2 us (24%)
  starting transfers between devices  37.3 us (18%)
  other arithmetic  6.73 us (3%)
    dot_general x7, matrix products, dot(): return jnp.dot(a, b, preferred_element_type=F32)  41.7 us
    ppermute x17, starting transfers between devices, exchange(): got = lax.ppermute(sent, axis, xor_perm(size, bits))  23.5 us
    dynamic_update_slice x17, local copies, waits for them, and re-layouts, exchange(): out = lax.dynamic_update_index_in_dim(out, got, me ^ bits, 0)  18.8 us
    dynamic_update_slice x14, local copies, waits for them, and re-layouts, place(): out = lax.dynamic_update_slice(out, piece, ((me ^ i) * rows, 0))  17.4 us
    ppermute x17, waiting for transfers between devices, exchange(): got = lax.ppermute(sent, axis, xor_perm(size, bits))  15.9 us
    ppermute x2, waiting for transfers between devices, target_square(): lax.ppermute(down_x, 'dp', py)  14.9 us
    ppermute x2, waiting for transfers between devices, target_square(): lax.ppermute(down_0, 'dp', py)  10.9 us
    broadcast_in_dim x4, local copies, waits for them, and re-layouts, place(): out = jnp.zeros((4 * rows, pieces[0].shape[1]), BF)  6.24 us
  transfers between devices with their start and end apart: 31, of which 12 were waited for; matrix products, arithmetic and copies ran while one was open for 41% of the time, Pallas kernels for 0%

profile of v1, /device:TPU:0, one launch (start us, length us, event | category | flops | bytes accessed | tf_op | source)
XLA Modules:
  0.0 206.7 jit_solution(15075405724991962519)
XLA Ops:
  1.9 2.0 broadcast_in_dim.130
  5.2 3.0 %collective-permute-start = (bf16[352,1024]{1,0:T(8,128)(2,1)}, bf16[352,1024]{1,0:T(8,128)(2,1)}, u32[]{:S(2)}, u32[]{:S(2)}) collective-permute-start(bf16[352,1024]{1,0:T(8,128)(2,1)} %get-tuple-element.18), channel_id=1, source_target_pairs={{0,8},{8,0},{16,24},{24,16},{1,9},{9,1},{17,25},{25,17},{2,10},{10... | collective-permute-start | bytes 2162696 | tf_op jit(solution)/shard_map/ppermute | solution.py:76
  8.2 1.5 collective-permute-start.1
  11.4 1.6 collective-permute-start.15
  16.0 1.8 broadcast_in_dim.131
  25.1 2.6 %collective-permute-start.17 = (bf16[32,1024]{1,0:T(8,128)(2,1)S(1)}, bf16[32,1024]{1,0:T(8,128)(2,1)S(1)}, u32[]{:S(2)}, u32[]{:S(2)}) collective-permute-start(bf16[32,1024]{1,0:T(8,128)(2,1)S(1)} %get-tuple-element.35), channel_id=1, source_target_pairs={{0,4},{1,5},{2,6},{3,7},{4,0},{5,1},{6,2},{7,3},{8,12},{9,13},{10,... | collective-permute-start | bytes 196616 | tf_op jit(solution)/shard_map/ppermute | solution.py:99
  28.7 3.6 %collective-permute-start.19 = (bf16[32,1024]{1,0:T(8,128)(2,1)S(1)}, bf16[32,1024]{1,0:T(8,128)(2,1)S(1)}, u32[]{:S(2)}, u32[]{:S(2)}) collective-permute-start(bf16[32,1024]{1,0:T(8,128)(2,1)S(1)} %get-tuple-element.33), channel_id=1, source_target_pairs={{0,6},{1,7},{2,4},{3,5},{4,2},{5,3},{6,0},{7,1},{8,14},{9,15},{10,... | collective-permute-start | bytes 196616 | tf_op jit(solution)/shard_map/ppermute | solution.py:99
  32.3 4.0 %collective-permute-start.20 = (bf16[32,1024]{1,0:T(8,128)(2,1)S(1)}, bf16[32,1024]{1,0:T(8,128)(2,1)S(1)}, u32[]{:S(2)}, u32[]{:S(2)}) collective-permute-start(bf16[32,1024]{1,0:T(8,128)(2,1)S(1)} %get-tuple-element.32), channel_id=1, source_target_pairs={{0,7},{1,6},{2,5},{3,4},{4,3},{5,2},{6,1},{7,0},{8,15},{9,14},{10,... | collective-permute-start | bytes 196616 | tf_op jit(solution)/shard_map/ppermute | solution.py:99
  37.1 1.6 collective-permute-start.9
  38.7 5.9 %fusion.2 = f32[256,2816]{1,0:T(8,128)} fusion(bf16[256,1024]{1,0:T(8,128)(2,1)S(1)} %bitcast.130, bf16[1,2816,1024]{2,1,0:T(8,128)(2,1)} %param.18), kind=kOutput, calls=%fused_computation.2 | convolution fusion | flops 1476395008 | bytes 9175040 | tf_op jit(solution)/shard_map/dot_general | solution.py:133
  44.6 8.4 %fusion.63 = bf16[256,1024]{1,0:T(8,128)(2,1)S(1)} fusion(bf16[1,2816,1024]{2,1,0:T(8,128)(2,1)} %param.19, f32[256,2816]{1,0:T(8,128)} %fusion.2, bf16[256,1024]{1,0:T(8,128)(2,1)S(1)} %bitcast.131, bf16[1,2816,1024]{2,1,0:T(8,128)(2,1)} %param.17), kind=kOutput, calls=%fused_computation.75 | convolution fusion | flops 2957377536 | bytes 15466496 | tf_op jit(solution)/shard_map/dot_general | solution.py:26
  55.2 4.9 %collective-permute-done.21 = bf16[256,256]{1,0:T(8,128)(2,1)S(1)} collective-permute-done((bf16[256,256]{1,0:T(8,128)(2,1)S(1)}, bf16[256,256]{1,0:T(8,128)(2,1)S(1)}, u32[]{:S(2)}, u32[]{:S(2)}) %collective-permute-start.21) | collective-permute-done | bytes 131104 | tf_op jit(solution)/shard_map/ppermute | solution.py:99
  60.6 4.5 %collective-permute-done.22 = bf16[256,256]{1,0:T(8,128)(2,1)S(1)} collective-permute-done((bf16[256,256]{1,0:T(8,128)(2,1)S(1)}, bf16[256,256]{1,0:T(8,128)(2,1)S(1)}, u32[]{:S(2)}, u32[]{:S(2)}) %collective-permute-start.22) | collective-permute-done | bytes 131104 | tf_op jit(solution)/shard_map/ppermute | solution.py:99
  65.5 5.5 %collective-permute-done.23 = bf16[256,256]{1,0:T(8,128)(2,1)S(1)} collective-permute-done((bf16[256,256]{1,0:T(8,128)(2,1)S(1)}, bf16[256,256]{1,0:T(8,128)(2,1)S(1)}, u32[]{:S(2)}, u32[]{:S(2)}) %collective-permute-start.23) | collective-permute-done | bytes 131104 | tf_op jit(solution)/shard_map/ppermute | solution.py:99
  71.8 1.6 collective-permute-start.10
  73.4 1.7 constant_dynamic-update-slice_fusion.6
  75.7 1.8 constant_dynamic-update-slice_fusion.2
  77.4 5.2 %collective-permute-done.7 = bf16[352,512]{1,0:T(8,128)(2,1)} collective-permute-done((bf16[352,512]{1,0:T(8,128)(2,1)}, bf16[352,512]{1,0:T(8,128)(2,1)}, u32[]{:S(2)}, u32[]{:S(2)}) %collective-permute-start.7) | collective-permute-done | bytes 360480 | tf_op jit(solution)/shard_map/ppermute | solution.py:76
  82.7 1.7 constant_dynamic-update-slice_fusion.5
  84.4 2.0 collective-permute-done.10
  87.7 1.5 collective-permute-start.4
  89.2 2.0 constant_dynamic-update-slice_fusion.14
  91.8 1.5 collective-permute-start.2
  93.3 4.7 %collective-permute-done.11 = bf16[128,1408]{1,0:T(8,128)(2,1)S(1)} collective-permute-done((bf16[128,1408]{1,0:T(8,128)(2,1)}, bf16[128,1408]{1,0:T(8,128)(2,1)S(1)}, u32[]{:S(2)}, u32[]{:S(2)}) %collective-permute-start.11) | collective-permute-done | bytes 360480 | tf_op jit(solution)/shard_map/ppermute | solution.py:78
  99.2 2.1 %constant_dynamic-update-slice_fusion.13 = bf16[1408,1024]{1,0:T(8,128)(2,1)} fusion(bf16[1408,1024]{1,0:T(8,128)(2,1)} %constant_dynamic-update-slice_fusion.14, bf16[352,1024]{1,0:T(8,128)(2,1)} %collective-permute-done.1, s32[]{:T(128)S(6)} %select_n.200), kind=kLoop, calls=%fused_computation.165 | loop fusion | bytes 1441796 | tf_op jit(solution)/shard_map/dynamic_update_slice | solution.py:58
  101.3 1.5 collective-permute-done.8
  104.5 8.9 %collective-permute-done.4 = bf16[256,1408]{1,0:T(8,128)(2,1)S(1)} collective-permute-done((bf16[256,1408]{1,0:T(8,128)(2,1)S(1)}, bf16[256,1408]{1,0:T(8,128)(2,1)S(1)}, u32[]{:S(2)}, u32[]{:S(2)}) %collective-permute-start.4) | collective-permute-done | bytes 720928 | tf_op jit(solution)/shard_map/ppermute | solution.py:77
  116.1 10.2 %collective-permute-done.5 = bf16[256,1408]{1,0:T(8,128)(2,1)S(1)} collective-permute-done((bf16[256,1408]{1,0:T(8,128)(2,1)S(1)}, bf16[256,1408]{1,0:T(8,128)(2,1)S(1)}, u32[]{:S(2)}, u32[]{:S(2)}) %collective-permute-start.5) | collective-permute-done | bytes 720928 | tf_op jit(solution)/shard_map/ppermute | solution.py:78
  129.1 6.6 %fusion.73 = f32[640,1408]{1,0:T(8,128)} fusion(bf16[512,1408]{1,0:T(8,128)(2,1)} %constant_dynamic-update-slice_fusion, bf16[1408,512]{1,0:T(8,128)(2,1)} %constant_dynamic-update-slice_fusion.4, bf16[640,1408]{1,0:T(8,128)(2,1)} %copy-done.1, f32[640]{0:T(1024)S(1)} %add_rsqrt_fusion, f32[640]{0:T(1024)S(1)} %broadcast_multiply_fusion, f32[1408]{0:T(1024)S(1)} %copy-done.9), kind=kOutput, calls=%fused_computation.83 | convolution fusion | flops 1852948480 | bytes 8301056 | tf_op jit(solution)/shard_map/dot_general | solution.py:26
  135.7 10.0 %add_convert_fusion = bf16[640,1408]{1,0:T(8,128)(2,1)} fusion(f32[640,1408]{1,0:T(8,128)} %fusion.73, bf16[1024,1408]{1,0:T(8,128)(2,1)} %constant_dynamic-update-slice_fusion.8, bf16[1408,1024]{1,0:T(8,128)(2,1)} %constant_dynamic-update-slice_fusion.12, bf16[640,1408]{1,0:T(8,128)(2,1)} %copy-done.1, f32[640]{0:T(1024)S(1)} %add_rsqrt_fusion, ...), kind=kOutput, calls=%fused_computation.25 | convolution fusion | flops 3703193600 | bytes 12986880 | tf_op jit(solution)/shard_map/dot_general | solution.py:26
  147.7 3.0 %collective-permute-start.25 = (bf16[4,8192]{1,0:T(4,128)(2,1)S(1)}, bf16[4,8192]{1,0:T(4,128)(2,1)S(1)}, u32[]{:S(2)}, u32[]{:S(2)}) collective-permute-start(bf16[4,8192]{1,0:T(4,128)(2,1)S(1)} %bitcast.145), channel_id=1, source_target_pairs={{0,2},{1,3},{2,0},{3,1},{4,6},{5,7},{6,4},{7,5},{8,10},{9,11},{10,... | collective-permute-start | bytes 196616 | tf_op jit(solution)/shard_map/ppermute | solution.py:99
  151.6 2.5 %collective-permute-start.27 = (bf16[4,8192]{1,0:T(4,128)(2,1)S(1)}, bf16[4,8192]{1,0:T(4,128)(2,1)S(1)}, u32[]{:S(2)}, u32[]{:S(2)}) collective-permute-start(bf16[4,8192]{1,0:T(4,128)(2,1)S(1)} %bitcast.140), channel_id=1, source_target_pairs={{0,4},{1,5},{2,6},{3,7},{4,0},{5,1},{6,2},{7,3},{8,12},{9,13},{10,... | collective-permute-start | bytes 196616 | tf_op jit(solution)/shard_map/ppermute | solution.py:99
  156.1 2.5 %collective-permute-start.29 = (bf16[4,8192]{1,0:T(4,128)(2,1)}, bf16[4,8192]{1,0:T(4,128)(2,1)}, u32[]{:S(2)}, u32[]{:S(2)}) collective-permute-start(bf16[4,8192]{1,0:T(4,128)(2,1)} %bitcast.120), channel_id=1, source_target_pairs={{0,6},{1,7},{2,4},{3,5},{4,2},{5,3},{6,0},{7,1},{8,14},{9,15},{10,... | collective-permute-start | bytes 196616 | tf_op jit(solution)/shard_map/ppermute | solution.py:99
  159.5 2.2 %dynamic_update_slice.139 = bf16[8,4,8192]{2,0,1:T(8,128)(2,1)S(1)} dynamic-update-slice(bf16[8,4,8192]{2,0,1:T(8,128)(2,1)S(1)} %broadcast_in_dim.142, bf16[1,4,8192]{2,0,1:T(2,128)(2,1)S(1)} %get-tuple-element.27, s32[]{:T(128)S(6)} %select_n.222, s32[]{:T(128)} %constant.175.clone.1, s32[]{:T(128)} %constant.175.clone.1) | dynamic-update-slice | bytes 131076 | tf_op jit(solution)/shard_map/jit(dynamic_update_index_in_dim)/dynamic_update_slice | solution.py:94
  164.2 1.7 copy.33
  165.8 1.6 copy.34
  167.4 1.6 copy.35
  169.0 2.9 %dynamic_update_slice.140 = bf16[8,4,8192]{2,0,1:T(8,128)(2,1)S(1)} dynamic-update-slice(bf16[8,4,8192]{2,0,1:T(8,128)(2,1)S(1)} %dynamic_update_slice.139, bf16[1,4,8192]{2,0,1:T(2,128)(2,1)} %copy.29, s32[]{:T(128)S(6)} %select_n.223, s32[]{:T(128)} %constant.175.clone.1, s32[]{:T(128)} %constant.175.clone.1) | dynamic-update-slice | bytes 131076 | tf_op jit(solution)/shard_map/jit(dynamic_update_index_in_dim)/dynamic_update_slice | solution.py:100
  172.0 2.0 dynamic_update_slice.141
  174.0 2.0 dynamic_update_slice.142
  176.0 2.0 dynamic_update_slice.143
  178.0 3.0 %dynamic_update_slice.144 = bf16[8,4,8192]{2,0,1:T(8,128)(2,1)S(1)} dynamic-update-slice(bf16[8,4,8192]{2,0,1:T(8,128)(2,1)S(1)} %dynamic_update_slice.143, bf16[1,4,8192]{2,0,1:T(2,128)(2,1)} %copy.33, s32[]{:T(128)S(6)} %select_n.227, s32[]{:T(128)} %constant.175.clone.1, s32[]{:T(128)} %constant.175.clone.1) | dynamic-update-slice | bytes 131076 | tf_op jit(solution)/shard_map/jit(dynamic_update_index_in_dim)/dynamic_update_slice | solution.py:100
  181.0 3.0 %dynamic_update_slice.145 = bf16[8,4,8192]{2,0,1:T(8,128)(2,1)S(1)} dynamic-update-slice(bf16[8,4,8192]{2,0,1:T(8,128)(2,1)S(1)} %dynamic_update_slice.144, bf16[1,4,8192]{2,0,1:T(2,128)(2,1)} %copy.34, s32[]{:T(128)S(6)} %select_n.228, s32[]{:T(128)} %constant.175.clone.1, s32[]{:T(128)} %constant.175.clone.1) | dynamic-update-slice | bytes 131076 | tf_op jit(solution)/shard_map/jit(dynamic_update_index_in_dim)/dynamic_update_slice | solution.py:100
  184.0 3.0 %dynamic_update_slice.146 = bf16[8,4,8192]{2,0,1:T(8,128)(2,1)S(1)} dynamic-update-slice(bf16[8,4,8192]{2,0,1:T(8,128)(2,1)S(1)} %dynamic_update_slice.145, bf16[1,4,8192]{2,0,1:T(2,128)(2,1)} %copy.35, s32[]{:T(128)S(6)} %select_n.229, s32[]{:T(128)} %constant.175.clone.1, s32[]{:T(128)} %constant.175.clone.1) | dynamic-update-slice | bytes 131076 | tf_op jit(solution)/shard_map/jit(dynamic_update_index_in_dim)/dynamic_update_slice | solution.py:100
  187.1 1.5 fusion.135
  188.6 2.0 fusion.67
  190.7 6.0 %fusion.75 = f32[640,1408]{1,0:T(8,128)} fusion(bf16[512,1408]{1,0:T(8,128)(2,1)} %constant_dynamic-update-slice_fusion, bf16[1408,512]{1,0:T(8,128)(2,1)} %constant_dynamic-update-slice_fusion.4, bf16[640,1408]{1,0:T(8,128)(2,1)S(1)} %copy-done, f32[1408]{0:T(1024)S(1)} %copy-done.9, f32[640]{0:T(1024)S(1)} %add_rsqrt_fusion.1, ...), kind=kOutput, calls=%fused_computation.84 | convolution fusion | flops 1852948480 | bytes 8301056 | tf_op jit(solution)/shard_map/dot_general | solution.py:26
  196.7 10.0 %fusion.17 = bf16[640,1408]{1,0:T(8,128)(2,1)} fusion(bf16[640,1408]{1,0:T(8,128)(2,1)S(1)} %copy-done, bf16[640,1408]{1,0:T(8,128)(2,1)} %collective-permute-done.13, f32[640,1408]{1,0:T(8,128)} %fusion.75, bf16[1024,1408]{1,0:T(8,128)(2,1)} %constant_dynamic-update-slice_fusion.8, bf16[1408,1024]{1,0:T(8,128)(2,1)} %constant_dynamic-update-slice_fusion.12, ...), kind=kOutput, calls=%fused_computation.24 | convolution fusion | flops 3706798080 | bytes 14789120 | tf_op jit(solution)/shard_map/dot_general | solution.py:26
  (128 shorter events, 39.0 us)
Async XLA Ops:
  1.9 7.8 %copy-start.7 = (s32[384,2]{0,1:T(2,128)S(1)}, s32[384,2]{0,1:T(2,128)}, u32[]{:S(2)}) copy-start(s32[384,2]{0,1:T(2,128)} %param.15) | copy-start | bytes 9220
  1.9 8.2 %copy-start.3 = (bf16[384,1024]{1,0:T(8,128)(2,1)S(1)}, bf16[384,1024]{1,0:T(8,128)(2,1)}, u32[]{:S(2)}) copy-start(bf16[384,1024]{1,0:T(8,128)(2,1)} %param.14) | copy-start | bytes 2359300
  3.9 9.3 %copy-start.8 = (f32[384,2]{0,1:T(2,128)S(1)}, f32[384,2]{0,1:T(2,128)}, u32[]{:S(2)}) copy-start(f32[384,2]{0,1:T(2,128)} %param.16) | copy-start | bytes 9220
  5.2 82.5 %collective-permute-start = (bf16[352,1024]{1,0:T(8,128)(2,1)}, bf16[352,1024]{1,0:T(8,128)(2,1)}, u32[]{:S(2)}, u32[]{:S(2)}) collective-permute-start(bf16[352,1024]{1,0:T(8,128)(2,1)} %get-tuple-element.18), channel_id=1, source_target_pairs={{0,8},{8,0},{16,24},{24,16},{1,9},{9,1},{17,25},{25,17},{2,10},{10... | collective-permute-start | bytes 2162696 | tf_op jit(solution)/shard_map/ppermute | solution.py:76
  8.2 83.1 %collective-permute-start.1 = (bf16[352,1024]{1,0:T(8,128)(2,1)}, bf16[352,1024]{1,0:T(8,128)(2,1)}, u32[]{:S(2)}, u32[]{:S(2)}) collective-permute-start(bf16[352,1024]{1,0:T(8,128)(2,1)} %get-tuple-element.18), channel_id=1, source_target_pairs={{0,16},{8,24},{16,0},{24,8},{1,17},{9,25},{17,1},{25,9},{2,18},{10... | collective-permute-start | bytes 2162696 | tf_op jit(solution)/shard_map/ppermute | solution.py:76
  9.8 5.8 %copy-start = (bf16[640,1408]{1,0:T(8,128)(2,1)S(1)}, bf16[640,1408]{1,0:T(8,128)(2,1)}, u32[]{:S(2)}) copy-start(bf16[640,1408]{1,0:T(8,128)(2,1)} %param.10) | copy-start | bytes 5406724
  11.4 13.7 %collective-permute-start.14 = (bf16[32,1024]{1,0:T(8,128)(2,1)}, bf16[32,1024]{1,0:T(8,128)(2,1)}, u32[]{:S(2)}, u32[]{:S(2)}) collective-permute-start(bf16[32,1024]{1,0:T(8,128)(2,1)} %get-tuple-element.38), channel_id=1, source_target_pairs={{0,1},{1,0},{2,3},{3,2},{4,5},{5,4},{6,7},{7,6},{8,9},{9,8},{10,11... | collective-permute-start | bytes 196616 | tf_op jit(solution)/shard_map/ppermute | solution.py:99
  11.4 17.2 %collective-permute-start.15 = (bf16[32,1024]{1,0:T(8,128)(2,1)}, bf16[32,1024]{1,0:T(8,128)(2,1)S(1)}, u32[]{:S(2)}, u32[]{:S(2)}) collective-permute-start(bf16[32,1024]{1,0:T(8,128)(2,1)} %get-tuple-element.37), channel_id=1, source_target_pairs={{0,2},{1,3},{2,0},{3,1},{4,6},{5,7},{6,4},{7,5},{8,10},{9,11},{10,... | collective-permute-start | bytes 196616 | tf_op jit(solution)/shard_map/ppermute | solution.py:99
  13.0 15.7 %collective-permute-start.16 = (bf16[32,1024]{1,0:T(8,128)(2,1)S(1)}, bf16[32,1024]{1,0:T(8,128)(2,1)S(1)}, u32[]{:S(2)}, u32[]{:S(2)}) collective-permute-start(bf16[32,1024]{1,0:T(8,128)(2,1)S(1)} %get-tuple-element.36), channel_id=1, source_target_pairs={{0,3},{1,2},{2,1},{3,0},{4,7},{5,6},{6,5},{7,4},{8,11},{9,10},{10,... | collective-permute-start | bytes 196616 | tf_op jit(solution)/shard_map/ppermute | solution.py:99
  16.0 2.7 %copy-start.5 = (bf16[768,1408]{1,0:T(8,128)(2,1)S(1)}, bf16[768,1408]{1,0:T(8,128)(2,1)}, u32[]{:S(2)}) copy-start(bf16[768,1408]{1,0:T(8,128)(2,1)} %param.13) | copy-start | bytes 6488068
  25.1 7.2 %collective-permute-start.17 = (bf16[32,1024]{1,0:T(8,128)(2,1)S(1)}, bf16[32,1024]{1,0:T(8,128)(2,1)S(1)}, u32[]{:S(2)}, u32[]{:S(2)}) collective-permute-start(bf16[32,1024]{1,0:T(8,128)(2,1)S(1)} %get-tuple-element.35), channel_id=1, source_target_pairs={{0,4},{1,5},{2,6},{3,7},{4,0},{5,1},{6,2},{7,3},{8,12},{9,13},{10,... | collective-permute-start | bytes 196616 | tf_op jit(solution)/shard_map/ppermute | solution.py:99
  28.6 8.0 %collective-permute-start.18 = (bf16[32,1024]{1,0:T(8,128)(2,1)S(1)}, bf16[32,1024]{1,0:T(8,128)(2,1)S(1)}, u32[]{:S(2)}, u32[]{:S(2)}) collective-permute-start(bf16[32,1024]{1,0:T(8,128)(2,1)S(1)} %get-tuple-element.34), channel_id=1, source_target_pairs={{0,5},{1,4},{2,7},{3,6},{4,1},{5,0},{6,3},{7,2},{8,13},{9,12},{10,... | collective-permute-start | bytes 196616 | tf_op jit(solution)/shard_map/ppermute | solution.py:99
  28.7 8.4 %collective-permute-start.19 = (bf16[32,1024]{1,0:T(8,128)(2,1)S(1)}, bf16[32,1024]{1,0:T(8,128)(2,1)S(1)}, u32[]{:S(2)}, u32[]{:S(2)}) collective-permute-start(bf16[32,1024]{1,0:T(8,128)(2,1)S(1)} %get-tuple-element.33), channel_id=1, source_target_pairs={{0,6},{1,7},{2,4},{3,5},{4,2},{5,3},{6,0},{7,1},{8,14},{9,15},{10,... | collective-permute-start | bytes 196616 | tf_op jit(solution)/shard_map/ppermute | solution.py:99
  32.3 6.4 %collective-permute-start.20 = (bf16[32,1024]{1,0:T(8,128)(2,1)S(1)}, bf16[32,1024]{1,0:T(8,128)(2,1)S(1)}, u32[]{:S(2)}, u32[]{:S(2)}) collective-permute-start(bf16[32,1024]{1,0:T(8,128)(2,1)S(1)} %get-tuple-element.32), channel_id=1, source_target_pairs={{0,7},{1,6},{2,5},{3,4},{4,3},{5,2},{6,1},{7,0},{8,15},{9,14},{10,... | collective-permute-start | bytes 196616 | tf_op jit(solution)/shard_map/ppermute | solution.py:99
  36.5 35.2 %collective-permute-start.6 = (bf16[352,512]{1,0:T(8,128)(2,1)}, bf16[352,512]{1,0:T(8,128)(2,1)}, u32[]{:S(2)}, u32[]{:S(2)}) collective-permute-start(bf16[352,512]{1,0:T(8,128)(2,1)} %get-tuple-element.40), channel_id=1, source_target_pairs={{0,8},{8,0},{16,24},{24,16},{1,9},{9,1},{17,25},{25,17},{2,10},{10... | collective-permute-start | bytes 1081352 | tf_op jit(solution)/shard_map/ppermute | solution.py:76
  37.1 38.0 %collective-permute-start.9 = (bf16[128,1408]{1,0:T(8,128)(2,1)S(1)}, bf16[128,1408]{1,0:T(8,128)(2,1)}, u32[]{:S(2)}, u32[]{:S(2)}) collective-permute-start(bf16[128,1408]{1,0:T(8,128)(2,1)S(1)} %get-tuple-element.9), channel_id=1, source_target_pairs={{0,8},{8,0},{16,24},{24,16},{1,9},{9,1},{17,25},{25,17},{2,10},{10... | collective-permute-start | bytes 1081352 | tf_op jit(solution)/shard_map/ppermute | solution.py:77
  54.5 5.6 %collective-permute-start.21 = (bf16[256,256]{1,0:T(8,128)(2,1)S(1)}, bf16[256,256]{1,0:T(8,128)(2,1)S(1)}, u32[]{:S(2)}, u32[]{:S(2)}) collective-permute-start(bf16[256,256]{1,0:T(8,128)(2,1)S(1)} %bitcast.136), channel_id=1, source_target_pairs={{0,8},{8,0},{16,24},{24,16},{1,9},{9,1},{17,25},{25,17},{2,10},{10... | collective-permute-start | bytes 393224 | tf_op jit(solution)/shard_map/ppermute | solution.py:99
  60.1 5.0 %collective-permute-start.22 = (bf16[256,256]{1,0:T(8,128)(2,1)S(1)}, bf16[256,256]{1,0:T(8,128)(2,1)S(1)}, u32[]{:S(2)}, u32[]{:S(2)}) collective-permute-start(bf16[256,256]{1,0:T(8,128)(2,1)S(1)} %bitcast.135), channel_id=1, source_target_pairs={{0,16},{8,24},{16,0},{24,8},{1,17},{9,25},{17,1},{25,9},{2,18},{10... | collective-permute-start | bytes 393224 | tf_op jit(solution)/shard_map/ppermute | solution.py:99
  65.1 5.9 %collective-permute-start.23 = (bf16[256,256]{1,0:T(8,128)(2,1)S(1)}, bf16[256,256]{1,0:T(8,128)(2,1)S(1)}, u32[]{:S(2)}, u32[]{:S(2)}) collective-permute-start(bf16[256,256]{1,0:T(8,128)(2,1)S(1)} %bitcast.134), channel_id=1, source_target_pairs={{0,24},{8,16},{16,8},{24,0},{1,25},{9,17},{17,9},{25,1},{2,26},{10... | collective-permute-start | bytes 393224 | tf_op jit(solution)/shard_map/ppermute | solution.py:99
  71.0 11.7 %collective-permute-start.7 = (bf16[352,512]{1,0:T(8,128)(2,1)}, bf16[352,512]{1,0:T(8,128)(2,1)}, u32[]{:S(2)}, u32[]{:S(2)}) collective-permute-start(bf16[352,512]{1,0:T(8,128)(2,1)} %get-tuple-element.40), channel_id=1, source_target_pairs={{0,16},{8,24},{16,0},{24,8},{1,17},{9,25},{17,1},{25,9},{2,18},{10... | collective-permute-start | bytes 1081352 | tf_op jit(solution)/shard_map/ppermute | solution.py:76
  71.7 16.0 %copy-start.4 = (bf16[256,1408]{1,0:T(8,128)(2,1)S(1)}, bf16[256,1408]{1,0:T(8,128)(2,1)}, u32[]{:S(2)}) copy-start(bf16[256,1408]{1,0:T(8,128)(2,1)} %get-tuple-element.7) | copy-start | bytes 2162692
  71.8 14.7 %collective-permute-start.10 = (bf16[128,1408]{1,0:T(8,128)(2,1)S(1)}, bf16[128,1408]{1,0:T(8,128)(2,1)S(1)}, u32[]{:S(2)}, u32[]{:S(2)}) collective-permute-start(bf16[128,1408]{1,0:T(8,128)(2,1)S(1)} %get-tuple-element.9), channel_id=1, source_target_pairs={{0,16},{8,24},{16,0},{24,8},{1,17},{9,25},{17,1},{25,9},{2,18},{10... | collective-permute-start | bytes 1081352 | tf_op jit(solution)/shard_map/ppermute | solution.py:77
  75.1 16.7 %collective-permute-start.3 = (bf16[256,1408]{1,0:T(8,128)(2,1)}, bf16[256,1408]{1,0:T(8,128)(2,1)S(1)}, u32[]{:S(2)}, u32[]{:S(2)}) collective-permute-start(bf16[256,1408]{1,0:T(8,128)(2,1)} %get-tuple-element.7), channel_id=1, source_target_pairs={{0,8},{8,0},{16,24},{24,16},{1,9},{9,1},{17,25},{25,17},{2,10},{10... | collective-permute-start | bytes 2162696 | tf_op jit(solution)/shard_map/ppermute | solution.py:77
  82.7 44.6 %collective-permute-start.12 = (bf16[640,1408]{1,0:T(8,128)(2,1)S(1)}, bf16[640,1408]{1,0:T(8,128)(2,1)S(1)}, u32[]{:S(2)}, u32[]{:S(2)}) collective-permute-start(bf16[640,1408]{1,0:T(8,128)(2,1)S(1)} %copy-done), channel_id=1, source_target_pairs={{0,1},{1,0},{2,3},{3,2},{4,5},{5,4},{6,7},{7,6},{8,9},{9,8},{10,11... | collective-permute-start | bytes 5406728 | tf_op jit(solution)/shard_map/ppermute | solution.py:53
  86.4 11.6 %collective-permute-start.11 = (bf16[128,1408]{1,0:T(8,128)(2,1)}, bf16[128,1408]{1,0:T(8,128)(2,1)S(1)}, u32[]{:S(2)}, u32[]{:S(2)}) collective-permute-start(bf16[128,1408]{1,0:T(8,128)(2,1)} %collective-permute-done.9), channel_id=1, source_target_pairs={{0,16},{8,24},{16,0},{24,8},{1,17},{9,25},{17,1},{25,9},{2,18},{10... | collective-permute-start | bytes 1081352 | tf_op jit(solution)/shard_map/ppermute | solution.py:78
  87.7 25.7 %collective-permute-start.4 = (bf16[256,1408]{1,0:T(8,128)(2,1)S(1)}, bf16[256,1408]{1,0:T(8,128)(2,1)S(1)}, u32[]{:S(2)}, u32[]{:S(2)}) collective-permute-start(bf16[256,1408]{1,0:T(8,128)(2,1)S(1)} %copy-done.4), channel_id=1, source_target_pairs={{0,16},{8,24},{16,0},{24,8},{1,17},{9,25},{17,1},{25,9},{2,18},{10... | collective-permute-start | bytes 2162696 | tf_op jit(solution)/shard_map/ppermute | solution.py:77
  91.3 11.6 %collective-permute-start.8 = (bf16[352,512]{1,0:T(8,128)(2,1)}, bf16[352,512]{1,0:T(8,128)(2,1)S(1)}, u32[]{:S(2)}, u32[]{:S(2)}) collective-permute-start(bf16[352,512]{1,0:T(8,128)(2,1)} %collective-permute-done.7), channel_id=1, source_target_pairs={{0,8},{8,0},{16,24},{24,16},{1,9},{9,1},{17,25},{25,17},{2,10},{10... | collective-permute-start | bytes 1081352 | tf_op jit(solution)/shard_map/ppermute | solution.py:78
  91.8 23.4 %collective-permute-start.2 = (bf16[352,1024]{1,0:T(8,128)(2,1)}, bf16[352,1024]{1,0:T(8,128)(2,1)S(1)}, u32[]{:S(2)}, u32[]{:S(2)}) collective-permute-start(bf16[352,1024]{1,0:T(8,128)(2,1)} %collective-permute-done.1), channel_id=1, source_target_pairs={{0,8},{8,0},{16,24},{24,16},{1,9},{9,1},{17,25},{25,17},{2,10},{10... | collective-permute-start | bytes 2162696 | tf_op jit(solution)/shard_map/ppermute | solution.py:78
  98.0 28.3 %collective-permute-start.5 = (bf16[256,1408]{1,0:T(8,128)(2,1)S(1)}, bf16[256,1408]{1,0:T(8,128)(2,1)S(1)}, u32[]{:S(2)}, u32[]{:S(2)}) collective-permute-start(bf16[256,1408]{1,0:T(8,128)(2,1)S(1)} %collective-permute-done.3), channel_id=1, source_target_pairs={{0,16},{8,24},{16,0},{24,8},{1,17},{9,25},{17,1},{25,9},{2,18},{10... | collective-permute-start | bytes 2162696 | tf_op jit(solution)/shard_map/ppermute | solution.py:78
  116.1 13.0 %copy-start.9 = (f32[1408]{0:T(1024)S(1)}, f32[1408]{0:T(1024)}, u32[]{:S(2)}) copy-start(f32[1408]{0:T(1024)} %param.11) | copy-start | bytes 16900
  127.3 1.2 copy-start.1
  145.7 51.0 %collective-permute-start.13 = (bf16[640,1408]{1,0:T(8,128)(2,1)}, bf16[640,1408]{1,0:T(8,128)(2,1)}, u32[]{:S(2)}, u32[]{:S(2)}) collective-permute-start(bf16[640,1408]{1,0:T(8,128)(2,1)} %add_convert_fusion), channel_id=1, source_target_pairs={{0,1},{1,0},{2,3},{3,2},{4,5},{5,4},{6,7},{7,6},{8,9},{9,8},{10,11... | collective-permute-start | bytes 5406728 | tf_op jit(solution)/shard_map/ppermute | solution.py:87
  147.1 8.6 %collective-permute-start.24 = (bf16[4,8192]{1,0:T(4,128)(2,1)S(1)}, bf16[4,8192]{1,0:T(4,128)(2,1)S(1)}, u32[]{:S(2)}, u32[]{:S(2)}) collective-permute-start(bf16[4,8192]{1,0:T(4,128)(2,1)S(1)} %bitcast.146), channel_id=1, source_target_pairs={{0,1},{1,0},{2,3},{3,2},{4,5},{5,4},{6,7},{7,6},{8,9},{9,8},{10,11... | collective-permute-start | bytes 196616 | tf_op jit(solution)/shard_map/ppermute | solution.py:99
  147.7 8.4 %collective-permute-start.25 = (bf16[4,8192]{1,0:T(4,128)(2,1)S(1)}, bf16[4,8192]{1,0:T(4,128)(2,1)S(1)}, u32[]{:S(2)}, u32[]{:S(2)}) collective-permute-start(bf16[4,8192]{1,0:T(4,128)(2,1)S(1)} %bitcast.145), channel_id=1, source_target_pairs={{0,2},{1,3},{2,0},{3,1},{4,6},{5,7},{6,4},{7,5},{8,10},{9,11},{10,... | collective-permute-start | bytes 196616 | tf_op jit(solution)/shard_map/ppermute | solution.py:99
  150.8 7.8 %collective-permute-start.26 = (bf16[4,8192]{1,0:T(4,128)(2,1)S(1)}, bf16[4,8192]{1,0:T(4,128)(2,1)S(1)}, u32[]{:S(2)}, u32[]{:S(2)}) collective-permute-start(bf16[4,8192]{1,0:T(4,128)(2,1)S(1)} %bitcast.144), channel_id=1, source_target_pairs={{0,3},{1,2},{2,1},{3,0},{4,7},{5,6},{6,5},{7,4},{8,11},{9,10},{10,... | collective-permute-start | bytes 196616 | tf_op jit(solution)/shard_map/ppermute | solution.py:99
  151.6 11.0 %collective-permute-start.27 = (bf16[4,8192]{1,0:T(4,128)(2,1)S(1)}, bf16[4,8192]{1,0:T(4,128)(2,1)S(1)}, u32[]{:S(2)}, u32[]{:S(2)}) collective-permute-start(bf16[4,8192]{1,0:T(4,128)(2,1)S(1)} %bitcast.140), channel_id=1, source_target_pairs={{0,4},{1,5},{2,6},{3,7},{4,0},{5,1},{6,2},{7,3},{8,12},{9,13},{10,... | collective-permute-start | bytes 196616 | tf_op jit(solution)/shard_map/ppermute | solution.py:99
  155.7 7.9 %collective-permute-start.28 = (bf16[4,8192]{1,0:T(4,128)(2,1)S(1)}, bf16[4,8192]{1,0:T(4,128)(2,1)S(1)}, u32[]{:S(2)}, u32[]{:S(2)}) collective-permute-start(bf16[4,8192]{1,0:T(4,128)(2,1)S(1)} %bitcast.142), channel_id=1, source_target_pairs={{0,5},{1,4},{2,7},{3,6},{4,1},{5,0},{6,3},{7,2},{8,13},{9,12},{10,... | collective-permute-start | bytes 196616 | tf_op jit(solution)/shard_map/ppermute | solution.py:99
  156.1 9.7 %collective-permute-start.29 = (bf16[4,8192]{1,0:T(4,128)(2,1)}, bf16[4,8192]{1,0:T(4,128)(2,1)}, u32[]{:S(2)}, u32[]{:S(2)}) collective-permute-start(bf16[4,8192]{1,0:T(4,128)(2,1)} %bitcast.120), channel_id=1, source_target_pairs={{0,6},{1,7},{2,4},{3,5},{4,2},{5,3},{6,0},{7,1},{8,14},{9,15},{10,... | collective-permute-start | bytes 196616 | tf_op jit(solution)/shard_map/ppermute | solution.py:99
  158.6 8.8 %collective-permute-start.30 = (bf16[4,8192]{1,0:T(4,128)(2,1)}, bf16[4,8192]{1,0:T(4,128)(2,1)}, u32[]{:S(2)}, u32[]{:S(2)}) collective-permute-start(bf16[4,8192]{1,0:T(4,128)(2,1)} %bitcast.119), channel_id=1, source_target_pairs={{0,7},{1,6},{2,5},{3,4},{4,3},{5,2},{6,1},{7,0},{8,15},{9,14},{10,... | collective-permute-start | bytes 196616 | tf_op jit(solution)/shard_map/ppermute | solution.py:99
  163.5 0.6 copy-start.6
  164.1 24.5 %copy-start.2 = (bf16[32,32,384]{2,1,0:T(8,128)(2,1)S(1)}, bf16[32,32,384]{2,1,0:T(8,128)(2,1)}, u32[]{:S(2)}) copy-start(bf16[32,32,384]{2,1,0:T(8,128)(2,1)} %fusion.34) | copy-start | bytes 2359300

commit v2 on v0

v2 whole, which is shorter than its diff:
```python
import jax
import jax.numpy as jnp
from jax import lax
from jax.experimental import pallas as pl
from jax.experimental.pallas import tpu as pltpu
from jax.sharding import PartitionSpec as P

EXP_DEV = 4
TOP = 2
CAP = 32
BF = jnp.bfloat16
F32 = jnp.float32


def xor_perm(size, bits):
    return [(i, i ^ bits) for i in range(size)]


def norm_rows(rows, gain):
    values = rows.astype(F32)
    average = jnp.mean(values, axis=-1, keepdims=True)
    centered = values - average
    variance = jnp.mean(centered * centered, axis=-1, keepdims=True)
    return (centered * lax.rsqrt(variance + 1e-06) * gain).astype(BF)


def dot(a, b):
    return jnp.dot(a, b, preferred_element_type=F32)


def feed_forward(normed, up, down):
    hidden = jax.nn.gelu(dot(normed, up), approximate=True).astype(BF)
    return dot(hidden, down)


def target_gathered(target_in, ln_gain, up_target, down_target):
    normed = norm_rows(target_in, ln_gain)
    projected = feed_forward(
        normed,
        lax.all_gather(up_target, "dp", axis=0, tiled=True),
        lax.all_gather(down_target, "dp", axis=0, tiled=True),
    )
    return (target_in.astype(F32) + projected).astype(BF)


def after(value, *others):
    return lax.optimization_barrier((value, others))[0]


def gelu(v):
    return 0.5 * v * (1.0 + jnp.tanh(0.7978845608028654 * (v + 0.044715 * (v * v * v))))


def cut_up_kernel(at_ref, up_ref, top_ref, low_ref):
    rows = top_ref.shape[0]
    top_ref[...] = up_ref[:rows, :]
    low_ref[...] = up_ref[rows:, :]


def cut_up(at, up_target):
    depth, width = up_target.shape
    part = jax.ShapeDtypeStruct((depth // 2, width // 2), BF)
    block = width // 8
    out = pl.BlockSpec((depth // 2, block), lambda j, at: (0, j))
    return pl.pallas_call(
        cut_up_kernel,
        out_shape=(part, part),
        grid_spec=pltpu.PrefetchScalarGridSpec(
            num_scalar_prefetch=1,
            grid=(4,),
            in_specs=[
                pl.BlockSpec((depth, block), lambda j, at: (0, (at[0] ^ j) * 2 + at[1]))
            ],
            out_specs=(out, out),
        ),
        compiler_params=pltpu.CompilerParams(vmem_limit_bytes=8 * 2**20),
        cost_estimate=pl.CostEstimate(
            flops=0, bytes_accessed=2 * depth * width, transcendentals=0
        ),
        name="cut_up",
    )(at, up_target)


def up_kernel(at_ref, other_ref, own_ref, *refs):
    pieces, (out_ref, x_ref, w_ref, sem, x_sem) = refs[:8], refs[8:]
    step = pl.program_id(0)
    depth, width = pieces[0].shape
    block = width // 4
    me = at_ref[0]
    rows = own_ref.shape[0]
    tile = out_ref.shape[1]
    x_made = [
        pltpu.make_async_copy(ref, x_ref.at[pl.ds(i * rows, rows)], x_sem.at[i])
        for i, ref in enumerate((other_ref, own_ref))
    ]

    def copies(n):
        found = []
        for j in (2 * n, 2 * n + 1):
            for p, piece in enumerate(pieces):
                i, h = p // 2, p % 2
                row = pl.multiple_of(((me ^ i) * 2 + h) * depth, 16)
                found.append(
                    pltpu.make_async_copy(
                        piece.at[:, pl.ds((j ^ i) * block, block)],
                        w_ref.at[pl.ds(row, depth), pl.ds(j * block, block)],
                        sem.at[n, len(found)],
                    )
                )
        return found

    @pl.when(step == 0)
    def _():
        for c in copies(0) + x_made + copies(1):
            c.start()
        for c in copies(0) + x_made:
            c.wait()

    @pl.when(step == pl.num_programs(0) // 2)
    def _():
        for c in copies(1):
            c.wait()

    w = w_ref[:, pl.ds(pl.multiple_of(step * tile, tile), tile)]
    out_ref[...] = gelu(dot(x_ref[...], w)).astype(BF)


def up_call(at, other_n, own_n, pieces):
    rows, depth = own_n.shape
    width = pieces[0].shape[1]
    tile = 256
    hbm = pl.BlockSpec(memory_space=pltpu.HBM)
    return pl.pallas_call(
        up_kernel,
        out_shape=jax.ShapeDtypeStruct((2 * rows, width), BF),
        grid=(width // tile,),
        in_specs=[pl.BlockSpec(memory_space=pltpu.SMEM)] + [hbm] * 10,
        out_specs=pl.BlockSpec((2 * rows, tile), lambda n: (0, n)),
        scratch_shapes=[
            pltpu.VMEM((2 * rows, depth), BF),
            pltpu.VMEM((depth, width), BF),
            pltpu.SemaphoreType.DMA((2, 16)),
            pltpu.SemaphoreType.DMA((2,)),
        ],
        compiler_params=pltpu.CompilerParams(vmem_limit_bytes=20 * 2**20),
        cost_estimate=pl.CostEstimate(
            flops=8 * rows * depth * width, bytes_accessed=12 * 10**6, transcendentals=0
        ),
        name="up",
    )(at, other_n, own_n, *pieces)


def down_kernel(h_ref, *refs):
    pieces, (out_ref, w_ref, sem) = refs[:6], refs[6:]
    count = pieces[0].shape[0]

    @pl.when(pl.program_id(0) == 0)
    def _():
        made = [
            pltpu.make_async_copy(piece, w_ref.at[pl.ds(i * count, count)], sem.at[i])
            for i, piece in enumerate(pieces)
        ]
        for c in made:
            c.start()
        for c in made:
            c.wait()

    out_ref[...] = dot(h_ref[:, : 6 * count], w_ref[...])


def down_call(hidden, pieces):
    rows, width = hidden.shape
    count, wide = pieces[0].shape
    tile = 320
    return pl.pallas_call(
        down_kernel,
        out_shape=jax.ShapeDtypeStruct((rows, wide), F32),
        grid=(rows // tile,),
        in_specs=[pl.BlockSpec((tile, width), lambda m: (m, 0))]
        + [pl.BlockSpec(memory_space=pltpu.HBM)] * 6,
        out_specs=pl.BlockSpec((tile, wide), lambda m: (m, 0)),
        scratch_shapes=[
            pltpu.VMEM((6 * count, wide), BF),
            pltpu.SemaphoreType.DMA((6,)),
        ],
        compiler_params=pltpu.CompilerParams(vmem_limit_bytes=20 * 2**20),
        cost_estimate=pl.CostEstimate(
            flops=16 * rows * count * wide, bytes_accessed=15 * 10**6, transcendentals=0
        ),
        name="down",
    )(hidden, *pieces)


def last_kernel(h_ref, da, db, sum_ref, *refs):
    top = da.shape[0]
    out_ref = refs[-1]
    total = sum_ref[...] + dot(h_ref[:, :top], da[...]) + dot(h_ref[:, top:], db[...])
    if len(refs) == 2:
        total = total + refs[0][...].astype(F32)
    out_ref[...] = total.astype(out_ref.dtype)


def last_call(hidden, da, db, sums, first, rows_in, dtype):
    top, wide = da.shape
    count = hidden.shape[1] // 4
    rows, tile = hidden.shape[0] // 2, 320
    skip = first // tile
    whole = pl.BlockSpec((top, wide), lambda m: (0, 0))
    extra = [] if rows_in is None else [rows_in]
    return pl.pallas_call(
        last_kernel,
        out_shape=jax.ShapeDtypeStruct((rows, wide), dtype),
        grid=(rows // tile,),
        in_specs=[
            pl.BlockSpec((tile, count), lambda m: (m + skip, 3)),
            whole,
            whole,
            pl.BlockSpec((tile, wide), lambda m: (m + skip, 0)),
        ]
        + [pl.BlockSpec((tile, wide), lambda m: (m, 0)) for _ in extra],
        out_specs=pl.BlockSpec((tile, wide), lambda m: (m, 0)),
        compiler_params=pltpu.CompilerParams(vmem_limit_bytes=24 * 2**20),
        cost_estimate=pl.CostEstimate(
            flops=3 * rows * count * wide, bytes_accessed=6 * 10**6, transcendentals=0
        ),
        name="last",
    )(hidden, da, db, sums, *extra)


def program_square(
    target_in,
    ln_gain,
    up_target,
    down_target,
    pred_rows,
    expert_ids,
    combine_weights,
    gate_experts,
    up_experts,
    down_experts,
):
    depth, width = up_target.shape
    block = width // 4
    half = block // 2
    wide = down_target.shape[1]
    me = lax.axis_index("dp")
    core = lax.axis_index("expert") % 2
    px, py = xor_perm(4, 1), xor_perm(4, 2)
    pc = xor_perm(lax.axis_size("expert"), 1)

    at = jnp.stack([me, core]).astype(jnp.int32)

    def both(parts):
        return [lax.ppermute(parts[h], "dp", p) for p in (px, py) for h in range(2)]

    ups = cut_up(at, up_target)
    ux_t, ux_b, uy_t, uy_b = both(ups)
    dispatched = lax.all_to_all(
        dispatch_rows(pred_rows, expert_ids), "expert", 0, 0, tiled=True
    )
    other_in = lax.ppermute(target_in, "expert", pc)
    ud_t, ud_b = lax.ppermute(uy_t, "dp", px), lax.ppermute(ux_b, "dp", py)
    part = half // 2
    downs = [
        lax.dynamic_slice(down_target, (core * half + h * part, 0), (part, wide))
        for h in range(2)
    ]
    dx_t, dx_b, dy_t, dy_b = both([after(d, ux_b, uy_t) for d in downs])
    dd_t, dd_b = lax.ppermute(dy_t, "dp", px), lax.ppermute(dx_b, "dp", py)
    other_n, own_n = norm_rows(other_in, ln_gain), norm_rows(target_in, ln_gain)
    dispatched = after(dispatched, ux_b, uy_t, other_n, own_n)
    by_cols = expert_call(dispatched, gate_experts, up_experts, down_experts)
    back = lax.all_to_all(by_cols, ("dp", "expert"), 0, 0, tiled=True)
    hidden = up_call(
        at,
        after(other_n, by_cols),
        own_n,
        (*ups, ux_t, ux_b, uy_t, uy_b, ud_t, ud_b),
    )
    sums = down_call(hidden, (*downs, dx_t, dx_b, dy_t, dy_b))
    predicted = combine(pred_rows, expert_ids, combine_weights, back)
    sums = after(sums, predicted)
    rows = target_in.shape[0]
    other_sum = last_call(hidden, dd_t, dd_b, sums, 0, None, BF)
    received = lax.ppermute(other_sum, "expert", pc)
    own_sum = last_call(hidden, dd_t, dd_b, sums, rows, target_in, F32)
    return (own_sum + received.astype(F32)).astype(BF), predicted


def slots_of(expert_ids, rows, n_all):
    chosen = expert_ids.T
    each = jnp.arange(n_all, dtype=jnp.int32)[:, None]
    named_k = [chosen[k][None, :] == each for k in range(TOP)]
    named = named_k[0]
    for more in named_k[1:]:
        named = named | more
    before = jnp.arange(rows)[:, None] < jnp.arange(rows)[None, :]
    slot = dot(named.astype(BF), before.astype(BF)).astype(jnp.int32)
    return named_k, jnp.where(named, slot, -1)


def dispatch_rows(pred_rows, expert_ids):
    owners = lax.axis_size("expert")
    rows, width = pred_rows.shape
    group = lax.axis_index("dp") % EXP_DEV
    _, slot = slots_of(expert_ids - group * owners, rows, owners)
    pick = slot[:, None, :] == jnp.arange(CAP, dtype=jnp.int32)[None, :, None]
    pick = pick.reshape(owners * CAP, rows).astype(BF)
    return dot(pick, pred_rows).astype(BF).reshape(owners, CAP, width)


def expert_kernel(x_ref, g_ref, u_ref, d_ref, out_ref, total):
    step = pl.program_id(0)
    contract = (((1,), (1,)), ((), ()))
    x = x_ref[...]
    gate = lax.dot_general(x, g_ref[0], contract, preferred_element_type=F32)
    up = lax.dot_general(x, u_ref[0], contract, preferred_element_type=F32)
    act = (gate / (1.0 + jnp.exp(-gate)) * up).astype(BF)
    part = dot(act, d_ref[0])

    @pl.when(step == 0)
    def _():
        total[...] = part

    @pl.when(step > 0)
    def _():
        total[...] += part

    @pl.when(step == pl.num_programs(0) - 1)
    def _():
        if len(out_ref.shape) == 2:
            out_ref[...] = total[...].astype(BF)
        else:
            share = out_ref.shape[2]
            for d in range(out_ref.shape[0]):
                out_ref[d] = total[:, d * share : (d + 1) * share].astype(BF)


def expert_call(dispatched, gate_experts, up_experts, down_experts):
    owners, cap, width = dispatched.shape
    n_dp = lax.axis_size("dp")
    share = width // n_dp
    rows = owners * cap
    hidden = gate_experts.shape[1]
    tile = 704 if hidden % 704 == 0 else hidden
    whole = share % 128 == 0
    shape = (n_dp, rows, share) if whole else (rows, width)
    weights = pl.BlockSpec((1, tile, width), lambda i: (0, i, 0))
    out = pl.pallas_call(
        expert_kernel,
        out_shape=jax.ShapeDtypeStruct(shape, BF),
        grid=(hidden // tile,),
        in_specs=[pl.BlockSpec((rows, width), lambda i: (0, 0))] + [weights] * 3,
        out_specs=pl.BlockSpec(shape, lambda i: (0,) * len(shape)),
        scratch_shapes=[pltpu.VMEM((rows, width), F32)],
        compiler_params=pltpu.CompilerParams(vmem_limit_bytes=24 * 2**20),
        cost_estimate=pl.CostEstimate(
            flops=6 * rows * hidden * width,
            bytes_accessed=6 * hidden * width + 4 * rows * width,
            transcendentals=0,
        ),
        name="expert",
    )(
        dispatched.reshape(rows, width),
        *[
            pltpu.with_memory_space_constraint(w, pltpu.HBM)
            for w in (gate_experts, up_experts, down_experts)
        ],
    )
    if not whole:
        out = out.reshape(rows, n_dp, share).transpose(1, 0, 2)
    return out.reshape(n_dp * owners, cap, share)


def combine(pred_rows, expert_ids, combine_weights, back):
    owners = lax.axis_size("expert")
    n_dp = lax.axis_size("dp")
    rows, width = pred_rows.shape
    n_all = EXP_DEV * owners
    share = width // n_dp
    named_k, slot = slots_of(expert_ids, rows, n_all)
    spread = slot[:, None, :] == jnp.arange(CAP, dtype=jnp.int32)[None, :, None]
    weight = sum(
        jnp.where(named_k[k], combine_weights[:, k][None, :], 0.0) for k in range(TOP)
    )
    mix = jnp.where(spread, weight[:, None, :], 0.0).reshape(n_all * CAP, rows)
    over = (((0,), (0,)), ((), ()))
    high = mix.astype(BF)
    low = (mix - high.astype(F32)).astype(BF)
    mixed_out = 0.0
    back = back.reshape(n_dp // EXP_DEV, n_all * CAP, share)
    for q in range(n_dp // EXP_DEV):
        for part in (high, low):
            mixed_out = mixed_out + lax.dot_general(
                part, back[q], over, preferred_element_type=F32
            )
    residual = lax.dynamic_slice_in_dim(
        pred_rows, lax.axis_index("dp") * share, share, 1
    ).astype(F32)
    return (residual + mixed_out).astype(BF)


def program_any(
    target_in,
    ln_gain,
    up_target,
    down_target,
    pred_rows,
    expert_ids,
    combine_weights,
    gate_experts,
    up_experts,
    down_experts,
):
    dispatched = lax.all_to_all(
        dispatch_rows(pred_rows, expert_ids), "expert", 0, 0, tiled=True
    )
    by_cols = expert_call(dispatched, gate_experts, up_experts, down_experts)
    back = lax.all_to_all(by_cols, ("dp", "expert"), 0, 0, tiled=True)
    predicted = combine(pred_rows, expert_ids, combine_weights, back)
    target_out = target_gathered(target_in, ln_gain, up_target, down_target)
    return target_out, predicted


def solution(mesh):
    square = mesh.shape["dp"] == 4 and mesh.shape["expert"] % 2 == 0
    on_device = program_square if square else program_any

    in_specs = (
        P(("dp", "expert"), None),
        P(),
        P("dp", None),
        P("dp", None),
        P("expert", None),
        P("expert", None),
        P("expert", None),
        P(("dp", "expert"), None, None),
        P(("dp", "expert"), None, None),
        P(("dp", "expert"), None, None),
    )
    out_specs = (P(("dp", "expert"), None), P("expert", "dp"))
    return jax.shard_map(
        on_device, mesh=mesh, in_specs=in_specs, out_specs=out_specs, check_vma=False
    )
```

time: 347 us -> 105 us (0.30)
  waiting for transfers between devices: 237 us -> 13 us
  Pallas kernels: 0 us -> 33.3 us
  matrix products: 29 us -> 7.1 us
  blocking collectives: 21.7 us -> 0 us
  starting transfers between devices: 3.9 us -> 25.4 us
  local copies, waits for them, and re-layouts: 31.6 us -> 13.3 us
  between operations: 14 us -> 0.85 us
    all_gather x2 -> x0, waiting for transfers between devices: 182 us -> none  [the longest x1 91.7 us: on_device(): lax.all_gather(up_target, 'dp', axis=0, tiled=True)]
    pallas_call x0 -> x6, Pallas kernels: none -> 33.3 us  [the longest x1 11.1 us: up_call(): pl.pallas_call(up_kernel, out_shape=jax.ShapeDtypeStruct((2 * rows, width...]
    reduce_scatter x1 -> x0, waiting for transfers between devices: 27.5 us -> none  [on_device(): lax.psum_scatter(mixed_part, 'dp', scatter_dimension=1, tiled=True)]
    all_to_all x1 -> x2, waiting for transfers between devices: 26.3 us -> 0.01 us  [the longest x1 0.01 us: program_square(): back = lax.all_to_all(by_cols, ('dp', 'expert'), 0, 0, tiled=True)]
    scatter x1 -> x0, local copies, waits for them, and re-layouts: 22.5 us -> none  [on_device(): outgoing = outgoing.at[send_pos].set(pred_rows[row_index], mode='drop')]
    dot_general x4 -> x5, matrix products: 29 us -> 7.1 us  [the longest x2 4.4 us: combine(): lax.dot_general(part, back[q], over, preferred_element_type=F32)]
    all_to_all x1 -> x0, blocking collectives: 21.7 us -> none  [on_device(): lax.all_to_all(outgoing.reshape(owner_count, CAP, model_width), 'expert',...]
    ppermute x0 -> x14, starting transfers between devices: none -> 13.9 us  [the longest x8 11.5 us: both(): return [lax.ppermute(parts[h], 'dp', p) for p in (px, py) for h in range(2)]]
  transfers between devices with their start and end apart: 4 -> 16, of which waited for: 4 -> 5; matrix products, arithmetic and copies ran while one was open for 1% -> 18% of each run, Pallas kernels for 0% -> 29%
where the time goes in v2:
time: 105 us; the launch traced here: 104 us
  Pallas kernels  33.3 us (32%)
  starting transfers between devices  25.4 us (24%)
  local copies, waits for them, and re-layouts  13.3 us (13%)
  waiting for transfers between devices  13 us (12%)
  other arithmetic  10.9 us (10%)
  matrix products  7.1 us (7%)
    ppermute x8, starting transfers between devices, both(): return [lax.ppermute(parts[h], 'dp', p) for p in (px, py) for h in range(2)]  11.5 us
    pallas_call x1, Pallas kernels, up_call(): pl.pallas_call(up_kernel, out_shape=jax.ShapeDtypeStruct((2 * rows, width...  11.1 us
    unnamed x26, local copies, waits for them, and re-layouts  11 us
    ppermute x8, waiting for transfers between devices, both(): return [lax.ppermute(parts[h], 'dp', p) for p in (px, py) for h in range(2)]  10.7 us
    pallas_call x1, Pallas kernels, expert_call(): pl.pallas_call(expert_kernel, out_shape=jax.ShapeDtypeStruct(shape, BF),...  10.1 us
    pallas_call x1, Pallas kernels, down_call(): pl.pallas_call(down_kernel, out_shape=jax.ShapeDtypeStruct((rows, wide),...  7.12 us
    all_to_all x1, starting transfers between devices, program_square(): back = lax.all_to_all(by_cols, ('dp', 'expert'), 0, 0, tiled=True)  6.2 us
    all_to_all x1, starting transfers between devices, program_square(): lax.all_to_all(dispatch_rows(pred_rows, expert_ids), 'expert', 0, 0, tile...  5.32 us
  transfers between devices with their start and end apart: 16, of which 5 were waited for; matrix products, arithmetic and copies ran while one was open for 18% of the time, Pallas kernels for 29%

profile of v2, /device:TPU:0, one launch (start us, length us, event | category | flops | bytes accessed | tf_op | source)
XLA Modules:
  0.0 103.9 jit_solution(15911776437832056843)
XLA Ops:
  0.7 0.1 pad_add_fusion.at_ref
  0.7 1.7 %copy-done.5 = bf16[352,3072]{1,0:T(8,128)(2,1)S(1)} copy-done((bf16[352,3072]{1,0:T(8,128)(2,1)S(1)}, bf16[352,3072]{1,0:T(8,128)(2,1)}, u32[]{:S(2)}) %copy-start.5) | copy-done | bytes 2162712
  2.5 2.2 %cut_up.1 = (bf16[176,1536]{1,0:T(8,128)(2,1)S(1)}, bf16[176,1536]{1,0:T(8,128)(2,1)}) custom-call(s32[2]{0:T(128)S(1)} %pad_add_fusion.at_ref, bf16[352,3072]{1,0:T(8,128)(2,1)S(1)} %copy-done.5), custom_call_target="tpu_custom_call" | custom-call | bytes 2162688 | tf_op jit(solution)/shard_map/cut_up/pallas_call | solution.py:65
  4.6 3.0 %collective-permute-start.4 = (bf16[176,1536]{1,0:T(8,128)(2,1)}, bf16[176,1536]{1,0:T(8,128)(2,1)}, u32[]{:S(2)}, u32[]{:S(2)}) collective-permute-start(bf16[176,1536]{1,0:T(8,128)(2,1)} %get-tuple-element.9.refs_1_), channel_id=1, source_target_pairs={{0,16},{8,24},{16,0},{24,8},{1,17},{9,25},{17,1},{25,9},{2,18},{10... | collective-permute-start | bytes 1622024 | tf_op jit(solution)/shard_map/ppermute | solution.py:254
  7.6 1.5 %collective-permute-start.1 = (bf16[176,1536]{1,0:T(8,128)(2,1)}, bf16[176,1536]{1,0:T(8,128)(2,1)}, u32[]{:S(2)}, u32[]{:S(2)}) collective-permute-start(bf16[176,1536]{1,0:T(8,128)(2,1)} %get-tuple-element.9.refs_1_), channel_id=1, source_target_pairs={{0,8},{8,0},{16,24},{24,16},{1,9},{9,1},{17,25},{25,17},{2,10},{10... | collective-permute-start | bytes 1622024 | tf_op jit(solution)/shard_map/ppermute | solution.py:254
  9.1 0.5 collective-permute-start.3
  9.7 0.7 subtract_bitcast_fusion
  10.4 0.1 eq.118
  10.5 0.1 fusion.15
  10.6 0.2 bitcast_compare_fusion
  10.8 2.4 %convolution_convert_fusion = bf16[256,1024]{1,0:T(8,128)(2,1)} fusion(pred[256,384]{1,0:T(32,128)(4,1)S(1)} %bitcast_compare_fusion, bf16[384,1024]{1,0:T(8,128)(2,1)} %param.14), kind=kOutput, calls=%fused_computation.19 | convolution fusion | flops 201588736 | bytes 1409024 | tf_op jit(solution)/shard_map/dot_general | solution.py:28
  13.2 5.3 %all-to-all-start = ((bf16[8,32,1024]{2,1,0:T(8,128)(2,1)}), bf16[8,32,1024]{2,1,0:T(8,128)(2,1)S(1)}, u32[]{:S(2)}, u32[]{:S(2)}) async-start(bf16[8,32,1024]{2,1,0:T(8,128)(2,1)} %bitcast.4), calls=%async_computation | async-start | bytes 1048576 | tf_op jit(solution)/shard_map/all_to_all | solution.py:258
  18.5 0.5 collective-permute-start
  19.0 0.3 convert_reduce_fusion
  19.3 0.6 fusion.4
  20.0 0.2 fusion.14
  20.2 2.1 %constant_dynamic-slice_fusion = (bf16[192,1408]{1,0:T(8,128)(2,1)S(1)}, bf16[192,1408]{1,0:T(8,128)(2,1)}) fusion(bf16[768,1408]{1,0:T(8,128)(2,1)} %param.13, s32[]{:T(128)S(6)} %select_n.54, s32[]{:T(128)S(6)} %select_n.53), kind=kLoop, calls=%fused_computation.59 | loop fusion | bytes 2162696 | tf_op jit(solution)/shard_map/dynamic_slice | solution.py:265
  22.3 0.8 collective-permute-done.1.refs_3_
  23.1 8.7 %collective-permute-done.2.refs_4_ = bf16[176,1536]{1,0:T(8,128)(2,1)} collective-permute-done((bf16[176,1536]{1,0:T(8,128)(2,1)S(1)}, bf16[176,1536]{1,0:T(8,128)(2,1)}, u32[]{:S(2)}, u32[]{:S(2)}) %collective-permute-start.2) | collective-permute-done | bytes 540704 | tf_op jit(solution)/shard_map/ppermute | solution.py:254
  31.8 1.7 %collective-permute-start.7 = (bf16[192,1408]{1,0:T(8,128)(2,1)}, bf16[192,1408]{1,0:T(8,128)(2,1)}, u32[]{:S(2)}, u32[]{:S(2)}) collective-permute-start(bf16[192,1408]{1,0:T(8,128)(2,1)} %get-tuple-element.13.refs_0_), channel_id=1, source_target_pairs={{0,16},{8,24},{16,0},{24,8},{1,17},{9,25},{17,1},{25,9},{2,18},{10... | collective-permute-start | bytes 1622024 | tf_op jit(solution)/shard_map/ppermute | solution.py:254
  33.5 1.5 %collective-permute-start.9 = (bf16[192,1408]{1,0:T(8,128)(2,1)S(1)}, bf16[192,1408]{1,0:T(8,128)(2,1)}, u32[]{:S(2)}, u32[]{:S(2)}) collective-permute-start(bf16[192,1408]{1,0:T(8,128)(2,1)S(1)} %get-tuple-element.14.refs_1_), channel_id=1, source_target_pairs={{0,8},{8,0},{16,24},{24,16},{1,9},{9,1},{17,25},{25,17},{2,10},{10... | collective-permute-start | bytes 1622024 | tf_op jit(solution)/shard_map/ppermute | solution.py:254
  35.0 0.5 collective-permute-start.6
  35.5 1.8 %convert_reduce_fusion.1 = f32[640]{0:T(1024)S(1)} fusion(bf16[640,1408]{1,0:T(8,128)(2,1)} %collective-permute-done), kind=kLoop, calls=%fused_computation.3 | loop fusion | flops 1801600 | bytes 1804800 | tf_op jit(solution)/shard_map/reduce_sum | solution.py:21
  37.3 2.1 %fusion.7 = f32[640]{0:T(1024)S(1)} fusion(bf16[640,1408]{1,0:T(8,128)(2,1)} %collective-permute-done, f32[640]{0:T(1024)S(1)} %broadcast_multiply_fusion.1), kind=kLoop, calls=%fused_computation.11 | loop fusion | flops 3603840 | bytes 1807360 | tf_op jit(solution)/shard_map/reduce_sum | solution.py:23
  39.4 0.4 collective-permute-start.5
  39.8 3.6 %fusion.6 = (bf16[640,1408]{1,0:T(8,128)(2,1)}, bf16[640,1408]{1,0:T(8,128)(2,1)}) fusion(bf16[640,1408]{1,0:T(8,128)(2,1)S(1)} %copy-done, f32[640]{0:T(1024)S(1)} %add_rsqrt_fusion, f32[640]{0:T(1024)S(1)} %broadcast_multiply_fusion, f32[1408]{0:T(1024)S(1)} %copy-done.11, f32[640]{0:T(1024)S(1)} %add_rsqrt_fusion.1, f32[640]{0:T(1024)S(1)} %broadcast_multiply_fusion.1, ...), kind=kLoop, calls=%fused_computation.10 | loop fusion | flops 9011200 | bytes 7224832 | tf_op jit(solution)/shard_map/convert_element_type | solution.py:24
  43.4 10.1 %expert.1 = bf16[4,256,256]{2,1,0:T(8,128)(2,1)} custom-call(bf16[256,1024]{1,0:T(8,128)(2,1)S(1)} %bitcast.24, bf16[1,2816,1024]{2,1,0:T(8,128)(2,1)} %g_ref.1, bf16[1,2816,1024]{2,1,0:T(8,128)(2,1)} %u_ref.1, bf16[1,2816,1024]{2,1,0:T(8,128)(2,1)} %d_ref.1), custom_call_target="tpu_custom_call" | custom-call | flops 4429185024 | bytes 18350080 | tf_op jit(solution)/shard_map/expert/pallas_call | solution.py:349
  53.5 6.2 %all-to-all-start.1 = ((bf16[32,32,256]{2,1,0:T(8,128)(2,1)}), bf16[32,32,256]{2,1,0:T(8,128)(2,1)}, u32[]{:S(2)}, u32[]{:S(2)}) async-start(bf16[32,32,256]{2,1,0:T(8,128)(2,1)} %bitcast.6), calls=%async_computation.1 | async-start | bytes 1048576 | tf_op jit(solution)/shard_map/all_to_all | solution.py:273
  59.7 1.8 %collective-permute-start.11 = (bf16[192,1408]{1,0:T(8,128)(2,1)}, bf16[192,1408]{1,0:T(8,128)(2,1)S(1)}, u32[]{:S(2)}, u32[]{:S(2)}) collective-permute-start(bf16[192,1408]{1,0:T(8,128)(2,1)} %get-tuple-element.13.refs_0_), channel_id=1, source_target_pairs={{0,8},{8,0},{16,24},{24,16},{1,9},{9,1},{17,25},{25,17},{2,10},{10... | collective-permute-start | bytes 1622024 | tf_op jit(solution)/shard_map/ppermute | solution.py:254
  61.5 1.5 %collective-permute-start.12 = (bf16[192,1408]{1,0:T(8,128)(2,1)S(1)}, bf16[192,1408]{1,0:T(8,128)(2,1)S(1)}, u32[]{:S(2)}, u32[]{:S(2)}) collective-permute-start(bf16[192,1408]{1,0:T(8,128)(2,1)S(1)} %get-tuple-element.14.refs_1_), channel_id=1, source_target_pairs={{0,16},{8,24},{16,0},{24,8},{1,17},{9,25},{17,1},{25,9},{2,18},{10... | collective-permute-start | bytes 1622024 | tf_op jit(solution)/shard_map/ppermute | solution.py:254
  63.0 0.6 collective-permute-start.8
  63.5 0.3 collective-permute-start.10
  63.9 1.5 %copy-done.6 = bf16[640,1408]{1,0:T(8,128)(2,1)S(1)} copy-done((bf16[640,1408]{1,0:T(8,128)(2,1)S(1)}, bf16[640,1408]{1,0:T(8,128)(2,1)}, u32[]{:S(2)}) %copy-start.6) | copy-done | bytes 1802264
  65.3 1.5 %copy-done.7 = bf16[640,1408]{1,0:T(8,128)(2,1)S(1)} copy-done((bf16[640,1408]{1,0:T(8,128)(2,1)S(1)}, bf16[640,1408]{1,0:T(8,128)(2,1)}, u32[]{:S(2)}) %copy-start.7) | copy-done | bytes 1802264
  66.8 1.0 %copy-done.9 = bf16[176,1536]{1,0:T(8,128)(2,1)S(1)} copy-done((bf16[176,1536]{1,0:T(8,128)(2,1)S(1)}, bf16[176,1536]{1,0:T(8,128)(2,1)}, u32[]{:S(2)}) %copy-start.9) | copy-done | bytes 540696
  67.9 11.1 %up.1.h_ref = bf16[1280,1536]{1,0:T(8,128)(2,1)S(1)} custom-call(s32[2]{0:T(128)S(1)} %pad_add_fusion.at_ref, bf16[640,1408]{1,0:T(8,128)(2,1)S(1)} %copy-done.7, bf16[640,1408]{1,0:T(8,128)(2,1)S(1)} %copy-done.6, bf16[176,1536]{1,0:T(8,128)(2,1)S(1)} %copy-done.9, bf16[176,1536]{1,0:T(8,128)(2,1)} %get-tuple-element.9.refs_1_, ...), custom_call_target="tpu_custom_call" | custom-call | flops 11072962560 | bytes 12000000 | tf_op jit(solution)/shard_map/up/pallas_call | solution.py:133
  79.0 1.1 %collective-permute-done.11.refs_2_ = bf16[192,1408]{1,0:T(8,128)(2,1)S(1)} collective-permute-done((bf16[192,1408]{1,0:T(8,128)(2,1)}, bf16[192,1408]{1,0:T(8,128)(2,1)S(1)}, u32[]{:S(2)}, u32[]{:S(2)}) %collective-permute-start.11) | collective-permute-done | bytes 540704 | tf_op jit(solution)/shard_map/ppermute | solution.py:254
  80.1 0.2 collective-permute-done.12.refs_5_
  80.3 7.1 %down.1.sum_ref = f32[1280,1408]{1,0:T(8,128)S(1)} custom-call(bf16[1280,1536]{1,0:T(8,128)(2,1)S(1)} %up.1.h_ref, bf16[192,1408]{1,0:T(8,128)(2,1)} %get-tuple-element.13.refs_0_, bf16[192,1408]{1,0:T(8,128)(2,1)S(1)} %get-tuple-element.14.refs_1_, bf16[192,1408]{1,0:T(8,128)(2,1)S(1)} %collective-permute-done.11.refs_2_, ...), custom_call_target="tpu_custom_call" | custom-call | flops 5536481280 | bytes 15000000 | tf_op jit(solution)/shard_map/down/pallas_call | solution.py:175
  87.4 2.9 %copy-done.1 = f32[1280,1408]{1,0:T(8,128)} copy-done((f32[1280,1408]{1,0:T(8,128)}, f32[1280,1408]{1,0:T(8,128)S(1)}, u32[]{:S(2)}) %copy-start.1) | copy-done | bytes 7208984
  90.4 2.0 %copy-done.3 = bf16[1280,1536]{1,0:T(8,128)(2,1)} copy-done((bf16[1280,1536]{1,0:T(8,128)(2,1)}, bf16[1280,1536]{1,0:T(8,128)(2,1)S(1)}, u32[]{:S(2)}) %copy-start.3) | copy-done | bytes 3932184
  92.3 1.6 %convolution_bitcast_fusion = f32[384,256]{1,0:T(8,128)S(1)} fusion(bf16[32,32,256]{2,1,0:T(8,128)(2,1)} %all-to-all-done.1, f32[32,384]{1,0:T(8,128)S(1)} %select_add_fusion, s32[32,384]{1,0:T(8,128)S(1)} %fusion.14), kind=kOutput, calls=%fused_computation.20 | convolution fusion | flops 203685888 | bytes 1015808 | tf_op jit(solution)/shard_map/dot_general | solution.py:394
  94.0 2.8 %fusion.13 = bf16[384,256]{1,0:T(8,128)(2,1)} fusion(f32[384,256]{1,0:T(8,128)S(1)} %convolution_bitcast_fusion, bf16[32,32,256]{2,1,0:T(8,128)(2,1)} %all-to-all-done.1, f32[32,384]{1,0:T(8,128)S(1)} %select_add_fusion, s32[32,384]{1,0:T(8,128)S(1)} %fusion.14, bf16[384,1024]{1,0:T(8,128)(2,1)} %param.14, s32[]{:T(128)S(6)} %select_n.55), kind=kOutput, calls=%fused_computation.24 | convolution fusion | flops 202506240 | bytes 1409028 | tf_op jit(solution)/shard_map/dot_general | solution.py:394
  96.8 0.4 copy-done.4
  97.1 1.4 %last.3 = bf16[640,1408]{1,0:T(8,128)(2,1)S(1)} custom-call(bf16[1280,1536]{1,0:T(8,128)(2,1)S(1)} %copy-done.4, bf16[192,1408]{1,0:T(8,128)(2,1)S(1)} %collective-permute-done.8.da, bf16[192,1408]{1,0:T(8,128)(2,1)S(1)} %collective-permute-done.10.db, f32[1280,1408]{1,0:T(8,128)S(1)} %copy-done.2), custom_call_target="tpu_custom_call" | custom-call | flops 1038090240 | bytes 6000000 | tf_op jit(solution)/shard_map/last/pallas_call | solution.py:210
  98.6 1.4 %last.2 = f32[640,1408]{1,0:T(8,128)S(1)} custom-call(bf16[1280,1536]{1,0:T(8,128)(2,1)S(1)} %copy-done.4, bf16[192,1408]{1,0:T(8,128)(2,1)S(1)} %collective-permute-done.8.da, bf16[192,1408]{1,0:T(8,128)(2,1)S(1)} %collective-permute-done.10.db, f32[1280,1408]{1,0:T(8,128)S(1)} %copy-done.2, bf16[640,1408]{1,0:T(8,128)(2,1)S(1)} %copy-done), custom_call_target="tpu_custom_call" | custom-call | flops 1038090240 | bytes 6000000 | tf_op jit(solution)/shard_map/last/pallas_call | solution.py:210
  100.1 2.3 %collective-permute-done.13 = bf16[640,1408]{1,0:T(8,128)(2,1)S(1)} collective-permute-done((bf16[640,1408]{1,0:T(8,128)(2,1)S(1)}, bf16[640,1408]{1,0:T(8,128)(2,1)S(1)}, u32[]{:S(2)}, u32[]{:S(2)}) %collective-permute-start.13) | collective-permute-done | bytes 1802272 | tf_op jit(solution)/shard_map/ppermute | solution.py:285
  102.4 1.5 %add_convert_fusion = bf16[640,1408]{1,0:T(8,128)(2,1)} fusion(f32[640,1408]{1,0:T(8,128)S(1)} %last.2, bf16[640,1408]{1,0:T(8,128)(2,1)S(1)} %collective-permute-done.13), kind=kLoop, calls=%fused_computation.14 | loop fusion | flops 2703360 | bytes 7208960 | tf_op jit(solution)/shard_map/convert_element_type | solution.py:287
  (41 shorter events, 0.3 us)
Async XLA Ops:
  0.6 17.9 %copy-start = (bf16[640,1408]{1,0:T(8,128)(2,1)S(1)}, bf16[640,1408]{1,0:T(8,128)(2,1)}, u32[]{:S(2)}) copy-start(bf16[640,1408]{1,0:T(8,128)(2,1)} %refs_0_.1) | copy-start | bytes 5406724
  0.7 1.7 %copy-start.5 = (bf16[352,3072]{1,0:T(8,128)(2,1)S(1)}, bf16[352,3072]{1,0:T(8,128)(2,1)}, u32[]{:S(2)}) copy-start(bf16[352,3072]{1,0:T(8,128)(2,1)} %up_ref.1) | copy-start | bytes 6488068
  2.5 16.5 %copy-start.10 = (s32[384,2]{0,1:T(2,128)S(1)}, s32[384,2]{0,1:T(2,128)}, u32[]{:S(2)}) copy-start(s32[384,2]{0,1:T(2,128)} %param.15) | copy-start | bytes 9220
  4.6 17.7 %copy-start.8 = (bf16[176,1536]{1,0:T(8,128)(2,1)}, bf16[176,1536]{1,0:T(8,128)(2,1)S(1)}, u32[]{:S(2)}) copy-start(bf16[176,1536]{1,0:T(8,128)(2,1)S(1)} %get-tuple-element.10.refs_0_) | copy-start | bytes 1622020
  4.6 15.5 %copy-start.12 = (f32[384,2]{0,1:T(2,128)S(1)}, f32[384,2]{0,1:T(2,128)}, u32[]{:S(2)}) copy-start(f32[384,2]{0,1:T(2,128)} %param.16) | copy-start | bytes 9220
  4.6 34.8 %collective-permute-start.4 = (bf16[176,1536]{1,0:T(8,128)(2,1)}, bf16[176,1536]{1,0:T(8,128)(2,1)}, u32[]{:S(2)}, u32[]{:S(2)}) collective-permute-start(bf16[176,1536]{1,0:T(8,128)(2,1)} %get-tuple-element.9.refs_1_), channel_id=1, source_target_pairs={{0,16},{8,24},{16,0},{24,8},{1,17},{9,25},{17,1},{25,9},{2,18},{10... | collective-permute-start | bytes 1622024 | tf_op jit(solution)/shard_map/ppermute | solution.py:254
  7.6 15.5 %collective-permute-start.1 = (bf16[176,1536]{1,0:T(8,128)(2,1)}, bf16[176,1536]{1,0:T(8,128)(2,1)}, u32[]{:S(2)}, u32[]{:S(2)}) collective-permute-start(bf16[176,1536]{1,0:T(8,128)(2,1)} %get-tuple-element.9.refs_1_), channel_id=1, source_target_pairs={{0,8},{8,0},{16,24},{24,16},{1,9},{9,1},{17,25},{25,17},{2,10},{10... | collective-permute-start | bytes 1622024 | tf_op jit(solution)/shard_map/ppermute | solution.py:254
  9.1 50.6 %collective-permute-start.3 = (bf16[176,1536]{1,0:T(8,128)(2,1)S(1)}, bf16[176,1536]{1,0:T(8,128)(2,1)}, u32[]{:S(2)}, u32[]{:S(2)}) collective-permute-start(bf16[176,1536]{1,0:T(8,128)(2,1)S(1)} %get-tuple-element.10.refs_0_), channel_id=1, source_target_pairs={{0,8},{8,0},{16,24},{24,16},{1,9},{9,1},{17,25},{25,17},{2,10},{10... | collective-permute-start | bytes 1622024 | tf_op jit(solution)/shard_map/ppermute | solution.py:254
  9.6 22.1 %collective-permute-start.2 = (bf16[176,1536]{1,0:T(8,128)(2,1)S(1)}, bf16[176,1536]{1,0:T(8,128)(2,1)}, u32[]{:S(2)}, u32[]{:S(2)}) collective-permute-start(bf16[176,1536]{1,0:T(8,128)(2,1)S(1)} %get-tuple-element.10.refs_0_), channel_id=1, source_target_pairs={{0,16},{8,24},{16,0},{24,8},{1,17},{9,25},{17,1},{25,9},{2,18},{10... | collective-permute-start | bytes 1622024 | tf_op jit(solution)/shard_map/ppermute | solution.py:254
  13.2 30.3 %all-to-all-start = ((bf16[8,32,1024]{2,1,0:T(8,128)(2,1)}), bf16[8,32,1024]{2,1,0:T(8,128)(2,1)S(1)}, u32[]{:S(2)}, u32[]{:S(2)}) async-start(bf16[8,32,1024]{2,1,0:T(8,128)(2,1)} %bitcast.4), calls=%async_computation | async-start | bytes 1048576 | tf_op jit(solution)/shard_map/all_to_all | solution.py:258
  18.5 16.5 %collective-permute-start = (bf16[640,1408]{1,0:T(8,128)(2,1)S(1)}, bf16[640,1408]{1,0:T(8,128)(2,1)}, u32[]{:S(2)}, u32[]{:S(2)}) collective-permute-start(bf16[640,1408]{1,0:T(8,128)(2,1)S(1)} %copy-done), channel_id=1, source_target_pairs={{0,1},{1,0},{2,3},{3,2},{4,5},{5,4},{6,7},{7,6},{8,9},{9,8},{10,11... | collective-permute-start | bytes 5406728 | tf_op jit(solution)/shard_map/ppermute | solution.py:261
  19.3 20.5 %copy-start.11 = (f32[1408]{0:T(1024)S(1)}, f32[1408]{0:T(1024)}, u32[]{:S(2)}) copy-start(f32[1408]{0:T(1024)} %param.11) | copy-start | bytes 16900
  31.8 31.2 %collective-permute-start.7 = (bf16[192,1408]{1,0:T(8,128)(2,1)}, bf16[192,1408]{1,0:T(8,128)(2,1)}, u32[]{:S(2)}, u32[]{:S(2)}) collective-permute-start(bf16[192,1408]{1,0:T(8,128)(2,1)} %get-tuple-element.13.refs_0_), channel_id=1, source_target_pairs={{0,16},{8,24},{16,0},{24,8},{1,17},{9,25},{17,1},{25,9},{2,18},{10... | collective-permute-start | bytes 1622024 | tf_op jit(solution)/shard_map/ppermute | solution.py:254
  33.5 30.0 %collective-permute-start.9 = (bf16[192,1408]{1,0:T(8,128)(2,1)S(1)}, bf16[192,1408]{1,0:T(8,128)(2,1)}, u32[]{:S(2)}, u32[]{:S(2)}) collective-permute-start(bf16[192,1408]{1,0:T(8,128)(2,1)S(1)} %get-tuple-element.14.refs_1_), channel_id=1, source_target_pairs={{0,8},{8,0},{16,24},{24,16},{1,9},{9,1},{17,25},{25,17},{2,10},{10... | collective-permute-start | bytes 1622024 | tf_op jit(solution)/shard_map/ppermute | solution.py:254
  35.0 26.5 %collective-permute-start.6 = (bf16[176,1536]{1,0:T(8,128)(2,1)}, bf16[176,1536]{1,0:T(8,128)(2,1)}, u32[]{:S(2)}, u32[]{:S(2)}) collective-permute-start(bf16[176,1536]{1,0:T(8,128)(2,1)} %collective-permute-done.1.refs_3_), channel_id=1, source_target_pairs={{0,16},{8,24},{16,0},{24,8},{1,17},{9,25},{17,1},{25,9},{2,18},{10... | collective-permute-start | bytes 1622024 | tf_op jit(solution)/shard_map/ppermute | solution.py:262
  39.4 24.4 %collective-permute-start.5 = (bf16[176,1536]{1,0:T(8,128)(2,1)}, bf16[176,1536]{1,0:T(8,128)(2,1)}, u32[]{:S(2)}, u32[]{:S(2)}) collective-permute-start(bf16[176,1536]{1,0:T(8,128)(2,1)} %collective-permute-done.2.refs_4_), channel_id=1, source_target_pairs={{0,8},{8,0},{16,24},{24,16},{1,9},{9,1},{17,25},{25,17},{2,10},{10... | collective-permute-start | bytes 1622024 | tf_op jit(solution)/shard_map/ppermute | solution.py:262
  53.5 38.8 %all-to-all-start.1 = ((bf16[32,32,256]{2,1,0:T(8,128)(2,1)}), bf16[32,32,256]{2,1,0:T(8,128)(2,1)}, u32[]{:S(2)}, u32[]{:S(2)}) async-start(bf16[32,32,256]{2,1,0:T(8,128)(2,1)} %bitcast.6), calls=%async_computation.1 | async-start | bytes 1048576 | tf_op jit(solution)/shard_map/all_to_all | solution.py:273
  59.7 20.4 %collective-permute-start.11 = (bf16[192,1408]{1,0:T(8,128)(2,1)}, bf16[192,1408]{1,0:T(8,128)(2,1)S(1)}, u32[]{:S(2)}, u32[]{:S(2)}) collective-permute-start(bf16[192,1408]{1,0:T(8,128)(2,1)} %get-tuple-element.13.refs_0_), channel_id=1, source_target_pairs={{0,8},{8,0},{16,24},{24,16},{1,9},{9,1},{17,25},{25,17},{2,10},{10... | collective-permute-start | bytes 1622024 | tf_op jit(solution)/shard_map/ppermute | solution.py:254
  61.5 18.8 %collective-permute-start.12 = (bf16[192,1408]{1,0:T(8,128)(2,1)S(1)}, bf16[192,1408]{1,0:T(8,128)(2,1)S(1)}, u32[]{:S(2)}, u32[]{:S(2)}) collective-permute-start(bf16[192,1408]{1,0:T(8,128)(2,1)S(1)} %get-tuple-element.14.refs_1_), channel_id=1, source_target_pairs={{0,16},{8,24},{16,0},{24,8},{1,17},{9,25},{17,1},{25,9},{2,18},{10... | collective-permute-start | bytes 1622024 | tf_op jit(solution)/shard_map/ppermute | solution.py:254
  63.0 33.8 %collective-permute-start.8 = (bf16[192,1408]{1,0:T(8,128)(2,1)}, bf16[192,1408]{1,0:T(8,128)(2,1)S(1)}, u32[]{:S(2)}, u32[]{:S(2)}) collective-permute-start(bf16[192,1408]{1,0:T(8,128)(2,1)} %collective-permute-done.7.refs_4_), channel_id=1, source_target_pairs={{0,8},{8,0},{16,24},{24,16},{1,9},{9,1},{17,25},{25,17},{2,10},{10... | collective-permute-start | bytes 1622024 | tf_op jit(solution)/shard_map/ppermute | solution.py:269
  63.5 33.2 %collective-permute-start.10 = (bf16[192,1408]{1,0:T(8,128)(2,1)}, bf16[192,1408]{1,0:T(8,128)(2,1)S(1)}, u32[]{:S(2)}, u32[]{:S(2)}) collective-permute-start(bf16[192,1408]{1,0:T(8,128)(2,1)} %collective-permute-done.9.refs_3_), channel_id=1, source_target_pairs={{0,16},{8,24},{16,0},{24,8},{1,17},{9,25},{17,1},{25,9},{2,18},{10... | collective-permute-start | bytes 1622024 | tf_op jit(solution)/shard_map/ppermute | solution.py:269
  63.9 1.5 %copy-start.6 = (bf16[640,1408]{1,0:T(8,128)(2,1)S(1)}, bf16[640,1408]{1,0:T(8,128)(2,1)}, u32[]{:S(2)}) copy-start(bf16[640,1408]{1,0:T(8,128)(2,1)} %get-tuple-element.24.own_ref) | copy-start | bytes 5406724
  65.3 1.5 %copy-start.7 = (bf16[640,1408]{1,0:T(8,128)(2,1)S(1)}, bf16[640,1408]{1,0:T(8,128)(2,1)}, u32[]{:S(2)}) copy-start(bf16[640,1408]{1,0:T(8,128)(2,1)} %get-tuple-element.12.other_ref) | copy-start | bytes 5406724
  66.8 1.0 %copy-start.9 = (bf16[176,1536]{1,0:T(8,128)(2,1)S(1)}, bf16[176,1536]{1,0:T(8,128)(2,1)}, u32[]{:S(2)}) copy-start(bf16[176,1536]{1,0:T(8,128)(2,1)} %copy-done.8) | copy-start | bytes 1622020
  87.4 2.9 %copy-start.1 = (f32[1280,1408]{1,0:T(8,128)}, f32[1280,1408]{1,0:T(8,128)S(1)}, u32[]{:S(2)}) copy-start(f32[1280,1408]{1,0:T(8,128)S(1)} %down.1.sum_ref) | copy-start | bytes 21626884
  90.4 2.0 %copy-start.3 = (bf16[1280,1536]{1,0:T(8,128)(2,1)}, bf16[1280,1536]{1,0:T(8,128)(2,1)S(1)}, u32[]{:S(2)}) copy-start(bf16[1280,1536]{1,0:T(8,128)(2,1)S(1)} %up.1.h_ref) | copy-start | bytes 11796484
  92.3 4.4 %copy-start.2 = (f32[1280,1408]{1,0:T(8,128)S(1)}, f32[1280,1408]{1,0:T(8,128)}, u32[]{:S(2)}) copy-start(f32[1280,1408]{1,0:T(8,128)} %copy-done.1) | copy-start | bytes 21626884
  94.0 3.2 %copy-start.4 = (bf16[1280,1536]{1,0:T(8,128)(2,1)S(1)}, bf16[1280,1536]{1,0:T(8,128)(2,1)}, u32[]{:S(2)}) copy-start(bf16[1280,1536]{1,0:T(8,128)(2,1)} %copy-done.3) | copy-start | bytes 11796484
  98.6 3.8 %collective-permute-start.13 = (bf16[640,1408]{1,0:T(8,128)(2,1)S(1)}, bf16[640,1408]{1,0:T(8,128)(2,1)S(1)}, u32[]{:S(2)}, u32[]{:S(2)}) collective-permute-start(bf16[640,1408]{1,0:T(8,128)(2,1)S(1)} %last.3), channel_id=1, source_target_pairs={{0,1},{1,0},{2,3},{3,2},{4,5},{5,4},{6,7},{7,6},{8,9},{9,8},{10,11... | collective-permute-start | bytes 5406728 | tf_op jit(solution)/shard_map/ppermute | solution.py:285

commit v3 on v2

--- a/solution.py
+++ b/solution.py
@@ -43,114 +43,203 @@
     return (target_in.astype(F32) + projected).astype(BF)
 
 
-def after(value, *others):
-    return lax.optimization_barrier((value, others))[0]
+ANYWHERE = pl.BlockSpec(memory_space=pl.ANY)
+
+
+def in_hbm(*arrays):
+    return [pltpu.with_memory_space_constraint(a, pltpu.HBM) for a in arrays]
+
+
+def halves_kernel(waited_ref, first_ref, second_ref, top_ref, low_ref):
+    top_ref[...] = first_ref[...]
+    low_ref[...] = second_ref[...]
+
+
+def halves(waited, first, second):
+    rows, width = first.shape
+    part = jax.ShapeDtypeStruct((rows // 2, width), first.dtype)
+    tile = width // 2 if width % 256 == 0 else width
+    out = pl.BlockSpec((rows // 2, tile), lambda i: (0, i))
+    return pl.pallas_call(
+        halves_kernel,
+        out_shape=(part, part),
+        grid=(width // tile,),
+        in_specs=[
+            ANYWHERE,
+            pl.BlockSpec((rows // 2, tile), lambda i: (0, i)),
+            pl.BlockSpec((rows // 2, tile), lambda i: (1, i)),
+        ],
+        out_specs=(out, out),
+        compiler_params=pltpu.CompilerParams(vmem_limit_bytes=8 * 2**20),
+        cost_estimate=pl.CostEstimate(flops=1, bytes_accessed=1, transcendentals=0),
+        name="halves",
+    )(*in_hbm(waited), first, second)
+
+
+def hold_kernel(*refs):
+    pass
+
+
+def hold(waited, *arrays):
+    n = len(arrays)
+    return pl.pallas_call(
+        hold_kernel,
+        out_shape=[jax.ShapeDtypeStruct(a.shape, a.dtype) for a in arrays],
+        in_specs=[ANYWHERE] * (n + 1),
+        out_specs=[ANYWHERE] * n,
+        input_output_aliases={i + 1: i for i in range(n)},
+        compiler_params=pltpu.CompilerParams(vmem_limit_bytes=2**20),
+        cost_estimate=pl.CostEstimate(flops=1, bytes_accessed=1, transcendentals=0),
+        name="hold",
+    )(*in_hbm(waited), *arrays)
 
 
 def gelu(v):
     return 0.5 * v * (1.0 + jnp.tanh(0.7978845608028654 * (v + 0.044715 * (v * v * v))))
 
 
-def cut_up_kernel(at_ref, up_ref, top_ref, low_ref):
-    rows = top_ref.shape[0]
-    top_ref[...] = up_ref[:rows, :]
-    low_ref[...] = up_ref[rows:, :]
+def cut_down_kernel(at_ref, down_ref, *refs):
+    for place, ref in enumerate(refs[-2:]):
+
+        @pl.when(pl.program_id(0) == place)
+        def _():
+            ref[...] = down_ref[...]
+
+
+def cut_down(at, down_target, waited):
+    count, wide = down_target.shape
+    part = jax.ShapeDtypeStruct((count // 4, wide), BF)
+    out = pl.BlockSpec((count // 4, wide), lambda i, at: (0, 0))
+    return pl.pallas_call(
+        cut_down_kernel,
+        out_shape=(part, part),
+        grid_spec=pltpu.PrefetchScalarGridSpec(
+            num_scalar_prefetch=1,
+            grid=(2,),
+            in_specs=[
+                pl.BlockSpec((count // 4, wide), lambda i, at: (at[1] * 2 + i, 0)),
+                ANYWHERE,
+            ],
+            out_specs=(out, out),
+        ),
+        compiler_params=pltpu.CompilerParams(vmem_limit_bytes=8 * 2**20),
+        cost_estimate=pl.CostEstimate(flops=1, bytes_accessed=1, transcendentals=0),
+        name="cut_down",
+    )(at, *in_hbm(down_target, waited))
+
+
+def norm_kernel(waited_ref, other_ref, own_ref, gain_ref, out_ref):
+    for place, ref in enumerate((other_ref, own_ref)):
+
+        @pl.when(pl.program_id(0) == place)
+        def _():
+            out_ref[...] = norm_rows(ref[...], gain_ref[...])
+
+
+def norm_call(waited, other_in, target_in, ln_gain):
+    rows, depth = target_in.shape
+    tile = 320
+    steps = rows // tile
+    return pl.pallas_call(
+        norm_kernel,
+        out_shape=pltpu.HBM((2 * rows, depth), BF),
+        grid=(2, steps),
+        in_specs=[
+            ANYWHERE,
+            pl.BlockSpec((tile, depth), lambda i, m: ((1 - i) * m + i * (steps - 1), 0)),
+            pl.BlockSpec((tile, depth), lambda i, m: (i * m, 0)),
+            pl.BlockSpec((1, depth), lambda i, m: (0, 0)),
+        ],
+        out_specs=pl.BlockSpec((tile, depth), lambda i, m: (i * steps + m, 0)),
+        compiler_params=pltpu.CompilerParams(vmem_limit_bytes=16 * 2**20),
+        cost_estimate=pl.CostEstimate(flops=1, bytes_accessed=1, transcendentals=0),
+        name="norm",
+    )(*in_hbm(waited), other_in, target_in, ln_gain[None])
+
+
+def cut_kernel(at_ref, whole_ref, *refs):
+    refs[-1][...] = whole_ref[...]
 
 
 def cut_up(at, up_target):
     depth, width = up_target.shape
-    part = jax.ShapeDtypeStruct((depth // 2, width // 2), BF)
     block = width // 8
-    out = pl.BlockSpec((depth // 2, block), lambda j, at: (0, j))
-    return pl.pallas_call(
-        cut_up_kernel,
-        out_shape=(part, part),
+    return pl.pallas_call(
+        cut_kernel,
+        out_shape=jax.ShapeDtypeStruct((depth, width // 2), BF),
         grid_spec=pltpu.PrefetchScalarGridSpec(
             num_scalar_prefetch=1,
             grid=(4,),
             in_specs=[
                 pl.BlockSpec((depth, block), lambda j, at: (0, (at[0] ^ j) * 2 + at[1]))
             ],
-            out_specs=(out, out),
+            out_specs=pl.BlockSpec((depth, block), lambda j, at: (0, j)),
         ),
         compiler_params=pltpu.CompilerParams(vmem_limit_bytes=8 * 2**20),
-        cost_estimate=pl.CostEstimate(
-            flops=0, bytes_accessed=2 * depth * width, transcendentals=0
-        ),
+        cost_estimate=pl.CostEstimate(flops=1, bytes_accessed=1, transcendentals=0),
         name="cut_up",
-    )(at, up_target)
-
-
-def up_kernel(at_ref, other_ref, own_ref, *refs):
-    pieces, (out_ref, x_ref, w_ref, sem, x_sem) = refs[:8], refs[8:]
-    step = pl.program_id(0)
+    )(at, *in_hbm(up_target))
+
+
+def up_kernel(waited_ref, x_ref, *refs):
+    pieces, (out_ref, w_ref, sem) = refs[:5], refs[5:]
+    m, n = pl.program_id(0), pl.program_id(1)
     depth, width = pieces[0].shape
     block = width // 4
-    me = at_ref[0]
-    rows = own_ref.shape[0]
-    tile = out_ref.shape[1]
-    x_made = [
-        pltpu.make_async_copy(ref, x_ref.at[pl.ds(i * rows, rows)], x_sem.at[i])
-        for i, ref in enumerate((other_ref, own_ref))
-    ]
+    me = lax.axis_index("dp")
 
     def copies(n):
         found = []
         for j in (2 * n, 2 * n + 1):
             for p, piece in enumerate(pieces):
-                i, h = p // 2, p % 2
-                row = pl.multiple_of(((me ^ i) * 2 + h) * depth, 16)
+                i, rows = min(p, 3), piece.shape[0]
+                row = pl.multiple_of((me ^ i) * depth + (p // 4) * rows, 16)
                 found.append(
                     pltpu.make_async_copy(
                         piece.at[:, pl.ds((j ^ i) * block, block)],
-                        w_ref.at[pl.ds(row, depth), pl.ds(j * block, block)],
+                        w_ref.at[n, pl.ds(row, rows), pl.ds((j % 2) * block, block)],
                         sem.at[n, len(found)],
                     )
                 )
         return found
 
-    @pl.when(step == 0)
+    @pl.when((m == 0) & (n == 0))
     def _():
-        for c in copies(0) + x_made + copies(1):
+        for c in copies(0) + copies(1):
             c.start()
-        for c in copies(0) + x_made:
+        for c in copies(0):
             c.wait()
 
-    @pl.when(step == pl.num_programs(0) // 2)
+    @pl.when((m == 0) & (n == 1))
     def _():
         for c in copies(1):
             c.wait()
 
-    w = w_ref[:, pl.ds(pl.multiple_of(step * tile, tile), tile)]
-    out_ref[...] = gelu(dot(x_ref[...], w)).astype(BF)
-
-
-def up_call(at, other_n, own_n, pieces):
-    rows, depth = own_n.shape
+    out_ref[...] = gelu(dot(x_ref[...], w_ref[n])).astype(BF)
+
+
+def up_call(waited, normed, pieces):
+    rows, depth = normed.shape
     width = pieces[0].shape[1]
-    tile = 256
-    hbm = pl.BlockSpec(memory_space=pltpu.HBM)
+    tile = 640
     return pl.pallas_call(
         up_kernel,
-        out_shape=jax.ShapeDtypeStruct((2 * rows, width), BF),
-        grid=(width // tile,),
-        in_specs=[pl.BlockSpec(memory_space=pltpu.SMEM)] + [hbm] * 10,
-        out_specs=pl.BlockSpec((2 * rows, tile), lambda n: (0, n)),
+        out_shape=pltpu.HBM((rows, width), BF),
+        grid=(rows // tile, 2),
+        in_specs=[ANYWHERE, pl.BlockSpec((tile, depth), lambda m, n: (m, 0))]
+        + [ANYWHERE] * 5,
+        out_specs=pl.BlockSpec((tile, width // 2), lambda m, n: (m, n)),
         scratch_shapes=[
-            pltpu.VMEM((2 * rows, depth), BF),
-            pltpu.VMEM((depth, width), BF),
-            pltpu.SemaphoreType.DMA((2, 16)),
-            pltpu.SemaphoreType.DMA((2,)),
+            pltpu.VMEM((2, depth, width // 2), BF),
+            pltpu.SemaphoreType.DMA((2, 10)),
         ],
-        compiler_params=pltpu.CompilerParams(vmem_limit_bytes=20 * 2**20),
-        cost_estimate=pl.CostEstimate(
-            flops=8 * rows * depth * width, bytes_accessed=12 * 10**6, transcendentals=0
-        ),
+        compiler_params=pltpu.CompilerParams(vmem_limit_bytes=60 * 2**20),
+        cost_estimate=pl.CostEstimate(flops=1, bytes_accessed=1, transcendentals=0),
         name="up",
-    )(at, other_n, own_n, *pieces)
-
-
-def down_kernel(h_ref, *refs):
+    )(*in_hbm(waited, normed), *pieces)
+
+
+def down_kernel(waited_ref, h_ref, *refs):
     pieces, (out_ref, w_ref, sem) = refs[:6], refs[6:]
     count = pieces[0].shape[0]
 
@@ -168,7 +257,7 @@
     out_ref[...] = dot(h_ref[:, : 6 * count], w_ref[...])
 
 
-def down_call(hidden, pieces):
+def down_call(waited, hidden, pieces):
     rows, width = hidden.shape
     count, wide = pieces[0].shape
     tile = 320
@@ -176,31 +265,29 @@
         down_kernel,
         out_shape=jax.ShapeDtypeStruct((rows, wide), F32),
         grid=(rows // tile,),
-        in_specs=[pl.BlockSpec((tile, width), lambda m: (m, 0))]
-        + [pl.BlockSpec(memory_space=pltpu.HBM)] * 6,
+        in_specs=[ANYWHERE, pl.BlockSpec((tile, width), lambda m: (m, 0))]
+        + [ANYWHERE] * 6,
         out_specs=pl.BlockSpec((tile, wide), lambda m: (m, 0)),
         scratch_shapes=[
             pltpu.VMEM((6 * count, wide), BF),
             pltpu.SemaphoreType.DMA((6,)),
         ],
         compiler_params=pltpu.CompilerParams(vmem_limit_bytes=20 * 2**20),
-        cost_estimate=pl.CostEstimate(
-            flops=16 * rows * count * wide, bytes_accessed=15 * 10**6, transcendentals=0
-        ),
+        cost_estimate=pl.CostEstimate(flops=1, bytes_accessed=1, transcendentals=0),
         name="down",
-    )(hidden, *pieces)
-
-
-def last_kernel(h_ref, da, db, sum_ref, *refs):
+    )(*in_hbm(waited, hidden), *pieces)
+
+
+def last_kernel(waited_ref, h_ref, da, db, sum_ref, *refs):
     top = da.shape[0]
-    out_ref = refs[-1]
+    *more, out_ref = refs
     total = sum_ref[...] + dot(h_ref[:, :top], da[...]) + dot(h_ref[:, top:], db[...])
-    if len(refs) == 2:
-        total = total + refs[0][...].astype(F32)
+    for ref in more:
+        total = total + ref[...].astype(F32)
     out_ref[...] = total.astype(out_ref.dtype)
 
 
-def last_call(hidden, da, db, sums, first, rows_in, dtype):
+def last_call(waited, hidden, da, db, sums, first, rows_in, dtype):
     top, wide = da.shape
     count = hidden.shape[1] // 4
     rows, tile = hidden.shape[0] // 2, 320
@@ -212,6 +299,7 @@
         out_shape=jax.ShapeDtypeStruct((rows, wide), dtype),
         grid=(rows // tile,),
         in_specs=[
+            ANYWHERE,
             pl.BlockSpec((tile, count), lambda m: (m + skip, 3)),
             whole,
             whole,
@@ -220,11 +308,9 @@
         + [pl.BlockSpec((tile, wide), lambda m: (m, 0)) for _ in extra],
         out_specs=pl.BlockSpec((tile, wide), lambda m: (m, 0)),
         compiler_params=pltpu.CompilerParams(vmem_limit_bytes=24 * 2**20),
-        cost_estimate=pl.CostEstimate(
-            flops=3 * rows * count * wide, bytes_accessed=6 * 10**6, transcendentals=0
-        ),
+        cost_estimate=pl.CostEstimate(flops=1, bytes_accessed=1, transcendentals=0),
         name="last",
-    )(hidden, da, db, sums, *extra)
+    )(waited, *in_hbm(hidden), da, db, sums, *extra)
 
 
 def program_square(
@@ -250,40 +336,34 @@
 
     at = jnp.stack([me, core]).astype(jnp.int32)
 
-    def both(parts):
-        return [lax.ppermute(parts[h], "dp", p) for p in (px, py) for h in range(2)]
-
-    ups = cut_up(at, up_target)
-    ux_t, ux_b, uy_t, uy_b = both(ups)
-    dispatched = lax.all_to_all(
-        dispatch_rows(pred_rows, expert_ids), "expert", 0, 0, tiled=True
+    def both(piece):
+        return lax.ppermute(piece, "dp", px), lax.ppermute(piece, "dp", py)
+
+    up_0 = cut_up(at, up_target)
+    up_x, up_y = both(up_0)
+    ids_t, weights_t = expert_ids.T, combine_weights.T
+    other_in = lax.ppermute(target_in, "expert", pc)
+    outgoing = send_call(up_0, pred_rows, ids_t)
+    dispatched = lax.all_to_all(outgoing, "expert", 0, 0, tiled=True)
+    normed = norm_call(outgoing, other_in, target_in, ln_gain)
+    upper, lower = halves(normed, up_y, up_x)
+    ud_t, ud_b = lax.ppermute(upper, "dp", px), lax.ppermute(lower, "dp", py)
+    d_t, d_b = hold(upper, *cut_down(at, down_target, normed))
+    dx_t, dy_t = both(d_t)
+    dx_b, dy_b = both(d_b)
+    by_cols = expert_call(
+        dispatched, gate_experts, up_experts, down_experts, *in_hbm(upper)
     )
-    other_in = lax.ppermute(target_in, "expert", pc)
-    ud_t, ud_b = lax.ppermute(uy_t, "dp", px), lax.ppermute(ux_b, "dp", py)
-    part = half // 2
-    downs = [
-        lax.dynamic_slice(down_target, (core * half + h * part, 0), (part, wide))
-        for h in range(2)
-    ]
-    dx_t, dx_b, dy_t, dy_b = both([after(d, ux_b, uy_t) for d in downs])
+    back = lax.all_to_all(by_cols, ("dp", "expert"), 0, 0, tiled=True)
+    hidden = up_call(by_cols, normed, (up_0, up_x, up_y, ud_t, ud_b))
+    dx_b, dy_t = hold(hidden, dx_b, dy_t)
     dd_t, dd_b = lax.ppermute(dy_t, "dp", px), lax.ppermute(dx_b, "dp", py)
-    other_n, own_n = norm_rows(other_in, ln_gain), norm_rows(target_in, ln_gain)
-    dispatched = after(dispatched, ux_b, uy_t, other_n, own_n)
-    by_cols = expert_call(dispatched, gate_experts, up_experts, down_experts)
-    back = lax.all_to_all(by_cols, ("dp", "expert"), 0, 0, tiled=True)
-    hidden = up_call(
-        at,
-        after(other_n, by_cols),
-        own_n,
-        (*ups, ux_t, ux_b, uy_t, uy_b, ud_t, ud_b),
-    )
-    sums = down_call(hidden, (*downs, dx_t, dx_b, dy_t, dy_b))
-    predicted = combine(pred_rows, expert_ids, combine_weights, back)
-    sums = after(sums, predicted)
+    predicted = mix_call(at, hidden, pred_rows, ids_t, weights_t, back)
+    sums = down_call(predicted, hidden, (d_t, d_b, dx_t, dx_b, dy_t, dy_b))
     rows = target_in.shape[0]
-    other_sum = last_call(hidden, dd_t, dd_b, sums, 0, None, BF)
+    other_sum = last_call(*in_hbm(predicted), hidden, dd_t, dd_b, sums, 0, None, BF)
     received = lax.ppermute(other_sum, "expert", pc)
-    own_sum = last_call(hidden, dd_t, dd_b, sums, rows, target_in, F32)
+    own_sum = last_call(other_sum, hidden, dd_t, dd_b, sums, rows, target_in, F32)
     return (own_sum + received.astype(F32)).astype(BF), predicted
 
 
@@ -309,7 +389,8 @@
     return dot(pick, pred_rows).astype(BF).reshape(owners, CAP, width)
 
 
-def expert_kernel(x_ref, g_ref, u_ref, d_ref, out_ref, total):
+def expert_kernel(x_ref, g_ref, u_ref, d_ref, *refs):
+    out_ref, total = refs[-2:]
     step = pl.program_id(0)
     contract = (((1,), (1,)), ((), ()))
     x = x_ref[...]
@@ -336,7 +417,7 @@
                 out_ref[d] = total[:, d * share : (d + 1) * share].astype(BF)
 
 
-def expert_call(dispatched, gate_experts, up_experts, down_experts):
+def expert_call(dispatched, gate_experts, up_experts, down_experts, *waited):
     owners, cap, width = dispatched.shape
     n_dp = lax.axis_size("dp")
     share = width // n_dp
@@ -350,22 +431,18 @@
         expert_kernel,
         out_shape=jax.ShapeDtypeStruct(shape, BF),
         grid=(hidden // tile,),
-        in_specs=[pl.BlockSpec((rows, width), lambda i: (0, 0))] + [weights] * 3,
+        in_specs=[pl.BlockSpec((rows, width), lambda i: (0, 0))]
+        + [weights] * 3
+        + [pl.BlockSpec(memory_space=pl.ANY)] * len(waited),
         out_specs=pl.BlockSpec(shape, lambda i: (0,) * len(shape)),
         scratch_shapes=[pltpu.VMEM((rows, width), F32)],
         compiler_params=pltpu.CompilerParams(vmem_limit_bytes=24 * 2**20),
-        cost_estimate=pl.CostEstimate(
-            flops=6 * rows * hidden * width,
-            bytes_accessed=6 * hidden * width + 4 * rows * width,
-            transcendentals=0,
-        ),
+        cost_estimate=pl.CostEstimate(flops=1, bytes_accessed=1, transcendentals=0),
         name="expert",
     )(
         dispatched.reshape(rows, width),
-        *[
-            pltpu.with_memory_space_constraint(w, pltpu.HBM)
-            for w in (gate_experts, up_experts, down_experts)
-        ],
+        *in_hbm(gate_experts, up_experts, down_experts),
+        *waited,
     )
     if not whole:
         out = out.reshape(rows, n_dp, share).transpose(1, 0, 2)
@@ -400,6 +477,92 @@
     return (residual + mixed_out).astype(BF)
 
 
+def iota(shape, dim):
+    return lax.broadcasted_iota(jnp.int32, shape, dim)
+
+
+def slot_rows_of(ids_ref, first, count):
+    rows = ids_ref.shape[1]
+    n_slots = count * CAP
+    each = iota((count, rows), 0) + first
+    hits = [ids_ref[k : k + 1, :] == each for k in range(TOP)]
+    named = jnp.zeros((count, rows), F32)
+    for hit in hits:
+        named = jnp.where(hit, 1.0, named)
+    before = jnp.where(iota((rows, rows), 0) < iota((rows, rows), 1), 1.0, 0.0)
+    slot = dot(named.astype(BF), before.astype(BF))
+    slot = jnp.where(named > 0.0, slot, -1.0).astype(BF)
+    gap = iota((n_slots, count), 0) - CAP * iota((n_slots, count), 1)
+    spread = jnp.where((gap >= 0) & (gap < CAP), 1.0, 0.0).astype(BF)
+    place = (iota((n_slots, 1), 0) & (CAP - 1)).astype(F32)
+    return hits, spread, dot(spread, slot) == place
+
+
+def send_kernel(waited_ref, ids_ref, rows_ref, out_ref):
+    owners = out_ref.shape[0] // CAP
+    _, _, hit = slot_rows_of(ids_ref, (lax.axis_index("dp") % EXP_DEV) * owners, owners)
+    pick = jnp.where(hit, 1.0, 0.0).astype(BF)
+    out_ref[...] = dot(pick, rows_ref[...]).astype(BF)
+
+
+def send_call(waited, pred_rows, ids_t):
+    owners = lax.axis_size("expert")
+    rows, width = pred_rows.shape
+    vmem = pl.BlockSpec(memory_space=pltpu.VMEM)
+    out = pl.pallas_call(
+        send_kernel,
+        out_shape=jax.ShapeDtypeStruct((owners * CAP, width), BF),
+        in_specs=[ANYWHERE, vmem, vmem],
+        out_specs=vmem,
+        compiler_params=pltpu.CompilerParams(vmem_limit_bytes=12 * 2**20),
+        cost_estimate=pl.CostEstimate(flops=1, bytes_accessed=1, transcendentals=0),
+        name="send",
+    )(*in_hbm(waited), ids_t, pred_rows)
+    return out.reshape(owners, CAP, width)
+
+
+def mix_kernel(at_ref, waited_ref, ids_ref, weights_ref, back_ref, pred_ref, out_ref):
+    n_all = back_ref.shape[0] // CAP
+    hits, spread, hit = slot_rows_of(ids_ref, 0, n_all)
+    weight = 0.0
+    for k in range(TOP):
+        weight = weight + jnp.where(hits[k], weights_ref[k : k + 1, :], 0.0)
+    high = weight.astype(BF)
+    low = (weight - high.astype(F32)).astype(BF)
+    total = pred_ref[...].astype(F32)
+    for part in (high, low):
+        mix = jnp.where(hit, dot(spread, part), 0.0).astype(BF)
+        total = total + lax.dot_general(
+            mix, back_ref[...], (((0,), (0,)), ((), ())), preferred_element_type=F32
+        )
+    out_ref[...] = total.astype(BF)
+
+
+def mix_call(at, waited, pred_rows, ids_t, weights_t, back):
+    rows, width = pred_rows.shape
+    blocks, cap, share = back.shape
+    whole = lambda shape: pl.BlockSpec(shape, lambda i, at: (0, 0))
+    return pl.pallas_call(
+        mix_kernel,
+        out_shape=jax.ShapeDtypeStruct((rows, share), BF),
+        grid_spec=pltpu.PrefetchScalarGridSpec(
+            num_scalar_prefetch=1,
+            grid=(1,),
+            in_specs=[
+                ANYWHERE,
+                whole((TOP, rows)),
+                whole((TOP, rows)),
+                whole((blocks * cap, share)),
+                pl.BlockSpec((rows, share), lambda i, at: (0, at[0])),
+            ],
+            out_specs=whole((rows, share)),
+        ),
+        compiler_params=pltpu.CompilerParams(vmem_limit_bytes=16 * 2**20),
+        cost_estimate=pl.CostEstimate(flops=1, bytes_accessed=1, transcendentals=0),
+        name="mix",
+    )(at, *in_hbm(waited), ids_t, weights_t, back.reshape(blocks * cap, share), pred_rows)
+
+
 def program_any(
     target_in,
     ln_gain,

time: 105 us -> 98.2 us (0.935)
  Pallas kernels: 33.3 us -> 53.9 us
  local copies, waits for them, and re-layouts: 13.3 us -> 0.85 us
  other arithmetic: 10.9 us -> 1.61 us
  matrix products: 7.1 us -> 0 us
  waiting for transfers between devices: 13 us -> 17.7 us
  starting transfers between devices: 25.4 us -> 22.8 us
    pallas_call x2 -> x9, Pallas kernels: 13.3 us -> 30.1 us  [the longest x1 12.2 us: up_call(): pl.pallas_call(up_kernel, out_shape=pltpu.HBM((rows, width), BF), grid=(r...]
    unnamed x26 -> x20, local copies, waits for them, and re-layouts: 11 us -> 0.84 us
    dot_general x5 -> x0, matrix products: 7.1 us -> none  [the longest x2 4.4 us: combine(): lax.dot_general(part, back[q], over, preferred_element_type=F32)]
    ppermute x10 -> x8, waiting for transfers between devices: 10.7 us -> 15.7 us  [the longest x6 15.7 us: both(): return (lax.ppermute(piece, 'dp', px), lax.ppermute(piece, 'dp', py))]
    reduce_sum x4 -> x0, other arithmetic: 4.79 us -> none  [the longest x2 2.69 us: norm_rows(): variance = jnp.mean(centered * centered, axis=-1, keepdims=True)]
    convert_element_type x1 -> x0, other arithmetic: 3.63 us -> none  [norm_rows(): return (centered * lax.rsqrt(variance + 1e-06) * gain).astype(BF)]
    pallas_call x2, Pallas kernels: 2.85 us -> 5.12 us  [last_call(): pl.pallas_call(last_kernel, out_shape=jax.ShapeDtypeStruct((rows, wide),...]
    dynamic_slice x1 -> x0, local copies, waits for them, and re-layouts: 2.13 us -> none  [program_square(): lax.dynamic_slice(down_target, (core * half + h * part, 0), (part, wide))]
  transfers between devices with their start and end apart: 16 -> 14, of which waited for: 5 -> 6; matrix products, arithmetic and copies ran while one was open for 18% -> 0% of each run, Pallas kernels for 29% -> 51%
where the time goes in v3:
time: 98.2 us; the launch traced here: 97.7 us
  Pallas kernels  53.9 us (55%)
  starting transfers between devices  22.8 us (23%)
  waiting for transfers between devices  17.7 us (18%)
  other arithmetic  1.61 us (2%)
    ppermute x6, waiting for transfers between devices, both(): return (lax.ppermute(piece, 'dp', px), lax.ppermute(piece, 'dp', py))  15.7 us
    pallas_call x1, Pallas kernels, up_call(): pl.pallas_call(up_kernel, out_shape=pltpu.HBM((rows, width), BF), grid=(r...  12.2 us
    pallas_call x1, Pallas kernels, expert_call(): pl.pallas_call(expert_kernel, out_shape=jax.ShapeDtypeStruct(shape, BF),...  10 us
    ppermute x6, starting transfers between devices, both(): return (lax.ppermute(piece, 'dp', px), lax.ppermute(piece, 'dp', py))  9.33 us
    pallas_call x1, Pallas kernels, down_call(): pl.pallas_call(down_kernel, out_shape=jax.ShapeDtypeStruct((rows, wide),...  8.71 us
    pallas_call x2, Pallas kernels, last_call(): pl.pallas_call(last_kernel, out_shape=jax.ShapeDtypeStruct((rows, wide),...  5.12 us
    all_to_all x1, starting transfers between devices, program_square(): back = lax.all_to_all(by_cols, ('dp', 'expert'), 0, 0, tiled=True)  5.05 us
    pallas_call x1, Pallas kernels, norm_call(): pl.pallas_call(norm_kernel, out_shape=pltpu.HBM((2 * rows, depth), BF), g...  4.89 us
  transfers between devices with their start and end apart: 14, of which 6 were waited for; matrix products, arithmetic and copies ran while one was open for 0% of the time, Pallas kernels for 51%

profile of v3, /device:TPU:0, one launch (start us, length us, event | category | flops | bytes accessed | tf_op | source)
XLA Modules:
  0.0 97.7 jit_solution(16588455826830132369)
XLA Ops:
  0.6 0.5 collective-permute-start
  1.2 0.1 pad_add_fusion.at_ref
  1.2 2.7 %cut_up.1.waited_ref.refs_0_ = bf16[352,1536]{1,0:T(8,128)(2,1)S(1)} custom-call(s32[2]{0:T(128)S(1)} %pad_add_fusion.at_ref, bf16[352,3072]{1,0:T(8,128)(2,1)} %whole_ref.1), custom_call_target="tpu_custom_call" | custom-call | flops 1 | bytes 1 | tf_op jit(solution)/shard_map/cut_up/pallas_call | solution.py:167
  3.9 0.0 copy-start
  4.0 0.0 copy-start.9
  4.0 0.0 copy-start.1
  4.0 2.6 %collective-permute-start.2 = (bf16[352,1536]{1,0:T(8,128)(2,1)S(1)}, bf16[352,1536]{1,0:T(8,128)(2,1)}, u32[]{:S(2)}, u32[]{:S(2)}) collective-permute-start(bf16[352,1536]{1,0:T(8,128)(2,1)S(1)} %cut_up.1.waited_ref.refs_0_), channel_id=1, source_target_pairs={{0,8},{8,0},{16,24},{24,16},{1,9},{9,1},{17,25},{25,17},{2,10},{10... | collective-permute-start | bytes 3244040 | tf_op jit(solution)/shard_map/ppermute | solution.py:340
  6.6 1.5 %collective-permute-start.1 = (bf16[352,1536]{1,0:T(8,128)(2,1)S(1)}, bf16[352,1536]{1,0:T(8,128)(2,1)}, u32[]{:S(2)}, u32[]{:S(2)}) collective-permute-start(bf16[352,1536]{1,0:T(8,128)(2,1)S(1)} %cut_up.1.waited_ref.refs_0_), channel_id=1, source_target_pairs={{0,16},{8,24},{16,0},{24,8},{1,17},{9,25},{17,1},{25,9},{2,18},{10... | collective-permute-start | bytes 3244040 | tf_op jit(solution)/shard_map/ppermute | solution.py:340
  8.1 1.5 %send.1 = bf16[256,1024]{1,0:T(8,128)(2,1)} custom-call(bf16[352,1536]{1,0:T(8,128)(2,1)} %copy-done, s32[2,384]{1,0:T(2,128)S(1)} %bitcast.9, bf16[384,1024]{1,0:T(8,128)(2,1)S(1)} %copy-done.2), custom_call_target="tpu_custom_call" | custom-call | flops 1 | bytes 1 | tf_op jit(solution)/shard_map/send/pallas_call | solution.py:512
  9.6 4.9 %all-to-all-start = ((bf16[8,32,1024]{2,1,0:T(8,128)(2,1)}), bf16[8,32,1024]{2,1,0:T(8,128)(2,1)S(1)}, u32[]{:S(2)}, u32[]{:S(2)}) async-start(bf16[8,32,1024]{2,1,0:T(8,128)(2,1)} %bitcast.3.waited_ref), calls=%async_computation | async-start | bytes 1048576 | tf_op jit(solution)/shard_map/all_to_all | solution.py:347
  14.5 0.0 collective-permute-done.other_ref
  14.5 4.9 %norm.1.waited_ref.x_ref.refs_0_ = bf16[1280,1408]{1,0:T(8,128)(2,1)} custom-call(bf16[8,32,1024]{2,1,0:T(8,128)(2,1)} %bitcast.3.waited_ref, bf16[640,1408]{1,0:T(8,128)(2,1)} %collective-permute-done.other_ref, bf16[640,1408]{1,0:T(8,128)(2,1)S(1)} %copy-done.1, f32[1,1408]{1,0:T(1,128)S(1)} %broadcast_in_dim.3.gain_ref), custom_call_target="tpu_custom_call" | custom-call | flops 1 | bytes 1 | tf_op jit(solution)/shard_map/norm/pallas_call | solution.py:143
  19.4 2.8 %cut_down.1 = (bf16[192,1408]{1,0:T(8,128)(2,1)}, bf16[192,1408]{1,0:T(8,128)(2,1)}) custom-call(s32[2]{0:T(128)S(1)} %pad_add_fusion.at_ref, bf16[768,1408]{1,0:T(8,128)(2,1)} %down_ref.1, bf16[1280,1408]{1,0:T(8,128)(2,1)} %norm.1.waited_ref.x_ref.refs_0_), custom_call_target="tpu_custom_call" | custom-call | flops 1 | bytes 1 | tf_op jit(solution)/shard_map/cut_down/pallas_call | solution.py:113
  22.2 9.0 %collective-permute-done.2.second_ref.refs_1_ = bf16[352,1536]{1,0:T(8,128)(2,1)} collective-permute-done((bf16[352,1536]{1,0:T(8,128)(2,1)S(1)}, bf16[352,1536]{1,0:T(8,128)(2,1)}, u32[]{:S(2)}, u32[]{:S(2)}) %collective-permute-start.2) | collective-permute-done | bytes 1081376 | tf_op jit(solution)/shard_map/ppermute | solution.py:340
  31.2 1.5 %collective-permute-done.1.first_ref.refs_2_ = bf16[352,1536]{1,0:T(8,128)(2,1)} collective-permute-done((bf16[352,1536]{1,0:T(8,128)(2,1)S(1)}, bf16[352,1536]{1,0:T(8,128)(2,1)}, u32[]{:S(2)}, u32[]{:S(2)}) %collective-permute-start.1) | collective-permute-done | bytes 1081376 | tf_op jit(solution)/shard_map/ppermute | solution.py:340
  32.6 2.0 %halves.1 = (bf16[176,1536]{1,0:T(8,128)(2,1)S(1)}, bf16[176,1536]{1,0:T(8,128)(2,1)}) custom-call(bf16[1280,1408]{1,0:T(8,128)(2,1)} %norm.1.waited_ref.x_ref.refs_0_, bf16[352,1536]{1,0:T(8,128)(2,1)} %collective-permute-done.1.first_ref.refs_2_, bf16[352,1536]{1,0:T(8,128)(2,1)} %collective-permute-done.2.second_ref.refs_1_), custom_call_target="tpu_custom_call" | custom-call | flops 1 | bytes 1 | tf_op jit(solution)/shard_map/halves/pallas_call | solution.py:63
  34.6 1.5 %collective-permute-start.4 = (bf16[176,1536]{1,0:T(8,128)(2,1)}, bf16[176,1536]{1,0:T(8,128)(2,1)}, u32[]{:S(2)}, u32[]{:S(2)}) collective-permute-start(bf16[176,1536]{1,0:T(8,128)(2,1)} %get-tuple-element.11), channel_id=1, source_target_pairs={{0,16},{8,24},{16,0},{24,8},{1,17},{9,25},{17,1},{25,9},{2,18},{10... | collective-permute-start | bytes 1622024 | tf_op jit(solution)/shard_map/ppermute | solution.py:350
  36.1 0.5 collective-permute-start.3
  36.7 1.5 %collective-permute-start.5 = (bf16[192,1408]{1,0:T(8,128)(2,1)}, bf16[192,1408]{1,0:T(8,128)(2,1)S(1)}, u32[]{:S(2)}, u32[]{:S(2)}) collective-permute-start(bf16[192,1408]{1,0:T(8,128)(2,1)} %get-tuple-element.14.refs_1_), channel_id=1, source_target_pairs={{0,8},{8,0},{16,24},{24,16},{1,9},{9,1},{17,25},{25,17},{2,10},{10... | collective-permute-start | bytes 1622024 | tf_op jit(solution)/shard_map/ppermute | solution.py:340
  38.2 0.5 collective-permute-start.6
  38.7 0.0 all-to-all-done
  38.7 10.0 %expert.1 = bf16[4,256,256]{2,1,0:T(8,128)(2,1)} custom-call(bf16[256,1024]{1,0:T(8,128)(2,1)S(1)} %bitcast.8, bf16[1,2816,1024]{2,1,0:T(8,128)(2,1)} %g_ref.1, bf16[1,2816,1024]{2,1,0:T(8,128)(2,1)} %u_ref.1, bf16[1,2816,1024]{2,1,0:T(8,128)(2,1)} %d_ref.1, bf16[176,1536]{1,0:T(8,128)(2,1)} %copy-done.6), custom_call_target="tpu_custom_call" | custom-call | flops 1 | bytes 1 | tf_op jit(solution)/shard_map/expert/pallas_call | solution.py:430
  48.7 5.0 %all-to-all-start.1 = ((bf16[32,32,256]{2,1,0:T(8,128)(2,1)}), bf16[32,32,256]{2,1,0:T(8,128)(2,1)}, u32[]{:S(2)}, u32[]{:S(2)}) async-start(bf16[32,32,256]{2,1,0:T(8,128)(2,1)} %bitcast.5.waited_ref), calls=%async_computation.1 | async-start | bytes 1048576 | tf_op jit(solution)/shard_map/all_to_all | solution.py:357
  53.8 1.8 %collective-permute-start.10 = (bf16[192,1408]{1,0:T(8,128)(2,1)}, bf16[192,1408]{1,0:T(8,128)(2,1)}, u32[]{:S(2)}, u32[]{:S(2)}) collective-permute-start(bf16[192,1408]{1,0:T(8,128)(2,1)} %get-tuple-element.14.refs_1_), channel_id=1, source_target_pairs={{0,16},{8,24},{16,0},{24,8},{1,17},{9,25},{17,1},{25,9},{2,18},{10... | collective-permute-start | bytes 1622024 | tf_op jit(solution)/shard_map/ppermute | solution.py:340
  55.5 0.0 collective-permute-done.4.refs_4_
  55.5 1.5 %collective-permute-start.9 = (bf16[192,1408]{1,0:T(8,128)(2,1)}, bf16[192,1408]{1,0:T(8,128)(2,1)}, u32[]{:S(2)}, u32[]{:S(2)}) collective-permute-start(bf16[192,1408]{1,0:T(8,128)(2,1)} %get-tuple-element.15.refs_0_), channel_id=1, source_target_pairs={{0,8},{8,0},{16,24},{24,16},{1,9},{9,1},{17,25},{25,17},{2,10},{10... | collective-permute-start | bytes 1622024 | tf_op jit(solution)/shard_map/ppermute | solution.py:340
  57.0 0.0 collective-permute-done.3.refs_3_
  57.0 12.2 %up.1.waited_ref.refs_0_.h_ref = bf16[1280,1536]{1,0:T(8,128)(2,1)} custom-call(bf16[32,32,256]{2,1,0:T(8,128)(2,1)} %bitcast.5.waited_ref, bf16[1280,1408]{1,0:T(8,128)(2,1)} %norm.1.waited_ref.x_ref.refs_0_, bf16[352,1536]{1,0:T(8,128)(2,1)} %copy-done, bf16[352,1536]{1,0:T(8,128)(2,1)} %collective-permute-done.2.second_ref.refs_1_, ...), custom_call_target="tpu_custom_call" | custom-call | flops 1 | bytes 1 | tf_op jit(solution)/shard_map/up/pallas_call | solution.py:225
  69.2 0.0 copy-start.3
  69.2 0.0 copy-start.8
  69.2 0.0 collective-permute-done.5.refs_1_
  69.2 0.0 collective-permute-done.6.refs_2_
  69.3 0.0 copy-start.4
  69.3 0.8 copy-done.4
  70.1 0.6 collective-permute-start.7
  70.6 0.3 collective-permute-start.8
  70.9 0.0 all-to-all-done.1
  71.0 0.0 copy-start.5
  71.0 4.0 %mix.1.waited_ref = bf16[384,256]{1,0:T(8,128)(2,1)} custom-call(s32[2]{0:T(128)S(1)} %pad_add_fusion.at_ref, bf16[1280,1536]{1,0:T(8,128)(2,1)} %up.1.waited_ref.refs_0_.h_ref, s32[2,384]{1,0:T(2,128)S(1)} %bitcast.10, f32[2,384]{1,0:T(2,128)S(1)} %bitcast.11, bf16[1024,256]{1,0:T(8,128)(2,1)} %bitcast.7.back_ref, bf16[384,1024]{1,0:T(8,128)(2,1)S(1)} %copy-done.3), custom_call_target="tpu_custom_call" | custom-call | flops 1 | bytes 1 | tf_op jit(solution)/shard_map/mix/pallas_call | solution.py:545
  74.9 4.0 %collective-permute-done.10.refs_5_ = bf16[192,1408]{1,0:T(8,128)(2,1)} collective-permute-done((bf16[192,1408]{1,0:T(8,128)(2,1)}, bf16[192,1408]{1,0:T(8,128)(2,1)}, u32[]{:S(2)}, u32[]{:S(2)}) %collective-permute-start.10) | collective-permute-done | bytes 540704 | tf_op jit(solution)/shard_map/ppermute | solution.py:340
  78.9 1.3 %collective-permute-done.9.refs_2_ = bf16[192,1408]{1,0:T(8,128)(2,1)} collective-permute-done((bf16[192,1408]{1,0:T(8,128)(2,1)}, bf16[192,1408]{1,0:T(8,128)(2,1)}, u32[]{:S(2)}, u32[]{:S(2)}) %collective-permute-start.9) | collective-permute-done | bytes 540704 | tf_op jit(solution)/shard_map/ppermute | solution.py:340
  80.3 8.7 %down.1.sum_ref = f32[1280,1408]{1,0:T(8,128)S(1)} custom-call(bf16[384,256]{1,0:T(8,128)(2,1)} %mix.1.waited_ref, bf16[1280,1536]{1,0:T(8,128)(2,1)} %up.1.waited_ref.refs_0_.h_ref, bf16[192,1408]{1,0:T(8,128)(2,1)} %get-tuple-element.15.refs_0_, bf16[192,1408]{1,0:T(8,128)(2,1)} %get-tuple-element.14.refs_1_, ...), custom_call_target="tpu_custom_call" | custom-call | flops 1 | bytes 1 | tf_op jit(solution)/shard_map/down/pallas_call | solution.py:264
  89.0 0.8 collective-permute-done.7.da
  89.8 2.6 %last.2.waited_ref = bf16[640,1408]{1,0:T(8,128)(2,1)S(1)} custom-call(bf16[384,256]{1,0:T(8,128)(2,1)} %mix.1.waited_ref, bf16[1280,1536]{1,0:T(8,128)(2,1)} %up.1.waited_ref.refs_0_.h_ref, bf16[192,1408]{1,0:T(8,128)(2,1)S(1)} %collective-permute-done.7.da, bf16[192,1408]{1,0:T(8,128)(2,1)} %collective-permute-done.8.db, f32[1280,1408]{1,0:T(8,128)S(1)} %down.1.sum_ref), custom_call_target="tpu_custom_call" | custom-call | flops 1 | bytes 1 | tf_op jit(solution)/shard_map/last/pallas_call | solution.py:297
  92.4 0.1 collective-permute-start.11
  92.4 2.6 %last.3 = f32[640,1408]{1,0:T(8,128)S(1)} custom-call(bf16[640,1408]{1,0:T(8,128)(2,1)S(1)} %last.2.waited_ref, bf16[1280,1536]{1,0:T(8,128)(2,1)} %up.1.waited_ref.refs_0_.h_ref, bf16[192,1408]{1,0:T(8,128)(2,1)S(1)} %collective-permute-done.7.da, bf16[192,1408]{1,0:T(8,128)(2,1)} %collective-permute-done.8.db, f32[1280,1408]{1,0:T(8,128)S(1)} %down.1.sum_ref, ...), custom_call_target="tpu_custom_call" | custom-call | flops 1 | bytes 1 | tf_op jit(solution)/shard_map/last/pallas_call | solution.py:297
  95.0 1.2 %collective-permute-done.11 = bf16[640,1408]{1,0:T(8,128)(2,1)S(1)} collective-permute-done((bf16[640,1408]{1,0:T(8,128)(2,1)S(1)}, bf16[640,1408]{1,0:T(8,128)(2,1)S(1)}, u32[]{:S(2)}, u32[]{:S(2)}) %collective-permute-start.11) | collective-permute-done | bytes 1802272 | tf_op jit(solution)/shard_map/ppermute | solution.py:365
  96.2 1.5 %add_convert_fusion = bf16[640,1408]{1,0:T(8,128)(2,1)} fusion(f32[640,1408]{1,0:T(8,128)S(1)} %last.3, bf16[640,1408]{1,0:T(8,128)(2,1)S(1)} %collective-permute-done.11), kind=kLoop, calls=%fused_computation | loop fusion | flops 2703360 | bytes 7208960 | tf_op jit(solution)/shard_map/convert_element_type | solution.py:367
  (16 shorter events, 0.0 us)
Async XLA Ops:
  0.6 7.5 %copy-start.7 = (s32[384,2]{0,1:T(2,128)S(1)}, s32[384,2]{0,1:T(2,128)}, u32[]{:S(2)}) copy-start(s32[384,2]{0,1:T(2,128)} %param.15) | copy-start | bytes 9220
  0.6 13.8 %collective-permute-start = (bf16[640,1408]{1,0:T(8,128)(2,1)}, bf16[640,1408]{1,0:T(8,128)(2,1)}, u32[]{:S(2)}, u32[]{:S(2)}) collective-permute-start(bf16[640,1408]{1,0:T(8,128)(2,1)} %refs_0_.1), channel_id=1, source_target_pairs={{0,1},{1,0},{2,3},{3,2},{4,5},{5,4},{6,7},{7,6},{8,9},{9,8},{10,11... | collective-permute-start | bytes 5406728 | tf_op jit(solution)/shard_map/ppermute | solution.py:345
  1.2 6.9 %copy-start.2 = (bf16[384,1024]{1,0:T(8,128)(2,1)S(1)}, bf16[384,1024]{1,0:T(8,128)(2,1)}, u32[]{:S(2)}) copy-start(bf16[384,1024]{1,0:T(8,128)(2,1)} %pred_ref.1) | copy-start | bytes 2359300
  3.9 4.1 %copy-start = (bf16[352,1536]{1,0:T(8,128)(2,1)}, bf16[352,1536]{1,0:T(8,128)(2,1)S(1)}, u32[]{:S(2)}) copy-start(bf16[352,1536]{1,0:T(8,128)(2,1)S(1)} %cut_up.1.waited_ref.refs_0_) | copy-start | bytes 3244036
  4.0 10.5 %copy-start.9 = (f32[1408]{0:T(1024)S(1)}, f32[1408]{0:T(1024)}, u32[]{:S(2)}) copy-start(f32[1408]{0:T(1024)} %param.11) | copy-start | bytes 16900
  4.0 10.5 %copy-start.1 = (bf16[640,1408]{1,0:T(8,128)(2,1)S(1)}, bf16[640,1408]{1,0:T(8,128)(2,1)}, u32[]{:S(2)}) copy-start(bf16[640,1408]{1,0:T(8,128)(2,1)} %refs_0_.1) | copy-start | bytes 5406724
  4.0 27.2 %collective-permute-start.2 = (bf16[352,1536]{1,0:T(8,128)(2,1)S(1)}, bf16[352,1536]{1,0:T(8,128)(2,1)}, u32[]{:S(2)}, u32[]{:S(2)}) collective-permute-start(bf16[352,1536]{1,0:T(8,128)(2,1)S(1)} %cut_up.1.waited_ref.refs_0_), channel_id=1, source_target_pairs={{0,8},{8,0},{16,24},{24,16},{1,9},{9,1},{17,25},{25,17},{2,10},{10... | collective-permute-start | bytes 3244040 | tf_op jit(solution)/shard_map/ppermute | solution.py:340
  6.6 26.1 %collective-permute-start.1 = (bf16[352,1536]{1,0:T(8,128)(2,1)S(1)}, bf16[352,1536]{1,0:T(8,128)(2,1)}, u32[]{:S(2)}, u32[]{:S(2)}) collective-permute-start(bf16[352,1536]{1,0:T(8,128)(2,1)S(1)} %cut_up.1.waited_ref.refs_0_), channel_id=1, source_target_pairs={{0,16},{8,24},{16,0},{24,8},{1,17},{9,25},{17,1},{25,9},{2,18},{10... | collective-permute-start | bytes 3244040 | tf_op jit(solution)/shard_map/ppermute | solution.py:340
  9.6 29.1 %all-to-all-start = ((bf16[8,32,1024]{2,1,0:T(8,128)(2,1)}), bf16[8,32,1024]{2,1,0:T(8,128)(2,1)S(1)}, u32[]{:S(2)}, u32[]{:S(2)}) async-start(bf16[8,32,1024]{2,1,0:T(8,128)(2,1)} %bitcast.3.waited_ref), calls=%async_computation | async-start | bytes 1048576 | tf_op jit(solution)/shard_map/all_to_all | solution.py:347
  34.6 2.1 %copy-start.6 = (bf16[176,1536]{1,0:T(8,128)(2,1)}, bf16[176,1536]{1,0:T(8,128)(2,1)S(1)}, u32[]{:S(2)}) copy-start(bf16[176,1536]{1,0:T(8,128)(2,1)S(1)} %get-tuple-element.10.refs_0_) | copy-start | bytes 1622020
  34.6 20.9 %collective-permute-start.4 = (bf16[176,1536]{1,0:T(8,128)(2,1)}, bf16[176,1536]{1,0:T(8,128)(2,1)}, u32[]{:S(2)}, u32[]{:S(2)}) collective-permute-start(bf16[176,1536]{1,0:T(8,128)(2,1)} %get-tuple-element.11), channel_id=1, source_target_pairs={{0,16},{8,24},{16,0},{24,8},{1,17},{9,25},{17,1},{25,9},{2,18},{10... | collective-permute-start | bytes 1622024 | tf_op jit(solution)/shard_map/ppermute | solution.py:350
  36.1 20.9 %collective-permute-start.3 = (bf16[176,1536]{1,0:T(8,128)(2,1)S(1)}, bf16[176,1536]{1,0:T(8,128)(2,1)}, u32[]{:S(2)}, u32[]{:S(2)}) collective-permute-start(bf16[176,1536]{1,0:T(8,128)(2,1)S(1)} %get-tuple-element.10.refs_0_), channel_id=1, source_target_pairs={{0,8},{8,0},{16,24},{24,16},{1,9},{9,1},{17,25},{25,17},{2,10},{10... | collective-permute-start | bytes 1622024 | tf_op jit(solution)/shard_map/ppermute | solution.py:350
  36.7 32.5 %collective-permute-start.5 = (bf16[192,1408]{1,0:T(8,128)(2,1)}, bf16[192,1408]{1,0:T(8,128)(2,1)S(1)}, u32[]{:S(2)}, u32[]{:S(2)}) collective-permute-start(bf16[192,1408]{1,0:T(8,128)(2,1)} %get-tuple-element.14.refs_1_), channel_id=1, source_target_pairs={{0,8},{8,0},{16,24},{24,16},{1,9},{9,1},{17,25},{25,17},{2,10},{10... | collective-permute-start | bytes 1622024 | tf_op jit(solution)/shard_map/ppermute | solution.py:340
  38.2 31.1 %collective-permute-start.6 = (bf16[192,1408]{1,0:T(8,128)(2,1)}, bf16[192,1408]{1,0:T(8,128)(2,1)}, u32[]{:S(2)}, u32[]{:S(2)}) collective-permute-start(bf16[192,1408]{1,0:T(8,128)(2,1)} %get-tuple-element.15.refs_0_), channel_id=1, source_target_pairs={{0,16},{8,24},{16,0},{24,8},{1,17},{9,25},{17,1},{25,9},{2,18},{10... | collective-permute-start | bytes 1622024 | tf_op jit(solution)/shard_map/ppermute | solution.py:340
  48.7 22.2 %all-to-all-start.1 = ((bf16[32,32,256]{2,1,0:T(8,128)(2,1)}), bf16[32,32,256]{2,1,0:T(8,128)(2,1)}, u32[]{:S(2)}, u32[]{:S(2)}) async-start(bf16[32,32,256]{2,1,0:T(8,128)(2,1)} %bitcast.5.waited_ref), calls=%async_computation.1 | async-start | bytes 1048576 | tf_op jit(solution)/shard_map/all_to_all | solution.py:357
  53.8 25.2 %collective-permute-start.10 = (bf16[192,1408]{1,0:T(8,128)(2,1)}, bf16[192,1408]{1,0:T(8,128)(2,1)}, u32[]{:S(2)}, u32[]{:S(2)}) collective-permute-start(bf16[192,1408]{1,0:T(8,128)(2,1)} %get-tuple-element.14.refs_1_), channel_id=1, source_target_pairs={{0,16},{8,24},{16,0},{24,8},{1,17},{9,25},{17,1},{25,9},{2,18},{10... | collective-permute-start | bytes 1622024 | tf_op jit(solution)/shard_map/ppermute | solution.py:340
  55.5 24.7 %collective-permute-start.9 = (bf16[192,1408]{1,0:T(8,128)(2,1)}, bf16[192,1408]{1,0:T(8,128)(2,1)}, u32[]{:S(2)}, u32[]{:S(2)}) collective-permute-start(bf16[192,1408]{1,0:T(8,128)(2,1)} %get-tuple-element.15.refs_0_), channel_id=1, source_target_pairs={{0,8},{8,0},{16,24},{24,16},{1,9},{9,1},{17,25},{25,17},{2,10},{10... | collective-permute-start | bytes 1622024 | tf_op jit(solution)/shard_map/ppermute | solution.py:340
  69.2 1.8 %copy-start.3 = (bf16[384,1024]{1,0:T(8,128)(2,1)S(1)}, bf16[384,1024]{1,0:T(8,128)(2,1)}, u32[]{:S(2)}) copy-start(bf16[384,1024]{1,0:T(8,128)(2,1)} %pred_ref.1) | copy-start | bytes 2359300
  69.2 1.7 %copy-start.8 = (f32[384,2]{0,1:T(2,128)S(1)}, f32[384,2]{0,1:T(2,128)}, u32[]{:S(2)}) copy-start(f32[384,2]{0,1:T(2,128)} %param.16) | copy-start | bytes 9220
  69.3 0.8 copy-start.4
  70.1 19.7 %collective-permute-start.7 = (bf16[192,1408]{1,0:T(8,128)(2,1)}, bf16[192,1408]{1,0:T(8,128)(2,1)S(1)}, u32[]{:S(2)}, u32[]{:S(2)}) collective-permute-start(bf16[192,1408]{1,0:T(8,128)(2,1)} %get-tuple-element.16.refs_4_), channel_id=1, source_target_pairs={{0,8},{8,0},{16,24},{24,16},{1,9},{9,1},{17,25},{25,17},{2,10},{10... | collective-permute-start | bytes 1622024 | tf_op jit(solution)/shard_map/ppermute | solution.py:360
  70.6 19.2 %collective-permute-start.8 = (bf16[192,1408]{1,0:T(8,128)(2,1)}, bf16[192,1408]{1,0:T(8,128)(2,1)}, u32[]{:S(2)}, u32[]{:S(2)}) collective-permute-start(bf16[192,1408]{1,0:T(8,128)(2,1)} %copy-done.4), channel_id=1, source_target_pairs={{0,16},{8,24},{16,0},{24,8},{1,17},{9,25},{17,1},{25,9},{2,18},{10... | collective-permute-start | bytes 1622024 | tf_op jit(solution)/shard_map/ppermute | solution.py:360
  71.0 9.3 %copy-start.5 = (bf16[192,1408]{1,0:T(8,128)(2,1)S(1)}, bf16[192,1408]{1,0:T(8,128)(2,1)}, u32[]{:S(2)}) copy-start(bf16[192,1408]{1,0:T(8,128)(2,1)} %copy-done.4) | copy-start | bytes 1622020
  92.4 3.8 %collective-permute-start.11 = (bf16[640,1408]{1,0:T(8,128)(2,1)S(1)}, bf16[640,1408]{1,0:T(8,128)(2,1)S(1)}, u32[]{:S(2)}, u32[]{:S(2)}) collective-permute-start(bf16[640,1408]{1,0:T(8,128)(2,1)S(1)} %last.2.waited_ref), channel_id=1, source_target_pairs={{0,1},{1,0},{2,3},{3,2},{4,5},{5,4},{6,7},{7,6},{8,9},{9,8},{10,11... | collective-permute-start | bytes 5406728 | tf_op jit(solution)/shard_map/ppermute | solution.py:365

commit v4 on v3

--- a/solution.py
+++ b/solution.py
@@ -290,7 +290,7 @@
 def last_call(waited, hidden, da, db, sums, first, rows_in, dtype):
     top, wide = da.shape
     count = hidden.shape[1] // 4
-    rows, tile = hidden.shape[0] // 2, 320
+    rows, tile = hidden.shape[0] // 2, 640
     skip = first // tile
     whole = pl.BlockSpec((top, wide), lambda m: (0, 0))
     extra = [] if rows_in is None else [rows_in]
@@ -348,14 +348,15 @@
     normed = norm_call(outgoing, other_in, target_in, ln_gain)
     upper, lower = halves(normed, up_y, up_x)
     ud_t, ud_b = lax.ppermute(upper, "dp", px), lax.ppermute(lower, "dp", py)
-    d_t, d_b = hold(upper, *cut_down(at, down_target, normed))
+    d_t, d_b = cut_down(at, down_target, normed)
     dx_t, dy_t = both(d_t)
     dx_b, dy_b = both(d_b)
     by_cols = expert_call(
         dispatched, gate_experts, up_experts, down_experts, *in_hbm(upper)
     )
     back = lax.all_to_all(by_cols, ("dp", "expert"), 0, 0, tiled=True)
-    hidden = up_call(by_cols, normed, (up_0, up_x, up_y, ud_t, ud_b))
+    dx_b, dy_t = hold(by_cols, dx_b, dy_t)
+    hidden = up_call(dx_b, normed, (up_0, up_x, up_y, ud_t, ud_b))
     dx_b, dy_t = hold(hidden, dx_b, dy_t)
     dd_t, dd_b = lax.ppermute(dy_t, "dp", px), lax.ppermute(dx_b, "dp", py)
     predicted = mix_call(at, hidden, pred_rows, ids_t, weights_t, back)

time: 98.2 us -> 94.2 us (0.959); the launches traced: 97.7 us -> 92.6 us
  waiting for transfers between devices: 17.7 us -> 11.4 us
  starting transfers between devices: 22.8 us -> 23.8 us
    ppermute x6, waiting for transfers between devices: 15.7 us -> 10.2 us  [both(): return (lax.ppermute(piece, 'dp', px), lax.ppermute(piece, 'dp', py))]
    ppermute x2, starting transfers between devices: 0.89 us -> 2.78 us  [program_square(): dd_t, dd_b = (lax.ppermute(dy_t, 'dp', px), lax.ppermute(dx_b, 'dp', py))]
  transfers between devices with their start and end apart: 14 -> 14, of which waited for: 6 -> 3; matrix products, arithmetic and copies ran while one was open for 0% -> 0% of each run, Pallas kernels for 51% -> 54%
where the time goes in v4:
time: 94.2 us; the launch traced here: 92.6 us
  Pallas kernels  54.2 us (58%)
  starting transfers between devices  23.8 us (25%)
  waiting for transfers between devices  11.4 us (12%)
  other arithmetic  1.61 us (2%)
    pallas_call x1, Pallas kernels, up_call(): pl.pallas_call(up_kernel, out_shape=pltpu.HBM((rows, width), BF), grid=(r...  12.3 us
    pallas_call x1, Pallas kernels, expert_call(): pl.pallas_call(expert_kernel, out_shape=jax.ShapeDtypeStruct(shape, BF),...  11 us
    ppermute x6, waiting for transfers between devices, both(): return (lax.ppermute(piece, 'dp', px), lax.ppermute(piece, 'dp', py))  10.2 us
    pallas_call x1, Pallas kernels, down_call(): pl.pallas_call(down_kernel, out_shape=jax.ShapeDtypeStruct((rows, wide),...  8.71 us
    ppermute x6, starting transfers between devices, both(): return (lax.ppermute(piece, 'dp', px), lax.ppermute(piece, 'dp', py))  8.37 us
    pallas_call x2, Pallas kernels, last_call(): pl.pallas_call(last_kernel, out_shape=jax.ShapeDtypeStruct((rows, wide),...  5.1 us
    all_to_all x1, starting transfers between devices, program_square(): back = lax.all_to_all(by_cols, ('dp', 'expert'), 0, 0, tiled=True)  5.02 us
    pallas_call x1, Pallas kernels, norm_call(): pl.pallas_call(norm_kernel, out_shape=pltpu.HBM((2 * rows, depth), BF), g...  4.89 us
  transfers between devices with their start and end apart: 14, of which 3 were waited for; matrix products, arithmetic and copies ran while one was open for 0% of the time, Pallas kernels for 54%

profile of v4, /device:TPU:0, one launch (start us, length us, event | category | flops | bytes accessed | tf_op | source)
XLA Modules:
  0.0 92.6 jit_solution(4073400294139838514)
XLA Ops:
  0.6 0.5 collective-permute-start
  1.2 0.1 pad_add_fusion.at_ref
  1.2 2.7 %cut_up.1.waited_ref.refs_0_ = bf16[352,1536]{1,0:T(8,128)(2,1)S(1)} custom-call(s32[2]{0:T(128)S(1)} %pad_add_fusion.at_ref, bf16[352,3072]{1,0:T(8,128)(2,1)} %whole_ref.1), custom_call_target="tpu_custom_call" | custom-call | flops 1 | bytes 1 | tf_op jit(solution)/shard_map/cut_up/pallas_call | solution.py:167
  3.9 0.0 copy-start
  4.0 0.0 copy-start.9
  4.0 0.0 copy-start.3
  4.0 2.6 %collective-permute-start.2 = (bf16[352,1536]{1,0:T(8,128)(2,1)S(1)}, bf16[352,1536]{1,0:T(8,128)(2,1)}, u32[]{:S(2)}, u32[]{:S(2)}) collective-permute-start(bf16[352,1536]{1,0:T(8,128)(2,1)S(1)} %cut_up.1.waited_ref.refs_0_), channel_id=1, source_target_pairs={{0,8},{8,0},{16,24},{24,16},{1,9},{9,1},{17,25},{25,17},{2,10},{10... | collective-permute-start | bytes 3244040 | tf_op jit(solution)/shard_map/ppermute | solution.py:340
  6.6 1.5 %collective-permute-start.1 = (bf16[352,1536]{1,0:T(8,128)(2,1)S(1)}, bf16[352,1536]{1,0:T(8,128)(2,1)}, u32[]{:S(2)}, u32[]{:S(2)}) collective-permute-start(bf16[352,1536]{1,0:T(8,128)(2,1)S(1)} %cut_up.1.waited_ref.refs_0_), channel_id=1, source_target_pairs={{0,16},{8,24},{16,0},{24,8},{1,17},{9,25},{17,1},{25,9},{2,18},{10... | collective-permute-start | bytes 3244040 | tf_op jit(solution)/shard_map/ppermute | solution.py:340
  8.1 1.5 %send.1 = bf16[256,1024]{1,0:T(8,128)(2,1)} custom-call(bf16[352,1536]{1,0:T(8,128)(2,1)} %copy-done, s32[2,384]{1,0:T(2,128)S(1)} %bitcast.8, bf16[384,1024]{1,0:T(8,128)(2,1)S(1)} %copy-done.4), custom_call_target="tpu_custom_call" | custom-call | flops 1 | bytes 1 | tf_op jit(solution)/shard_map/send/pallas_call | solution.py:513
  9.6 4.9 %all-to-all-start = ((bf16[8,32,1024]{2,1,0:T(8,128)(2,1)}), bf16[8,32,1024]{2,1,0:T(8,128)(2,1)}, u32[]{:S(2)}, u32[]{:S(2)}) async-start(bf16[8,32,1024]{2,1,0:T(8,128)(2,1)} %bitcast.3.waited_ref), calls=%async_computation | async-start | bytes 1048576 | tf_op jit(solution)/shard_map/all_to_all | solution.py:347
  14.5 0.0 collective-permute-done.other_ref
  14.5 0.0 copy-done.3
  14.5 4.9 %norm.1.waited_ref.refs_0_.x_ref = bf16[1280,1408]{1,0:T(8,128)(2,1)} custom-call(bf16[8,32,1024]{2,1,0:T(8,128)(2,1)} %bitcast.3.waited_ref, bf16[640,1408]{1,0:T(8,128)(2,1)} %collective-permute-done.other_ref, bf16[640,1408]{1,0:T(8,128)(2,1)S(1)} %copy-done.3, f32[1,1408]{1,0:T(1,128)S(1)} %broadcast_in_dim.3.gain_ref), custom_call_target="tpu_custom_call" | custom-call | flops 1 | bytes 1 | tf_op jit(solution)/shard_map/norm/pallas_call | solution.py:143
  19.4 2.8 %cut_down.1 = (bf16[192,1408]{1,0:T(8,128)(2,1)}, bf16[192,1408]{1,0:T(8,128)(2,1)}) custom-call(s32[2]{0:T(128)S(1)} %pad_add_fusion.at_ref, bf16[768,1408]{1,0:T(8,128)(2,1)} %down_ref.1, bf16[1280,1408]{1,0:T(8,128)(2,1)} %norm.1.waited_ref.refs_0_.x_ref), custom_call_target="tpu_custom_call" | custom-call | flops 1 | bytes 1 | tf_op jit(solution)/shard_map/cut_down/pallas_call | solution.py:113
  22.2 0.5 collective-permute-start.3
  22.7 0.5 collective-permute-start.4
  23.2 8.2 %collective-permute-done.2.second_ref.refs_1_ = bf16[352,1536]{1,0:T(8,128)(2,1)} collective-permute-done((bf16[352,1536]{1,0:T(8,128)(2,1)S(1)}, bf16[352,1536]{1,0:T(8,128)(2,1)}, u32[]{:S(2)}, u32[]{:S(2)}) %collective-permute-start.2) | collective-permute-done | bytes 1081376 | tf_op jit(solution)/shard_map/ppermute | solution.py:340
  31.4 2.0 %collective-permute-done.1.first_ref.refs_2_ = bf16[352,1536]{1,0:T(8,128)(2,1)} collective-permute-done((bf16[352,1536]{1,0:T(8,128)(2,1)S(1)}, bf16[352,1536]{1,0:T(8,128)(2,1)}, u32[]{:S(2)}, u32[]{:S(2)}) %collective-permute-start.1) | collective-permute-done | bytes 1081376 | tf_op jit(solution)/shard_map/ppermute | solution.py:340
  33.4 1.3 %halves.1 = (bf16[176,1536]{1,0:T(8,128)(2,1)S(1)}, bf16[176,1536]{1,0:T(8,128)(2,1)S(1)}) custom-call(bf16[1280,1408]{1,0:T(8,128)(2,1)} %norm.1.waited_ref.refs_0_.x_ref, bf16[352,1536]{1,0:T(8,128)(2,1)} %collective-permute-done.1.first_ref.refs_2_, bf16[352,1536]{1,0:T(8,128)(2,1)} %collective-permute-done.2.second_ref.refs_1_), custom_call_target="tpu_custom_call" | custom-call | flops 1 | bytes 1 | tf_op jit(solution)/shard_map/halves/pallas_call | solution.py:63
  34.7 1.6 %collective-permute-start.6 = (bf16[176,1536]{1,0:T(8,128)(2,1)S(1)}, bf16[176,1536]{1,0:T(8,128)(2,1)}, u32[]{:S(2)}, u32[]{:S(2)}) collective-permute-start(bf16[176,1536]{1,0:T(8,128)(2,1)S(1)} %get-tuple-element.14), channel_id=1, source_target_pairs={{0,16},{8,24},{16,0},{24,8},{1,17},{9,25},{17,1},{25,9},{2,18},{10... | collective-permute-start | bytes 1622024 | tf_op jit(solution)/shard_map/ppermute | solution.py:350
  36.3 0.5 collective-permute-start.5
  36.8 0.0 all-to-all-done
  36.8 11.0 %expert.1 = bf16[4,256,256]{2,1,0:T(8,128)(2,1)} custom-call(bf16[256,1024]{1,0:T(8,128)(2,1)} %bitcast.4.x_ref, bf16[1,2816,1024]{2,1,0:T(8,128)(2,1)} %g_ref.1, bf16[1,2816,1024]{2,1,0:T(8,128)(2,1)} %u_ref.1, bf16[1,2816,1024]{2,1,0:T(8,128)(2,1)} %d_ref.1, bf16[176,1536]{1,0:T(8,128)(2,1)} %copy-done.6), custom_call_target="tpu_custom_call" | custom-call | flops 1 | bytes 1 | tf_op jit(solution)/shard_map/expert/pallas_call | solution.py:431
  47.8 5.0 %all-to-all-start.1 = ((bf16[32,32,256]{2,1,0:T(8,128)(2,1)}), bf16[32,32,256]{2,1,0:T(8,128)(2,1)}, u32[]{:S(2)}, u32[]{:S(2)}) async-start(bf16[32,32,256]{2,1,0:T(8,128)(2,1)} %bitcast.5.refs_0_), calls=%async_computation.1 | async-start | bytes 1048576 | tf_op jit(solution)/shard_map/all_to_all | solution.py:357
  52.9 1.8 %collective-permute-start.10 = (bf16[192,1408]{1,0:T(8,128)(2,1)}, bf16[192,1408]{1,0:T(8,128)(2,1)}, u32[]{:S(2)}, u32[]{:S(2)}) collective-permute-start(bf16[192,1408]{1,0:T(8,128)(2,1)} %get-tuple-element.11.refs_1_), channel_id=1, source_target_pairs={{0,16},{8,24},{16,0},{24,8},{1,17},{9,25},{17,1},{25,9},{2,18},{10... | collective-permute-start | bytes 1622024 | tf_op jit(solution)/shard_map/ppermute | solution.py:340
  54.6 0.0 collective-permute-done.3.refs_1_
  54.6 1.5 %collective-permute-start.9 = (bf16[192,1408]{1,0:T(8,128)(2,1)}, bf16[192,1408]{1,0:T(8,128)(2,1)}, u32[]{:S(2)}, u32[]{:S(2)}) collective-permute-start(bf16[192,1408]{1,0:T(8,128)(2,1)} %get-tuple-element.12.refs_0_), channel_id=1, source_target_pairs={{0,8},{8,0},{16,24},{24,16},{1,9},{9,1},{17,25},{25,17},{2,10},{10... | collective-permute-start | bytes 1622024 | tf_op jit(solution)/shard_map/ppermute | solution.py:340
  56.1 0.0 collective-permute-done.4.refs_2_
  56.1 0.8 copy-done.1
  56.9 0.0 collective-permute-done.6.refs_4_
  56.9 0.0 collective-permute-done.5.refs_3_
  56.9 12.3 %up.1.waited_ref.refs_0_.h_ref = bf16[1280,1536]{1,0:T(8,128)(2,1)} custom-call(bf16[192,1408]{1,0:T(8,128)(2,1)} %copy-done.1, bf16[1280,1408]{1,0:T(8,128)(2,1)} %norm.1.waited_ref.refs_0_.x_ref, bf16[352,1536]{1,0:T(8,128)(2,1)} %copy-done, bf16[352,1536]{1,0:T(8,128)(2,1)} %collective-permute-done.2.second_ref.refs_1_, ...), custom_call_target="tpu_custom_call" | custom-call | flops 1 | bytes 1 | tf_op jit(solution)/shard_map/up/pallas_call | solution.py:225
  69.2 0.0 copy-start.5
  69.2 0.0 copy-start.8
  69.2 0.6 collective-permute-start.7
  69.9 2.1 %collective-permute-start.8 = (bf16[192,1408]{1,0:T(8,128)(2,1)S(1)}, bf16[192,1408]{1,0:T(8,128)(2,1)}, u32[]{:S(2)}, u32[]{:S(2)}) collective-permute-start(bf16[192,1408]{1,0:T(8,128)(2,1)S(1)} %get-tuple-element.17.refs_3_), channel_id=1, source_target_pairs={{0,16},{8,24},{16,0},{24,8},{1,17},{9,25},{17,1},{25,9},{2,18},{10... | collective-permute-start | bytes 1622024 | tf_op jit(solution)/shard_map/ppermute | solution.py:361
  72.0 0.0 all-to-all-done.1
  72.0 4.0 %mix.1.waited_ref = bf16[384,256]{1,0:T(8,128)(2,1)} custom-call(s32[2]{0:T(128)S(1)} %pad_add_fusion.at_ref, bf16[1280,1536]{1,0:T(8,128)(2,1)} %up.1.waited_ref.refs_0_.h_ref, s32[2,384]{1,0:T(2,128)S(1)} %bitcast.9, f32[2,384]{1,0:T(2,128)S(1)} %bitcast.10, bf16[1024,256]{1,0:T(8,128)(2,1)} %bitcast.7.back_ref, bf16[384,1024]{1,0:T(8,128)(2,1)S(1)} %copy-done.5), custom_call_target="tpu_custom_call" | custom-call | flops 1 | bytes 1 | tf_op jit(solution)/shard_map/mix/pallas_call | solution.py:546
  76.0 0.0 collective-permute-done.10.refs_5_
  76.0 0.0 collective-permute-done.9.refs_2_
  76.0 8.7 %down.1.sum_ref = f32[1280,1408]{1,0:T(8,128)S(1)} custom-call(bf16[384,256]{1,0:T(8,128)(2,1)} %mix.1.waited_ref, bf16[1280,1536]{1,0:T(8,128)(2,1)} %up.1.waited_ref.refs_0_.h_ref, bf16[192,1408]{1,0:T(8,128)(2,1)} %get-tuple-element.12.refs_0_, bf16[192,1408]{1,0:T(8,128)(2,1)} %get-tuple-element.11.refs_1_, ...), custom_call_target="tpu_custom_call" | custom-call | flops 1 | bytes 1 | tf_op jit(solution)/shard_map/down/pallas_call | solution.py:264
  84.7 0.0 collective-permute-done.7.da
  84.7 0.0 collective-permute-done.8.db
  84.7 2.5 %last.2.waited_ref = bf16[640,1408]{1,0:T(8,128)(2,1)S(1)} custom-call(bf16[384,256]{1,0:T(8,128)(2,1)} %mix.1.waited_ref, bf16[1280,1536]{1,0:T(8,128)(2,1)} %up.1.waited_ref.refs_0_.h_ref, bf16[192,1408]{1,0:T(8,128)(2,1)} %collective-permute-done.7.da, bf16[192,1408]{1,0:T(8,128)(2,1)} %collective-permute-done.8.db, f32[1280,1408]{1,0:T(8,128)S(1)} %down.1.sum_ref), custom_call_target="tpu_custom_call" | custom-call | flops 1 | bytes 1 | tf_op jit(solution)/shard_map/last/pallas_call | solution.py:297
  87.3 0.1 collective-permute-start.11
  87.4 2.6 %last.3 = f32[640,1408]{1,0:T(8,128)S(1)} custom-call(bf16[640,1408]{1,0:T(8,128)(2,1)S(1)} %last.2.waited_ref, bf16[1280,1536]{1,0:T(8,128)(2,1)} %up.1.waited_ref.refs_0_.h_ref, bf16[192,1408]{1,0:T(8,128)(2,1)} %collective-permute-done.7.da, bf16[192,1408]{1,0:T(8,128)(2,1)} %collective-permute-done.8.db, f32[1280,1408]{1,0:T(8,128)S(1)} %down.1.sum_ref, ...), custom_call_target="tpu_custom_call" | custom-call | flops 1 | bytes 1 | tf_op jit(solution)/shard_map/last/pallas_call | solution.py:297
  89.9 1.2 %collective-permute-done.11 = bf16[640,1408]{1,0:T(8,128)(2,1)S(1)} collective-permute-done((bf16[640,1408]{1,0:T(8,128)(2,1)S(1)}, bf16[640,1408]{1,0:T(8,128)(2,1)S(1)}, u32[]{:S(2)}, u32[]{:S(2)}) %collective-permute-start.11) | collective-permute-done | bytes 1802272 | tf_op jit(solution)/shard_map/ppermute | solution.py:366
  91.1 1.5 %add_convert_fusion = bf16[640,1408]{1,0:T(8,128)(2,1)} fusion(f32[640,1408]{1,0:T(8,128)S(1)} %last.3, bf16[640,1408]{1,0:T(8,128)(2,1)S(1)} %collective-permute-done.11), kind=kLoop, calls=%fused_computation | loop fusion | flops 2703360 | bytes 7208960 | tf_op jit(solution)/shard_map/convert_element_type | solution.py:368
  (16 shorter events, 0.0 us)
Async XLA Ops:
  0.6 7.5 %copy-start.7 = (s32[384,2]{0,1:T(2,128)S(1)}, s32[384,2]{0,1:T(2,128)}, u32[]{:S(2)}) copy-start(s32[384,2]{0,1:T(2,128)} %param.15) | copy-start | bytes 9220
  0.6 13.8 %collective-permute-start = (bf16[640,1408]{1,0:T(8,128)(2,1)}, bf16[640,1408]{1,0:T(8,128)(2,1)}, u32[]{:S(2)}, u32[]{:S(2)}) collective-permute-start(bf16[640,1408]{1,0:T(8,128)(2,1)} %refs_0_.1), channel_id=1, source_target_pairs={{0,1},{1,0},{2,3},{3,2},{4,5},{5,4},{6,7},{7,6},{8,9},{9,8},{10,11... | collective-permute-start | bytes 5406728 | tf_op jit(solution)/shard_map/ppermute | solution.py:345
  1.2 6.9 %copy-start.4 = (bf16[384,1024]{1,0:T(8,128)(2,1)S(1)}, bf16[384,1024]{1,0:T(8,128)(2,1)}, u32[]{:S(2)}) copy-start(bf16[384,1024]{1,0:T(8,128)(2,1)} %pred_ref.1) | copy-start | bytes 2359300
  3.9 4.1 %copy-start = (bf16[352,1536]{1,0:T(8,128)(2,1)}, bf16[352,1536]{1,0:T(8,128)(2,1)S(1)}, u32[]{:S(2)}) copy-start(bf16[352,1536]{1,0:T(8,128)(2,1)S(1)} %cut_up.1.waited_ref.refs_0_) | copy-start | bytes 3244036
  4.0 10.5 %copy-start.9 = (f32[1408]{0:T(1024)S(1)}, f32[1408]{0:T(1024)}, u32[]{:S(2)}) copy-start(f32[1408]{0:T(1024)} %param.11) | copy-start | bytes 16900
  4.0 10.5 %copy-start.3 = (bf16[640,1408]{1,0:T(8,128)(2,1)S(1)}, bf16[640,1408]{1,0:T(8,128)(2,1)}, u32[]{:S(2)}) copy-start(bf16[640,1408]{1,0:T(8,128)(2,1)} %refs_0_.1) | copy-start | bytes 5406724
  4.0 27.4 %collective-permute-start.2 = (bf16[352,1536]{1,0:T(8,128)(2,1)S(1)}, bf16[352,1536]{1,0:T(8,128)(2,1)}, u32[]{:S(2)}, u32[]{:S(2)}) collective-permute-start(bf16[352,1536]{1,0:T(8,128)(2,1)S(1)} %cut_up.1.waited_ref.refs_0_), channel_id=1, source_target_pairs={{0,8},{8,0},{16,24},{24,16},{1,9},{9,1},{17,25},{25,17},{2,10},{10... | collective-permute-start | bytes 3244040 | tf_op jit(solution)/shard_map/ppermute | solution.py:340
  6.6 26.8 %collective-permute-start.1 = (bf16[352,1536]{1,0:T(8,128)(2,1)S(1)}, bf16[352,1536]{1,0:T(8,128)(2,1)}, u32[]{:S(2)}, u32[]{:S(2)}) collective-permute-start(bf16[352,1536]{1,0:T(8,128)(2,1)S(1)} %cut_up.1.waited_ref.refs_0_), channel_id=1, source_target_pairs={{0,16},{8,24},{16,0},{24,8},{1,17},{9,25},{17,1},{25,9},{2,18},{10... | collective-permute-start | bytes 3244040 | tf_op jit(solution)/shard_map/ppermute | solution.py:340
  9.6 27.2 %all-to-all-start = ((bf16[8,32,1024]{2,1,0:T(8,128)(2,1)}), bf16[8,32,1024]{2,1,0:T(8,128)(2,1)}, u32[]{:S(2)}, u32[]{:S(2)}) async-start(bf16[8,32,1024]{2,1,0:T(8,128)(2,1)} %bitcast.3.waited_ref), calls=%async_computation | async-start | bytes 1048576 | tf_op jit(solution)/shard_map/all_to_all | solution.py:347
  22.2 32.5 %collective-permute-start.3 = (bf16[192,1408]{1,0:T(8,128)(2,1)}, bf16[192,1408]{1,0:T(8,128)(2,1)S(1)}, u32[]{:S(2)}, u32[]{:S(2)}) collective-permute-start(bf16[192,1408]{1,0:T(8,128)(2,1)} %get-tuple-element.11.refs_1_), channel_id=1, source_target_pairs={{0,8},{8,0},{16,24},{24,16},{1,9},{9,1},{17,25},{25,17},{2,10},{10... | collective-permute-start | bytes 1622024 | tf_op jit(solution)/shard_map/ppermute | solution.py:340
  22.7 33.4 %collective-permute-start.4 = (bf16[192,1408]{1,0:T(8,128)(2,1)}, bf16[192,1408]{1,0:T(8,128)(2,1)}, u32[]{:S(2)}, u32[]{:S(2)}) collective-permute-start(bf16[192,1408]{1,0:T(8,128)(2,1)} %get-tuple-element.12.refs_0_), channel_id=1, source_target_pairs={{0,16},{8,24},{16,0},{24,8},{1,17},{9,25},{17,1},{25,9},{2,18},{10... | collective-permute-start | bytes 1622024 | tf_op jit(solution)/shard_map/ppermute | solution.py:340
  34.7 2.1 %copy-start.6 = (bf16[176,1536]{1,0:T(8,128)(2,1)}, bf16[176,1536]{1,0:T(8,128)(2,1)S(1)}, u32[]{:S(2)}) copy-start(bf16[176,1536]{1,0:T(8,128)(2,1)S(1)} %get-tuple-element.10.refs_0_) | copy-start | bytes 1622020
  34.7 22.2 %collective-permute-start.6 = (bf16[176,1536]{1,0:T(8,128)(2,1)S(1)}, bf16[176,1536]{1,0:T(8,128)(2,1)}, u32[]{:S(2)}, u32[]{:S(2)}) collective-permute-start(bf16[176,1536]{1,0:T(8,128)(2,1)S(1)} %get-tuple-element.14), channel_id=1, source_target_pairs={{0,16},{8,24},{16,0},{24,8},{1,17},{9,25},{17,1},{25,9},{2,18},{10... | collective-permute-start | bytes 1622024 | tf_op jit(solution)/shard_map/ppermute | solution.py:350
  36.3 20.6 %collective-permute-start.5 = (bf16[176,1536]{1,0:T(8,128)(2,1)S(1)}, bf16[176,1536]{1,0:T(8,128)(2,1)}, u32[]{:S(2)}, u32[]{:S(2)}) collective-permute-start(bf16[176,1536]{1,0:T(8,128)(2,1)S(1)} %get-tuple-element.10.refs_0_), channel_id=1, source_target_pairs={{0,8},{8,0},{16,24},{24,16},{1,9},{9,1},{17,25},{25,17},{2,10},{10... | collective-permute-start | bytes 1622024 | tf_op jit(solution)/shard_map/ppermute | solution.py:350
  47.8 24.2 %all-to-all-start.1 = ((bf16[32,32,256]{2,1,0:T(8,128)(2,1)}), bf16[32,32,256]{2,1,0:T(8,128)(2,1)}, u32[]{:S(2)}, u32[]{:S(2)}) async-start(bf16[32,32,256]{2,1,0:T(8,128)(2,1)} %bitcast.5.refs_0_), calls=%async_computation.1 | async-start | bytes 1048576 | tf_op jit(solution)/shard_map/all_to_all | solution.py:357
  52.9 23.1 %collective-permute-start.10 = (bf16[192,1408]{1,0:T(8,128)(2,1)}, bf16[192,1408]{1,0:T(8,128)(2,1)}, u32[]{:S(2)}, u32[]{:S(2)}) collective-permute-start(bf16[192,1408]{1,0:T(8,128)(2,1)} %get-tuple-element.11.refs_1_), channel_id=1, source_target_pairs={{0,16},{8,24},{16,0},{24,8},{1,17},{9,25},{17,1},{25,9},{2,18},{10... | collective-permute-start | bytes 1622024 | tf_op jit(solution)/shard_map/ppermute | solution.py:340
  54.6 21.4 %collective-permute-start.9 = (bf16[192,1408]{1,0:T(8,128)(2,1)}, bf16[192,1408]{1,0:T(8,128)(2,1)}, u32[]{:S(2)}, u32[]{:S(2)}) collective-permute-start(bf16[192,1408]{1,0:T(8,128)(2,1)} %get-tuple-element.12.refs_0_), channel_id=1, source_target_pairs={{0,8},{8,0},{16,24},{24,16},{1,9},{9,1},{17,25},{25,17},{2,10},{10... | collective-permute-start | bytes 1622024 | tf_op jit(solution)/shard_map/ppermute | solution.py:340
  56.1 0.8 copy-start.1
  56.9 12.3 %copy-start.2 = (bf16[192,1408]{1,0:T(8,128)(2,1)S(1)}, bf16[192,1408]{1,0:T(8,128)(2,1)}, u32[]{:S(2)}) copy-start(bf16[192,1408]{1,0:T(8,128)(2,1)} %copy-done.1) | copy-start | bytes 1622020
  69.2 2.8 %copy-start.5 = (bf16[384,1024]{1,0:T(8,128)(2,1)S(1)}, bf16[384,1024]{1,0:T(8,128)(2,1)}, u32[]{:S(2)}) copy-start(bf16[384,1024]{1,0:T(8,128)(2,1)} %pred_ref.1) | copy-start | bytes 2359300
  69.2 2.8 %copy-start.8 = (f32[384,2]{0,1:T(2,128)S(1)}, f32[384,2]{0,1:T(2,128)}, u32[]{:S(2)}) copy-start(f32[384,2]{0,1:T(2,128)} %param.16) | copy-start | bytes 9220
  69.2 15.5 %collective-permute-start.7 = (bf16[192,1408]{1,0:T(8,128)(2,1)}, bf16[192,1408]{1,0:T(8,128)(2,1)}, u32[]{:S(2)}, u32[]{:S(2)}) collective-permute-start(bf16[192,1408]{1,0:T(8,128)(2,1)} %get-tuple-element.16.refs_4_), channel_id=1, source_target_pairs={{0,8},{8,0},{16,24},{24,16},{1,9},{9,1},{17,25},{25,17},{2,10},{10... | collective-permute-start | bytes 1622024 | tf_op jit(solution)/shard_map/ppermute | solution.py:361
  69.9 14.9 %collective-permute-start.8 = (bf16[192,1408]{1,0:T(8,128)(2,1)S(1)}, bf16[192,1408]{1,0:T(8,128)(2,1)}, u32[]{:S(2)}, u32[]{:S(2)}) collective-permute-start(bf16[192,1408]{1,0:T(8,128)(2,1)S(1)} %get-tuple-element.17.refs_3_), channel_id=1, source_target_pairs={{0,16},{8,24},{16,0},{24,8},{1,17},{9,25},{17,1},{25,9},{2,18},{10... | collective-permute-start | bytes 1622024 | tf_op jit(solution)/shard_map/ppermute | solution.py:361
  87.3 3.8 %collective-permute-start.11 = (bf16[640,1408]{1,0:T(8,128)(2,1)S(1)}, bf16[640,1408]{1,0:T(8,128)(2,1)S(1)}, u32[]{:S(2)}, u32[]{:S(2)}) collective-permute-start(bf16[640,1408]{1,0:T(8,128)(2,1)S(1)} %last.2.waited_ref), channel_id=1, source_target_pairs={{0,1},{1,0},{2,3},{3,2},{4,5},{5,4},{6,7},{7,6},{8,9},{9,8},{10,11... | collective-permute-start | bytes 5406728 | tf_op jit(solution)/shard_map/ppermute | solution.py:366

commit v5 on v4

--- a/solution.py
+++ b/solution.py
@@ -346,9 +346,11 @@
     outgoing = send_call(up_0, pred_rows, ids_t)
     dispatched = lax.all_to_all(outgoing, "expert", 0, 0, tiled=True)
     normed = norm_call(outgoing, other_in, target_in, ln_gain)
-    upper, lower = halves(normed, up_y, up_x)
+    d_t, d_b = cut_down(at, down_target, normed)
+    n_slots = EXP_DEV * lax.axis_size("expert") * CAP
+    high, low = plan_call(d_t, ids_t, weights_t, n_slots)
+    upper, lower = halves(high, up_y, up_x)
     ud_t, ud_b = lax.ppermute(upper, "dp", px), lax.ppermute(lower, "dp", py)
-    d_t, d_b = cut_down(at, down_target, normed)
     dx_t, dy_t = both(d_t)
     dx_b, dy_b = both(d_b)
     by_cols = expert_call(
@@ -359,7 +361,7 @@
     hidden = up_call(dx_b, normed, (up_0, up_x, up_y, ud_t, ud_b))
     dx_b, dy_t = hold(hidden, dx_b, dy_t)
     dd_t, dd_b = lax.ppermute(dy_t, "dp", px), lax.ppermute(dx_b, "dp", py)
-    predicted = mix_call(at, hidden, pred_rows, ids_t, weights_t, back)
+    predicted = mix_call(at, hidden, pred_rows, high, low, back)
     sums = down_call(predicted, hidden, (d_t, d_b, dx_t, dx_b, dy_t, dy_b))
     rows = target_in.shape[0]
     other_sum = last_call(*in_hbm(predicted), hidden, dd_t, dd_b, sums, 0, None, BF)
@@ -522,24 +524,41 @@
     return out.reshape(owners, CAP, width)
 
 
-def mix_kernel(at_ref, waited_ref, ids_ref, weights_ref, back_ref, pred_ref, out_ref):
-    n_all = back_ref.shape[0] // CAP
+def plan_kernel(waited_ref, ids_ref, weights_ref, high_ref, low_ref):
+    n_all = high_ref.shape[1] // CAP
     hits, spread, hit = slot_rows_of(ids_ref, 0, n_all)
     weight = 0.0
     for k in range(TOP):
         weight = weight + jnp.where(hits[k], weights_ref[k : k + 1, :], 0.0)
     high = weight.astype(BF)
     low = (weight - high.astype(F32)).astype(BF)
+    for part, ref in ((high, high_ref), (low, low_ref)):
+        ref[...] = jnp.where(hit, dot(spread, part), 0.0).T.astype(BF)
+
+
+def plan_call(waited, ids_t, weights_t, n_slots):
+    rows = ids_t.shape[1]
+    vmem = pl.BlockSpec(memory_space=pltpu.VMEM)
+    part = pltpu.HBM((rows, n_slots), BF)
+    return pl.pallas_call(
+        plan_kernel,
+        out_shape=(part, part),
+        in_specs=[ANYWHERE, vmem, vmem],
+        out_specs=(vmem, vmem),
+        compiler_params=pltpu.CompilerParams(vmem_limit_bytes=24 * 2**20),
+        cost_estimate=pl.CostEstimate(flops=1, bytes_accessed=1, transcendentals=0),
+        name="plan",
+    )(*in_hbm(waited), ids_t, weights_t)
+
+
+def mix_kernel(at_ref, waited_ref, high_ref, low_ref, back_ref, pred_ref, out_ref):
     total = pred_ref[...].astype(F32)
-    for part in (high, low):
-        mix = jnp.where(hit, dot(spread, part), 0.0).astype(BF)
-        total = total + lax.dot_general(
-            mix, back_ref[...], (((0,), (0,)), ((), ())), preferred_element_type=F32
-        )
+    for ref in (high_ref, low_ref):
+        total = total + dot(ref[...], back_ref[...])
     out_ref[...] = total.astype(BF)
 
 
-def mix_call(at, waited, pred_rows, ids_t, weights_t, back):
+def mix_call(at, waited, pred_rows, high, low, back):
     rows, width = pred_rows.shape
     blocks, cap, share = back.shape
     whole = lambda shape: pl.BlockSpec(shape, lambda i, at: (0, 0))
@@ -551,8 +570,8 @@
             grid=(1,),
             in_specs=[
                 ANYWHERE,
-                whole((TOP, rows)),
-                whole((TOP, rows)),
+                whole((rows, blocks * cap)),
+                whole((rows, blocks * cap)),
                 whole((blocks * cap, share)),
                 pl.BlockSpec((rows, share), lambda i, at: (0, at[0])),
             ],
@@ -561,7 +580,9 @@
         compiler_params=pltpu.CompilerParams(vmem_limit_bytes=16 * 2**20),
         cost_estimate=pl.CostEstimate(flops=1, bytes_accessed=1, transcendentals=0),
         name="mix",
-    )(at, *in_hbm(waited), ids_t, weights_t, back.reshape(blocks * cap, share), pred_rows)
+    )(
+        at, *in_hbm(waited, high, low), back.reshape(blocks * cap, share), pred_rows
+    )
 
 
 def program_any(

time: 94.2 us -> 93.5 us (level)
  Pallas kernels: 54.2 us -> 55.8 us
  waiting for transfers between devices: 11.4 us -> 9.88 us
    ppermute x6, waiting for transfers between devices: 10.2 us -> 8.01 us  [both(): return (lax.ppermute(piece, 'dp', px), lax.ppermute(piece, 'dp', py))]
    pallas_call x0 -> x1, Pallas kernels: none -> 2.09 us  [plan_call(): pl.pallas_call(plan_kernel, out_shape=(part, part), in_specs=[ANYWHERE, v...]
  transfers between devices with their start and end apart: 14 -> 14, of which waited for: 3 -> 5; matrix products, arithmetic and copies ran while one was open for 0% -> 0% of each run, Pallas kernels for 54% -> 56%
where the time goes in v5:
time: 93.5 us; the launch traced here: 92.5 us
  Pallas kernels  55.8 us (60%)
  starting transfers between devices  23.5 us (25%)
  waiting for transfers between devices  9.88 us (11%)
  other arithmetic  1.61 us (2%)
    pallas_call x1, Pallas kernels, up_call(): pl.pallas_call(up_kernel, out_shape=pltpu.HBM((rows, width), BF), grid=(r...  12.3 us
    pallas_call x1, Pallas kernels, expert_call(): pl.pallas_call(expert_kernel, out_shape=jax.ShapeDtypeStruct(shape, BF),...  11.1 us
    pallas_call x1, Pallas kernels, down_call(): pl.pallas_call(down_kernel, out_shape=jax.ShapeDtypeStruct((rows, wide),...  8.71 us
    ppermute x6, starting transfers between devices, both(): return (lax.ppermute(piece, 'dp', px), lax.ppermute(piece, 'dp', py))  8.37 us
    ppermute x6, waiting for transfers between devices, both(): return (lax.ppermute(piece, 'dp', px), lax.ppermute(piece, 'dp', py))  8.01 us
    pallas_call x2, Pallas kernels, last_call(): pl.pallas_call(last_kernel, out_shape=jax.ShapeDtypeStruct((rows, wide),...  5.1 us
    all_to_all x1, starting transfers between devices, program_square(): back = lax.all_to_all(by_cols, ('dp', 'expert'), 0, 0, tiled=True)  5.02 us
    pallas_call x1, Pallas kernels, norm_call(): pl.pallas_call(norm_kernel, out_shape=pltpu.HBM((2 * rows, depth), BF), g...  4.9 us
  transfers between devices with their start and end apart: 14, of which 5 were waited for; matrix products, arithmetic and copies ran while one was open for 0% of the time, Pallas kernels for 56%

profile of v5, /device:TPU:0, one launch (start us, length us, event | category | flops | bytes accessed | tf_op | source)
XLA Modules:
  0.0 92.5 jit_solution(15749668606052822952)
XLA Ops:
  0.6 0.0 copy-start.7
  0.6 0.5 collective-permute-start
  1.2 0.1 pad_add_fusion.at_ref
  1.2 2.7 %cut_up.1.waited_ref.refs_0_ = bf16[352,1536]{1,0:T(8,128)(2,1)S(1)} custom-call(s32[2]{0:T(128)S(1)} %pad_add_fusion.at_ref, bf16[352,3072]{1,0:T(8,128)(2,1)} %whole_ref.1), custom_call_target="tpu_custom_call" | custom-call | flops 1 | bytes 1 | tf_op jit(solution)/shard_map/cut_up/pallas_call | solution.py:167
  3.9 0.0 copy-start
  4.0 0.0 copy-start.9
  4.0 0.0 copy-start.3
  4.0 2.6 %collective-permute-start.2 = (bf16[352,1536]{1,0:T(8,128)(2,1)S(1)}, bf16[352,1536]{1,0:T(8,128)(2,1)}, u32[]{:S(2)}, u32[]{:S(2)}) collective-permute-start(bf16[352,1536]{1,0:T(8,128)(2,1)S(1)} %cut_up.1.waited_ref.refs_0_), channel_id=1, source_target_pairs={{0,8},{8,0},{16,24},{24,16},{1,9},{9,1},{17,25},{25,17},{2,10},{10... | collective-permute-start | bytes 3244040 | tf_op jit(solution)/shard_map/ppermute | solution.py:340
  6.6 1.5 %collective-permute-start.1 = (bf16[352,1536]{1,0:T(8,128)(2,1)S(1)}, bf16[352,1536]{1,0:T(8,128)(2,1)}, u32[]{:S(2)}, u32[]{:S(2)}) collective-permute-start(bf16[352,1536]{1,0:T(8,128)(2,1)S(1)} %cut_up.1.waited_ref.refs_0_), channel_id=1, source_target_pairs={{0,16},{8,24},{16,0},{24,8},{1,17},{9,25},{17,1},{25,9},{2,18},{10... | collective-permute-start | bytes 3244040 | tf_op jit(solution)/shard_map/ppermute | solution.py:340
  8.1 1.5 %send.1 = bf16[256,1024]{1,0:T(8,128)(2,1)} custom-call(bf16[352,1536]{1,0:T(8,128)(2,1)} %copy-done, s32[2,384]{1,0:T(2,128)S(1)} %bitcast.8, bf16[384,1024]{1,0:T(8,128)(2,1)S(1)} %copy-done.4), custom_call_target="tpu_custom_call" | custom-call | flops 1 | bytes 1 | tf_op jit(solution)/shard_map/send/pallas_call | solution.py:515
  9.6 4.9 %all-to-all-start = ((bf16[8,32,1024]{2,1,0:T(8,128)(2,1)}), bf16[8,32,1024]{2,1,0:T(8,128)(2,1)}, u32[]{:S(2)}, u32[]{:S(2)}) async-start(bf16[8,32,1024]{2,1,0:T(8,128)(2,1)} %bitcast.3.waited_ref), calls=%async_computation | async-start | bytes 1048576 | tf_op jit(solution)/shard_map/all_to_all | solution.py:347
  14.5 0.0 collective-permute-done.other_ref
  14.5 4.9 %norm.1.refs_0_.x_ref = bf16[1280,1408]{1,0:T(8,128)(2,1)} custom-call(bf16[8,32,1024]{2,1,0:T(8,128)(2,1)} %bitcast.3.waited_ref, bf16[640,1408]{1,0:T(8,128)(2,1)} %collective-permute-done.other_ref, bf16[640,1408]{1,0:T(8,128)(2,1)S(1)} %copy-done.3, f32[1,1408]{1,0:T(1,128)S(1)} %broadcast_in_dim.3.gain_ref), custom_call_target="tpu_custom_call" | custom-call | flops 1 | bytes 1 | tf_op jit(solution)/shard_map/norm/pallas_call | solution.py:143
  19.4 2.8 %cut_down.1 = (bf16[192,1408]{1,0:T(8,128)(2,1)}, bf16[192,1408]{1,0:T(8,128)(2,1)}) custom-call(s32[2]{0:T(128)S(1)} %pad_add_fusion.at_ref, bf16[768,1408]{1,0:T(8,128)(2,1)} %down_ref.1, bf16[1280,1408]{1,0:T(8,128)(2,1)} %norm.1.refs_0_.x_ref), custom_call_target="tpu_custom_call" | custom-call | flops 1 | bytes 1 | tf_op jit(solution)/shard_map/cut_down/pallas_call | solution.py:113
  22.2 0.5 collective-permute-start.3
  22.8 0.5 collective-permute-start.4
  23.3 2.1 %plan.1 = (bf16[384,1024]{1,0:T(8,128)(2,1)}, bf16[384,1024]{1,0:T(8,128)(2,1)}) custom-call(bf16[192,1408]{1,0:T(8,128)(2,1)} %get-tuple-element.12.waited_ref.refs_0_, s32[2,384]{1,0:T(2,128)S(1)} %bitcast.9, f32[2,384]{1,0:T(2,128)S(1)} %bitcast.10), custom_call_target="tpu_custom_call" | custom-call | flops 1 | bytes 1 | tf_op jit(solution)/shard_map/plan/pallas_call | solution.py:543
  25.4 6.0 %collective-permute-done.2.second_ref.refs_1_ = bf16[352,1536]{1,0:T(8,128)(2,1)} collective-permute-done((bf16[352,1536]{1,0:T(8,128)(2,1)S(1)}, bf16[352,1536]{1,0:T(8,128)(2,1)}, u32[]{:S(2)}, u32[]{:S(2)}) %collective-permute-start.2) | collective-permute-done | bytes 1081376 | tf_op jit(solution)/shard_map/ppermute | solution.py:340
  31.4 2.0 %collective-permute-done.1.first_ref.refs_2_ = bf16[352,1536]{1,0:T(8,128)(2,1)} collective-permute-done((bf16[352,1536]{1,0:T(8,128)(2,1)S(1)}, bf16[352,1536]{1,0:T(8,128)(2,1)}, u32[]{:S(2)}, u32[]{:S(2)}) %collective-permute-start.1) | collective-permute-done | bytes 1081376 | tf_op jit(solution)/shard_map/ppermute | solution.py:340
  33.4 1.3 %halves.1 = (bf16[176,1536]{1,0:T(8,128)(2,1)S(1)}, bf16[176,1536]{1,0:T(8,128)(2,1)S(1)}) custom-call(bf16[384,1024]{1,0:T(8,128)(2,1)} %get-tuple-element.13.waited_ref.high_ref, bf16[352,1536]{1,0:T(8,128)(2,1)} %collective-permute-done.1.first_ref.refs_2_, bf16[352,1536]{1,0:T(8,128)(2,1)} %collective-permute-done.2.second_ref.refs_1_), custom_call_target="tpu_custom_call" | custom-call | flops 1 | bytes 1 | tf_op jit(solution)/shard_map/halves/pallas_call | solution.py:63
  34.7 1.6 %collective-permute-start.6 = (bf16[176,1536]{1,0:T(8,128)(2,1)S(1)}, bf16[176,1536]{1,0:T(8,128)(2,1)}, u32[]{:S(2)}, u32[]{:S(2)}) collective-permute-start(bf16[176,1536]{1,0:T(8,128)(2,1)S(1)} %get-tuple-element.17), channel_id=1, source_target_pairs={{0,16},{8,24},{16,0},{24,8},{1,17},{9,25},{17,1},{25,9},{2,18},{10... | collective-permute-start | bytes 1622024 | tf_op jit(solution)/shard_map/ppermute | solution.py:353
  36.3 0.5 collective-permute-start.5
  36.8 0.0 all-to-all-done
  36.8 11.1 %expert.1 = bf16[4,256,256]{2,1,0:T(8,128)(2,1)} custom-call(bf16[256,1024]{1,0:T(8,128)(2,1)} %bitcast.4.x_ref, bf16[1,2816,1024]{2,1,0:T(8,128)(2,1)} %g_ref.1, bf16[1,2816,1024]{2,1,0:T(8,128)(2,1)} %u_ref.1, bf16[1,2816,1024]{2,1,0:T(8,128)(2,1)} %d_ref.1, bf16[176,1536]{1,0:T(8,128)(2,1)} %copy-done.6), custom_call_target="tpu_custom_call" | custom-call | flops 1 | bytes 1 | tf_op jit(solution)/shard_map/expert/pallas_call | solution.py:433
  47.9 5.0 %all-to-all-start.1 = ((bf16[32,32,256]{2,1,0:T(8,128)(2,1)}), bf16[32,32,256]{2,1,0:T(8,128)(2,1)}, u32[]{:S(2)}, u32[]{:S(2)}) async-start(bf16[32,32,256]{2,1,0:T(8,128)(2,1)} %bitcast.6.refs_0_), calls=%async_computation.1 | async-start | bytes 1048576 | tf_op jit(solution)/shard_map/all_to_all | solution.py:359
  52.9 1.8 %collective-permute-start.10 = (bf16[192,1408]{1,0:T(8,128)(2,1)}, bf16[192,1408]{1,0:T(8,128)(2,1)}, u32[]{:S(2)}, u32[]{:S(2)}) collective-permute-start(bf16[192,1408]{1,0:T(8,128)(2,1)} %get-tuple-element.15.refs_1_), channel_id=1, source_target_pairs={{0,16},{8,24},{16,0},{24,8},{1,17},{9,25},{17,1},{25,9},{2,18},{10... | collective-permute-start | bytes 1622024 | tf_op jit(solution)/shard_map/ppermute | solution.py:340
  54.7 0.0 collective-permute-done.3.refs_1_
  54.7 1.5 %collective-permute-start.9 = (bf16[192,1408]{1,0:T(8,128)(2,1)}, bf16[192,1408]{1,0:T(8,128)(2,1)}, u32[]{:S(2)}, u32[]{:S(2)}) collective-permute-start(bf16[192,1408]{1,0:T(8,128)(2,1)} %get-tuple-element.12.waited_ref.refs_0_), channel_id=1, source_target_pairs={{0,8},{8,0},{16,24},{24,16},{1,9},{9,1},{17,25},{25,17},{2,10},{10... | collective-permute-start | bytes 1622024 | tf_op jit(solution)/shard_map/ppermute | solution.py:340
  56.1 0.0 collective-permute-done.4.refs_2_
  56.1 0.8 copy-done.1
  57.0 0.0 collective-permute-done.6.refs_4_
  57.0 0.0 collective-permute-done.5.refs_3_
  57.0 12.3 %up.1.waited_ref.refs_0_.h_ref = bf16[1280,1536]{1,0:T(8,128)(2,1)} custom-call(bf16[192,1408]{1,0:T(8,128)(2,1)} %copy-done.1, bf16[1280,1408]{1,0:T(8,128)(2,1)} %norm.1.refs_0_.x_ref, bf16[352,1536]{1,0:T(8,128)(2,1)} %copy-done, bf16[352,1536]{1,0:T(8,128)(2,1)} %collective-permute-done.2.second_ref.refs_1_, ...), custom_call_target="tpu_custom_call" | custom-call | flops 1 | bytes 1 | tf_op jit(solution)/shard_map/up/pallas_call | solution.py:225
  69.3 0.0 copy-start.5
  69.3 0.6 collective-permute-start.7
  69.9 1.9 %collective-permute-start.8 = (bf16[192,1408]{1,0:T(8,128)(2,1)S(1)}, bf16[192,1408]{1,0:T(8,128)(2,1)}, u32[]{:S(2)}, u32[]{:S(2)}) collective-permute-start(bf16[192,1408]{1,0:T(8,128)(2,1)S(1)} %get-tuple-element.21.refs_3_), channel_id=1, source_target_pairs={{0,16},{8,24},{16,0},{24,8},{1,17},{9,25},{17,1},{25,9},{2,18},{10... | collective-permute-start | bytes 1622024 | tf_op jit(solution)/shard_map/ppermute | solution.py:363
  71.8 0.0 all-to-all-done.1
  71.9 3.3 %mix.1.waited_ref = bf16[384,256]{1,0:T(8,128)(2,1)} custom-call(s32[2]{0:T(128)S(1)} %pad_add_fusion.at_ref, bf16[1280,1536]{1,0:T(8,128)(2,1)} %up.1.waited_ref.refs_0_.h_ref, bf16[384,1024]{1,0:T(8,128)(2,1)} %get-tuple-element.13.waited_ref.high_ref, bf16[384,1024]{1,0:T(8,128)(2,1)} %get-tuple-element.18.low_ref, bf16[1024,256]{1,0:T(8,128)(2,1)} %bitcast.7.back_ref, ...), custom_call_target="tpu_custom_call" | custom-call | flops 1 | bytes 1 | tf_op jit(solution)/shard_map/mix/pallas_call | solution.py:565
  75.2 0.0 collective-permute-done.10.refs_5_
  75.2 0.0 collective-permute-done.9.refs_2_
  75.2 8.7 %down.1.sum_ref = f32[1280,1408]{1,0:T(8,128)S(1)} custom-call(bf16[384,256]{1,0:T(8,128)(2,1)} %mix.1.waited_ref, bf16[1280,1536]{1,0:T(8,128)(2,1)} %up.1.waited_ref.refs_0_.h_ref, bf16[192,1408]{1,0:T(8,128)(2,1)} %get-tuple-element.12.waited_ref.refs_0_, bf16[192,1408]{1,0:T(8,128)(2,1)} %get-tuple-element.15.refs_1_, ...), custom_call_target="tpu_custom_call" | custom-call | flops 1 | bytes 1 | tf_op jit(solution)/shard_map/down/pallas_call | solution.py:264
  83.9 0.6 collective-permute-done.7.da
  84.5 0.1 collective-permute-done.8.db
  84.6 2.5 %last.2.waited_ref = bf16[640,1408]{1,0:T(8,128)(2,1)S(1)} custom-call(bf16[384,256]{1,0:T(8,128)(2,1)} %mix.1.waited_ref, bf16[1280,1536]{1,0:T(8,128)(2,1)} %up.1.waited_ref.refs_0_.h_ref, bf16[192,1408]{1,0:T(8,128)(2,1)} %collective-permute-done.7.da, bf16[192,1408]{1,0:T(8,128)(2,1)} %collective-permute-done.8.db, f32[1280,1408]{1,0:T(8,128)S(1)} %down.1.sum_ref), custom_call_target="tpu_custom_call" | custom-call | flops 1 | bytes 1 | tf_op jit(solution)/shard_map/last/pallas_call | solution.py:297
  87.1 0.1 collective-permute-start.11
  87.2 2.6 %last.3 = f32[640,1408]{1,0:T(8,128)S(1)} custom-call(bf16[640,1408]{1,0:T(8,128)(2,1)S(1)} %last.2.waited_ref, bf16[1280,1536]{1,0:T(8,128)(2,1)} %up.1.waited_ref.refs_0_.h_ref, bf16[192,1408]{1,0:T(8,128)(2,1)} %collective-permute-done.7.da, bf16[192,1408]{1,0:T(8,128)(2,1)} %collective-permute-done.8.db, f32[1280,1408]{1,0:T(8,128)S(1)} %down.1.sum_ref, ...), custom_call_target="tpu_custom_call" | custom-call | flops 1 | bytes 1 | tf_op jit(solution)/shard_map/last/pallas_call | solution.py:297
  89.8 1.2 %collective-permute-done.11 = bf16[640,1408]{1,0:T(8,128)(2,1)S(1)} collective-permute-done((bf16[640,1408]{1,0:T(8,128)(2,1)S(1)}, bf16[640,1408]{1,0:T(8,128)(2,1)S(1)}, u32[]{:S(2)}, u32[]{:S(2)}) %collective-permute-start.11) | collective-permute-done | bytes 1802272 | tf_op jit(solution)/shard_map/ppermute | solution.py:368
  90.9 1.5 %add_convert_fusion = bf16[640,1408]{1,0:T(8,128)(2,1)} fusion(f32[640,1408]{1,0:T(8,128)S(1)} %last.3, bf16[640,1408]{1,0:T(8,128)(2,1)S(1)} %collective-permute-done.11), kind=kLoop, calls=%fused_computation | loop fusion | flops 2703360 | bytes 7208960 | tf_op jit(solution)/shard_map/convert_element_type | solution.py:370
  (17 shorter events, 0.0 us)
Async XLA Ops:
  0.6 7.5 %copy-start.7 = (s32[384,2]{0,1:T(2,128)S(1)}, s32[384,2]{0,1:T(2,128)}, u32[]{:S(2)}) copy-start(s32[384,2]{0,1:T(2,128)} %param.15) | copy-start | bytes 9220
  0.6 13.9 %collective-permute-start = (bf16[640,1408]{1,0:T(8,128)(2,1)}, bf16[640,1408]{1,0:T(8,128)(2,1)}, u32[]{:S(2)}, u32[]{:S(2)}) collective-permute-start(bf16[640,1408]{1,0:T(8,128)(2,1)} %refs_0_.1), channel_id=1, source_target_pairs={{0,1},{1,0},{2,3},{3,2},{4,5},{5,4},{6,7},{7,6},{8,9},{9,8},{10,11... | collective-permute-start | bytes 5406728 | tf_op jit(solution)/shard_map/ppermute | solution.py:345
  1.2 6.9 %copy-start.4 = (bf16[384,1024]{1,0:T(8,128)(2,1)S(1)}, bf16[384,1024]{1,0:T(8,128)(2,1)}, u32[]{:S(2)}) copy-start(bf16[384,1024]{1,0:T(8,128)(2,1)} %pred_ref.1) | copy-start | bytes 2359300
  3.9 4.1 %copy-start = (bf16[352,1536]{1,0:T(8,128)(2,1)}, bf16[352,1536]{1,0:T(8,128)(2,1)S(1)}, u32[]{:S(2)}) copy-start(bf16[352,1536]{1,0:T(8,128)(2,1)S(1)} %cut_up.1.waited_ref.refs_0_) | copy-start | bytes 3244036
  4.0 10.5 %copy-start.9 = (f32[1408]{0:T(1024)S(1)}, f32[1408]{0:T(1024)}, u32[]{:S(2)}) copy-start(f32[1408]{0:T(1024)} %param.11) | copy-start | bytes 16900
  4.0 10.5 %copy-start.3 = (bf16[640,1408]{1,0:T(8,128)(2,1)S(1)}, bf16[640,1408]{1,0:T(8,128)(2,1)}, u32[]{:S(2)}) copy-start(bf16[640,1408]{1,0:T(8,128)(2,1)} %refs_0_.1) | copy-start | bytes 5406724
  4.0 27.4 %collective-permute-start.2 = (bf16[352,1536]{1,0:T(8,128)(2,1)S(1)}, bf16[352,1536]{1,0:T(8,128)(2,1)}, u32[]{:S(2)}, u32[]{:S(2)}) collective-permute-start(bf16[352,1536]{1,0:T(8,128)(2,1)S(1)} %cut_up.1.waited_ref.refs_0_), channel_id=1, source_target_pairs={{0,8},{8,0},{16,24},{24,16},{1,9},{9,1},{17,25},{25,17},{2,10},{10... | collective-permute-start | bytes 3244040 | tf_op jit(solution)/shard_map/ppermute | solution.py:340
  6.6 26.8 %collective-permute-start.1 = (bf16[352,1536]{1,0:T(8,128)(2,1)S(1)}, bf16[352,1536]{1,0:T(8,128)(2,1)}, u32[]{:S(2)}, u32[]{:S(2)}) collective-permute-start(bf16[352,1536]{1,0:T(8,128)(2,1)S(1)} %cut_up.1.waited_ref.refs_0_), channel_id=1, source_target_pairs={{0,16},{8,24},{16,0},{24,8},{1,17},{9,25},{17,1},{25,9},{2,18},{10... | collective-permute-start | bytes 3244040 | tf_op jit(solution)/shard_map/ppermute | solution.py:340
  9.6 27.2 %all-to-all-start = ((bf16[8,32,1024]{2,1,0:T(8,128)(2,1)}), bf16[8,32,1024]{2,1,0:T(8,128)(2,1)}, u32[]{:S(2)}, u32[]{:S(2)}) async-start(bf16[8,32,1024]{2,1,0:T(8,128)(2,1)} %bitcast.3.waited_ref), calls=%async_computation | async-start | bytes 1048576 | tf_op jit(solution)/shard_map/all_to_all | solution.py:347
  19.4 3.9 %copy-start.8 = (f32[384,2]{0,1:T(2,128)S(1)}, f32[384,2]{0,1:T(2,128)}, u32[]{:S(2)}) copy-start(f32[384,2]{0,1:T(2,128)} %param.16) | copy-start | bytes 9220
  22.2 32.4 %collective-permute-start.3 = (bf16[192,1408]{1,0:T(8,128)(2,1)}, bf16[192,1408]{1,0:T(8,128)(2,1)S(1)}, u32[]{:S(2)}, u32[]{:S(2)}) collective-permute-start(bf16[192,1408]{1,0:T(8,128)(2,1)} %get-tuple-element.15.refs_1_), channel_id=1, source_target_pairs={{0,8},{8,0},{16,24},{24,16},{1,9},{9,1},{17,25},{25,17},{2,10},{10... | collective-permute-start | bytes 1622024 | tf_op jit(solution)/shard_map/ppermute | solution.py:340
  22.8 33.4 %collective-permute-start.4 = (bf16[192,1408]{1,0:T(8,128)(2,1)}, bf16[192,1408]{1,0:T(8,128)(2,1)}, u32[]{:S(2)}, u32[]{:S(2)}) collective-permute-start(bf16[192,1408]{1,0:T(8,128)(2,1)} %get-tuple-element.12.waited_ref.refs_0_), channel_id=1, source_target_pairs={{0,16},{8,24},{16,0},{24,8},{1,17},{9,25},{17,1},{25,9},{2,18},{10... | collective-permute-start | bytes 1622024 | tf_op jit(solution)/shard_map/ppermute | solution.py:340
  34.7 2.1 %copy-start.6 = (bf16[176,1536]{1,0:T(8,128)(2,1)}, bf16[176,1536]{1,0:T(8,128)(2,1)S(1)}, u32[]{:S(2)}) copy-start(bf16[176,1536]{1,0:T(8,128)(2,1)S(1)} %get-tuple-element.14.refs_0_) | copy-start | bytes 1622020
  34.7 22.3 %collective-permute-start.6 = (bf16[176,1536]{1,0:T(8,128)(2,1)S(1)}, bf16[176,1536]{1,0:T(8,128)(2,1)}, u32[]{:S(2)}, u32[]{:S(2)}) collective-permute-start(bf16[176,1536]{1,0:T(8,128)(2,1)S(1)} %get-tuple-element.17), channel_id=1, source_target_pairs={{0,16},{8,24},{16,0},{24,8},{1,17},{9,25},{17,1},{25,9},{2,18},{10... | collective-permute-start | bytes 1622024 | tf_op jit(solution)/shard_map/ppermute | solution.py:353
  36.3 20.7 %collective-permute-start.5 = (bf16[176,1536]{1,0:T(8,128)(2,1)S(1)}, bf16[176,1536]{1,0:T(8,128)(2,1)}, u32[]{:S(2)}, u32[]{:S(2)}) collective-permute-start(bf16[176,1536]{1,0:T(8,128)(2,1)S(1)} %get-tuple-element.14.refs_0_), channel_id=1, source_target_pairs={{0,8},{8,0},{16,24},{24,16},{1,9},{9,1},{17,25},{25,17},{2,10},{10... | collective-permute-start | bytes 1622024 | tf_op jit(solution)/shard_map/ppermute | solution.py:353
  47.9 24.0 %all-to-all-start.1 = ((bf16[32,32,256]{2,1,0:T(8,128)(2,1)}), bf16[32,32,256]{2,1,0:T(8,128)(2,1)}, u32[]{:S(2)}, u32[]{:S(2)}) async-start(bf16[32,32,256]{2,1,0:T(8,128)(2,1)} %bitcast.6.refs_0_), calls=%async_computation.1 | async-start | bytes 1048576 | tf_op jit(solution)/shard_map/all_to_all | solution.py:359
  52.9 22.3 %collective-permute-start.10 = (bf16[192,1408]{1,0:T(8,128)(2,1)}, bf16[192,1408]{1,0:T(8,128)(2,1)}, u32[]{:S(2)}, u32[]{:S(2)}) collective-permute-start(bf16[192,1408]{1,0:T(8,128)(2,1)} %get-tuple-element.15.refs_1_), channel_id=1, source_target_pairs={{0,16},{8,24},{16,0},{24,8},{1,17},{9,25},{17,1},{25,9},{2,18},{10... | collective-permute-start | bytes 1622024 | tf_op jit(solution)/shard_map/ppermute | solution.py:340
  54.7 20.5 %collective-permute-start.9 = (bf16[192,1408]{1,0:T(8,128)(2,1)}, bf16[192,1408]{1,0:T(8,128)(2,1)}, u32[]{:S(2)}, u32[]{:S(2)}) collective-permute-start(bf16[192,1408]{1,0:T(8,128)(2,1)} %get-tuple-element.12.waited_ref.refs_0_), channel_id=1, source_target_pairs={{0,8},{8,0},{16,24},{24,16},{1,9},{9,1},{17,25},{25,17},{2,10},{10... | collective-permute-start | bytes 1622024 | tf_op jit(solution)/shard_map/ppermute | solution.py:340
  56.1 0.8 copy-start.1
  57.0 12.3 %copy-start.2 = (bf16[192,1408]{1,0:T(8,128)(2,1)S(1)}, bf16[192,1408]{1,0:T(8,128)(2,1)}, u32[]{:S(2)}) copy-start(bf16[192,1408]{1,0:T(8,128)(2,1)} %copy-done.1) | copy-start | bytes 1622020
  69.3 2.6 %copy-start.5 = (bf16[384,1024]{1,0:T(8,128)(2,1)S(1)}, bf16[384,1024]{1,0:T(8,128)(2,1)}, u32[]{:S(2)}) copy-start(bf16[384,1024]{1,0:T(8,128)(2,1)} %pred_ref.1) | copy-start | bytes 2359300
  69.3 15.3 %collective-permute-start.7 = (bf16[192,1408]{1,0:T(8,128)(2,1)}, bf16[192,1408]{1,0:T(8,128)(2,1)}, u32[]{:S(2)}, u32[]{:S(2)}) collective-permute-start(bf16[192,1408]{1,0:T(8,128)(2,1)} %get-tuple-element.20.refs_4_), channel_id=1, source_target_pairs={{0,8},{8,0},{16,24},{24,16},{1,9},{9,1},{17,25},{25,17},{2,10},{10... | collective-permute-start | bytes 1622024 | tf_op jit(solution)/shard_map/ppermute | solution.py:363
  69.9 14.7 %collective-permute-start.8 = (bf16[192,1408]{1,0:T(8,128)(2,1)S(1)}, bf16[192,1408]{1,0:T(8,128)(2,1)}, u32[]{:S(2)}, u32[]{:S(2)}) collective-permute-start(bf16[192,1408]{1,0:T(8,128)(2,1)S(1)} %get-tuple-element.21.refs_3_), channel_id=1, source_target_pairs={{0,16},{8,24},{16,0},{24,8},{1,17},{9,25},{17,1},{25,9},{2,18},{10... | collective-permute-start | bytes 1622024 | tf_op jit(solution)/shard_map/ppermute | solution.py:363
  87.1 3.8 %collective-permute-start.11 = (bf16[640,1408]{1,0:T(8,128)(2,1)S(1)}, bf16[640,1408]{1,0:T(8,128)(2,1)S(1)}, u32[]{:S(2)}, u32[]{:S(2)}) collective-permute-start(bf16[640,1408]{1,0:T(8,128)(2,1)S(1)} %last.2.waited_ref), channel_id=1, source_target_pairs={{0,1},{1,0},{2,3},{3,2},{4,5},{5,4},{6,7},{7,6},{8,9},{9,8},{10,11... | collective-permute-start | bytes 5406728 | tf_op jit(solution)/shard_map/ppermute | solution.py:368
